TPU v7x, 1024 devices: a whole 4x8x16 slice. The times are simulated.
1024 devices in a mesh: fsdp: 32 (over z_lo, x, core), rep: 32 (over y, z_hi).
Axes of the slice: x: 4, y: 8, z: 16 (z_hi: 4, z_lo: 4; z = z_hi * 4 + z_lo), core: 2. Of those that a mesh axis runs over, the one named last changes fastest.
Arguments:
- gradients: bfloat16 [32, 32, 32, 16, 2048], P('rep', 'fsdp'), may hold values from -1.1953125 to 1.1953125
- second_moment: float32 [32, 32, 16, 2048], P('fsdp', 'rep'), may hold values from 0.02 to 5
- left_rows: bfloat16 [32, 32, 64, 512], P('rep', 'fsdp'), may hold values from -1 to 2
- right_root: bfloat16 [32, 4, 512, 512], P('rep'), may hold values from -1 to 2
- owner_table: int32 [32, 32], replicated, may hold values from 0 to 31, as said below
- step_count: int32 [1], replicated, may hold values from 1 to 40
Outputs:
- update: bfloat16 [32, 32, 16, 2048], P('fsdp', 'rep')
- new_moment: float32 [32, 32, 16, 2048], P('fsdp', 'rep')
Inputs may be any that keep to these rules, and one draw needn't show every extreme that they name: `owner_table`: each row is a permutation of the work items' workers.
All inputs are finite; a program needn't handle non-finite values.
Results may differ from a plain program's by a relative error of at most 0.024.
Values may be sent and summed in bfloat16 or wider, within the bound.
No kernel may reach another device: no remote copies, remote signals or barrier semaphores. Data moves between devices by JAX's collectives and lax.ppermute only.
A program may use at most 32 MiB of HBM per device.

v0:
```python
import jax
import jax.numpy as jnp
from jax import lax
from jax.sharding import PartitionSpec as P

beta_two = 0.95
adam_eps = 1e-08


def adam_part(summed, moment, correction, blocks, block_width):
    new_part = beta_two * moment + (1.0 - beta_two) * summed * summed
    adam_dir = summed / (jnp.sqrt(new_part / correction) + adam_eps)
    row_count = summed.shape[0]
    part_sq = jnp.sum((adam_dir * adam_dir).reshape(row_count, blocks, block_width), axis=(0, 2))
    return (new_part, part_sq)


def route_out(summed, route_map, blocks, block_width):
    pieces = summed.astype(jnp.bfloat16).reshape(summed.shape[0], blocks, block_width)
    return jnp.einsum("kd,skc->dsc", route_map, pieces, preferred_element_type=jnp.float32).astype(
        jnp.bfloat16
    )


def contract(left_cols, received):
    return jnp.einsum("mfs,fsc->mc", left_cols, received, preferred_element_type=jnp.float32)


def local(gradients, second_moment, left_rows, right_root, owner_table, step_count):
    members = lax.axis_size("fsdp")
    group_id = lax.axis_index("rep")
    member = lax.axis_index("fsdp")
    sub_rows = gradients.shape[3]
    blocks = right_root.shape[1]
    block_width = right_root.shape[3]
    team_size = members // blocks
    share_rows = sub_rows // team_size
    owner_row = lax.dynamic_index_in_dim(owner_table, group_id, 0, keepdims=False)
    device_ids = lax.broadcasted_iota(jnp.int32, (members, members), 1)
    placed = owner_row[:, None] == device_ids
    placed_bf = placed.astype(jnp.bfloat16)
    route_map = jnp.any(placed.reshape(blocks, team_size, members), axis=1).astype(jnp.bfloat16)
    item_ids = lax.broadcasted_iota(jnp.int32, (members,), 0)
    my_item = jnp.sum(jnp.where(owner_row == member, item_ids, 0))
    my_block = my_item // team_size
    block_ids = lax.broadcasted_iota(jnp.int32, (blocks,), 0)
    block_pick = (block_ids == my_block).astype(jnp.float32)
    correction = 1.0 - jnp.power(jnp.float32(beta_two), step_count[0].astype(jnp.float32))
    moment = second_moment[0, 0]
    slab_rows = left_rows.shape[2]
    left_cols = left_rows[0, 0].reshape(slab_rows, members, sub_rows)
    summed = lax.psum_scatter(gradients, "rep", scatter_dimension=2, tiled=True).astype(
        jnp.float32
    )[0, 0, 0]
    new_moment, adam_sq = adam_part(summed, moment, correction, blocks, block_width)
    received = lax.all_to_all(
        route_out(summed, route_map, blocks, block_width),
        "fsdp",
        split_axis=0,
        concat_axis=0,
        tiled=True,
    )
    first_product = contract(left_cols, received)
    right_block = lax.dynamic_index_in_dim(right_root[0], my_block, 0, keepdims=False)
    precond = jnp.dot(
        first_product.astype(jnp.bfloat16), right_block, preferred_element_type=jnp.float32
    )
    precond_sq = jnp.sum(precond * precond)
    adam_total, precond_total = lax.psum((adam_sq, block_pick * precond_sq), "fsdp")
    graft_ratio = jnp.sqrt(adam_total / (precond_total + 1e-06))
    my_ratio = jnp.sum(block_pick * graft_ratio)
    scaled = (precond * my_ratio).astype(jnp.bfloat16).reshape(members, share_rows, block_width)
    returned = lax.all_to_all(scaled, "fsdp", split_axis=0, concat_axis=0, tiled=True)
    arranged = jnp.einsum(
        "kid,dtc->itkc",
        placed_bf.reshape(blocks, team_size, members),
        returned,
        preferred_element_type=jnp.float32,
    )
    update = arranged.astype(jnp.bfloat16).reshape(sub_rows, blocks * block_width)
    return (update[None, None], new_moment[None, None])


def solution(mesh):
    placed = (
        P("rep", "fsdp", None, None, None),
        P("fsdp", "rep", None, None),
        P("rep", "fsdp", None, None),
        P("rep", None, None, None),
        P(),
        P(),
    )
    return jax.shard_map(
        local,
        mesh=mesh,
        in_specs=placed,
        out_specs=(P("fsdp", "rep", None, None), P("fsdp", "rep", None, None)),
        check_vma=False,
    )
```

profile of v0, /device:TPU:1, one launch (start us, length us, event | category | flops | bytes accessed | tf_op | source)
XLA Modules:
  0.0 393.8 jit_solution(15596656601246249636)
XLA Ops:
  7.2 0.0 copy-start
  7.2 0.0 copy-start.3
  7.2 0.0 copy-start.2
  7.2 0.0 reduce-scatter.2.cloned.1.call-start
  7.2 0.7 reduce-scatter.2.cloned.1.call-update
  7.9 0.7 fusion.21
  8.6 0.1 eq.26
  8.7 0.1 fusion.14
  8.8 262.3 %reduce-scatter.2.cloned.1.call-done = bf16[1,1,1,16,2048]{4,3,2,1,0:T(8,128)(2,1)} async-done(((bf16[1,1,32,16,2048]{4,3,2,1,0:T(8,128)(2,1)}), bf16[1,1,1,16,2048]{4,3,2,1,0:T(8,128)(2,1)}) %reduce-scatter.2.cloned.1.call-update) | async-done | bytes 65552 | tf_op jit(solution)/shard_map/reduce_scatter | solution.py:52
  271.1 0.0 copy-start.1
  271.1 0.9 convert_element_type.31
  272.1 0.4 convolution_convert_fusion
  272.5 1.1 copy.22
  273.5 11.2 %all-to-all-start = ((bf16[32,16,512]{2,1,0:T(8,128)(2,1)}), bf16[32,16,512]{2,1,0:T(8,128)(2,1)S(1)}, u32[]{:S(2)}, u32[]{:S(2)}) async-start(bf16[32,16,512]{2,1,0:T(8,128)(2,1)} %copy.22), calls=%async_computation.1 | async-start | bytes 1048576 | tf_op jit(solution)/shard_map/all_to_all | solution.py:56
  284.7 1.3 fusion.19
  288.7 0.0 copy-done.3
  288.7 0.1 copy.23
  289.5 0.0 copy-done.2
  289.5 0.0 copy-done.1
  289.5 0.1 fusion.11
  289.6 0.1 reduce_sum.46
  289.7 11.4 %all-to-all-done = bf16[32,16,512]{2,1,0:T(8,128)(2,1)S(1)} async-done(((bf16[32,16,512]{2,1,0:T(8,128)(2,1)}), bf16[32,16,512]{2,1,0:T(8,128)(2,1)S(1)}, u32[]{:S(2)}, u32[]{:S(2)}) %all-to-all-start) | async-done | bytes 524320 | tf_op jit(solution)/shard_map/all_to_all | solution.py:56
  301.1 0.0 copy-done
  301.1 1.0 multiply_reduce_fusion
  302.1 0.6 compare_select_fusion.1
  302.8 66.4 %all-reduce = (f32[4]{0:T(128)S(1)}, f32[4]{0:T(128)S(1)}) all-reduce(f32[4]{0:T(128)S(1)} %reduce_sum.46, f32[4]{0:T(128)S(1)} %compare_select_fusion.1), channel_id=1, replica_groups=mesh['fsdp'=32,'rep'=32] {'fsdp'}, use_global_device_ids=true, to_apply=%region_5.6 | all-reduce | flops 8 | bytes 64 | tf_op jit(solution)/shard_map/psum | solution.py:69
  369.2 0.6 fusion.18
  369.8 0.7 multiply_convert_fusion
  370.5 0.7 reshape.64
  371.2 7.0 %all-to-all-start.1 = ((bf16[32,2,512]{2,1,0:T(2,128)(2,1)}), bf16[32,2,512]{2,1,0:T(2,128)(2,1)S(1)}, u32[]{:S(2)}, u32[]{:S(2)}) async-start(bf16[32,2,512]{2,1,0:T(2,128)(2,1)} %reshape.64), calls=%async_computation.2 | async-start | bytes 131072 | tf_op jit(solution)/shard_map/all_to_all | solution.py:73
  378.2 0.7 fusion.5
  378.9 7.2 %all-to-all-done.1 = bf16[32,2,512]{2,1,0:T(2,128)(2,1)S(1)} async-done(((bf16[32,2,512]{2,1,0:T(2,128)(2,1)}), bf16[32,2,512]{2,1,0:T(2,128)(2,1)S(1)}, u32[]{:S(2)}, u32[]{:S(2)}) %all-to-all-start.1) | async-done | bytes 65568 | tf_op jit(solution)/shard_map/all_to_all | solution.py:73
  386.0 0.2 fusion.2
  386.3 0.7 broadcast_in_dim_reshape.3
  (2 shorter events, 0.0 us)
Async XLA Ops:
  7.2 293.9 %copy-start = (bf16[1,4,512,512]{3,2,1,0:T(8,128)(2,1)S(1)}, bf16[1,4,512,512]{3,2,1,0:T(8,128)(2,1)}, u32[]{:S(2)}) copy-start(bf16[1,4,512,512]{3,2,1,0:T(8,128)(2,1)} %param.9) | copy-start | bytes 6291460
  7.2 281.5 %copy-start.3 = (bf16[1,1,64,512]{3,2,1,0:T(8,128)(2,1)S(1)}, bf16[1,1,64,512]{3,2,1,0:T(8,128)(2,1)}, u32[]{:S(2)}) copy-start(bf16[1,1,64,512]{3,2,1,0:T(8,128)(2,1)} %param.8) | copy-start | bytes 196612
  7.2 282.3 %copy-start.2 = (f32[1,1,16,2048]{3,2,1,0:T(8,128)S(1)}, f32[1,1,16,2048]{3,2,1,0:T(8,128)}, u32[]{:S(2)}) copy-start(f32[1,1,16,2048]{3,2,1,0:T(8,128)} %param.7) | copy-start | bytes 393220
  7.2 263.9 %reduce-scatter.2.cloned.1.call-start = ((), (), s32[]{:S(2)}) async-start(), calls=%async_computation.3 | async-start | bytes 2162688 | tf_op jit(solution)/shard_map/reduce_scatter | solution.py:52
  271.1 18.4 %copy-start.1 = (bf16[1,1,1,16,2048]{4,3,2,1,0:T(8,128)(2,1)S(1)}, bf16[1,1,1,16,2048]{4,3,2,1,0:T(8,128)(2,1)}, u32[]{:S(2)}) copy-start(bf16[1,1,1,16,2048]{4,3,2,1,0:T(8,128)(2,1)} %reduce-scatter.2.cloned.1.call-done) | copy-start | bytes 196612
  273.5 27.6 %all-to-all-start = ((bf16[32,16,512]{2,1,0:T(8,128)(2,1)}), bf16[32,16,512]{2,1,0:T(8,128)(2,1)S(1)}, u32[]{:S(2)}, u32[]{:S(2)}) async-start(bf16[32,16,512]{2,1,0:T(8,128)(2,1)} %copy.22), calls=%async_computation.1 | async-start | bytes 1048576 | tf_op jit(solution)/shard_map/all_to_all | solution.py:56
  371.2 14.9 %all-to-all-start.1 = ((bf16[32,2,512]{2,1,0:T(2,128)(2,1)}), bf16[32,2,512]{2,1,0:T(2,128)(2,1)S(1)}, u32[]{:S(2)}, u32[]{:S(2)}) async-start(bf16[32,2,512]{2,1,0:T(2,128)(2,1)} %reshape.64), calls=%async_computation.2 | async-start | bytes 131072 | tf_op jit(solution)/shard_map/all_to_all | solution.py:73
Sparse Core Ops, SparseCore 0:
  13.7 257.4 reduce-scatter.1
where the time goes:
time: 394 us
  waiting for transfers between devices  282 us (72%)
  blocking collectives  66.4 us (17%)
  starting transfers between devices  18.2 us (5%)
  between operations  17.5 us (4%)
  local copies, waits for them, and re-layouts  4.33 us (1%)
  other arithmetic  4.25 us (1%)
    reduce_scatter x1, waiting for transfers between devices, local(): lax.psum_scatter(gradients, 'rep', scatter_dimension=2, tiled=True)  262 us
    psum x1, blocking collectives, local(): lax.psum((adam_sq, block_pick * precond_sq), 'fsdp')  66.4 us
    all_to_all x1, waiting for transfers between devices, local(): lax.all_to_all(route_out(summed, route_map, blocks, block_width), 'fsdp',...  11.4 us
    all_to_all x1, starting transfers between devices, local(): lax.all_to_all(route_out(summed, route_map, blocks, block_width), 'fsdp',...  11.2 us
  transfers between devices with their start and end apart: 3, of which 3 were waited for; matrix products, arithmetic and copies ran while one was open for 1% of the time, Pallas kernels for 0%

commit v1 on v0

v1 whole, which is shorter than its diff:
```python
import jax
import jax.numpy as jnp
from jax import lax
from jax.experimental import pallas as pl
from jax.experimental.pallas import tpu as pltpu
from jax.sharding import Mesh, PartitionSpec as P

beta_two = 0.95
adam_eps = 1e-08
FS = ("z_lo", "x", "core")
REP = ("y", "z_hi")
f32 = jnp.float32
bf16 = jnp.bfloat16
VMEM_LIMIT = 32 * 1024 * 1024


def params():
    return pltpu.CompilerParams(vmem_limit_bytes=VMEM_LIMIT)


def ring_first(chunks, index, received, keep_low):
    _, parts, rows, width = chunks.shape
    half = parts // 2

    def body(idx, own, got, out):
        if keep_low:
            out[:half] = (own[0, :half].astype(f32) + got[...].astype(f32)).astype(bf16)
            out[half:] = own[0, half:]
        else:
            out[half:] = (own[0, half:].astype(f32) + got[...].astype(f32)).astype(bf16)
            out[:half] = own[0, :half]

    return pl.pallas_call(
        body,
        grid_spec=pltpu.PrefetchScalarGridSpec(
            num_scalar_prefetch=1,
            grid=(1,),
            in_specs=[
                pl.BlockSpec((1, parts, rows, width), lambda i, idx: (idx[0], 0, 0, 0)),
                pl.BlockSpec((half, rows, width), lambda i, idx: (0, 0, 0)),
            ],
            out_specs=pl.BlockSpec((parts, rows, width), lambda i, idx: (0, 0, 0)),
        ),
        out_shape=jax.ShapeDtypeStruct((parts, rows, width), bf16),
        compiler_params=params(),
        name="ring_first",
    )(index, chunks, received)


def ring_add(chunks, index, *received):
    _, parts, rows, width = chunks.shape
    piece = parts // 2

    def body(idx, own, *refs):
        total = own[0].astype(f32)
        for got in refs[:-1]:
            total = total + got[...].astype(f32)
        refs[-1][...] = total.astype(bf16)

    block = pl.BlockSpec((piece, rows, width), lambda i, idx: (i, 0, 0))
    return pl.pallas_call(
        body,
        grid_spec=pltpu.PrefetchScalarGridSpec(
            num_scalar_prefetch=1,
            grid=(parts // piece,),
            in_specs=[pl.BlockSpec((1, piece, rows, width), lambda i, idx: (idx[0], i, 0, 0))]
            + [block] * len(received),
            out_specs=block,
        ),
        out_shape=jax.ShapeDtypeStruct((parts, rows, width), bf16),
        compiler_params=params(),
        name="ring_add",
    )(index, chunks, *received)


def right_product(parts, right):
    count, rows, width = parts.shape
    blocks, size, _ = right.shape
    tiles = size // 128

    def body(got, root, summed, pieces):
        total = got[0].astype(f32)
        for i in range(1, count):
            total = total + got[i].astype(f32)
        summed[...] = total
        grad = total.astype(bf16)
        for k in range(blocks):
            prod = jnp.dot(
                grad[:, k * size : (k + 1) * size], root[k], preferred_element_type=f32
            ).astype(bf16)
            for x in range(tiles):
                tile = prod[:, x * 128 : (x + 1) * 128]
                for c in range(2):
                    pieces[(k * tiles + x) * 2 + c] = tile

    return pl.pallas_call(
        body,
        out_shape=(
            jax.ShapeDtypeStruct((rows, width), f32),
            jax.ShapeDtypeStruct((blocks * tiles * 2, rows, 128), bf16),
        ),
        compiler_params=params(),
        name="right_product",
    )(parts, right)


def adam_part(summed, moment, correction, blocks):
    rows, width = summed.shape
    size = width // blocks

    def body(corr, grad, old, new, squares):
        g = grad[...]
        m = beta_two * old[...] + (1.0 - beta_two) * g * g
        new[...] = m
        d = g / (jnp.sqrt(m / corr[0]) + adam_eps)
        d = d * d
        lane = lax.broadcasted_iota(jnp.int32, (8, 128), 1)
        acc = jnp.zeros((8, 128), f32)
        for k in range(blocks):
            acc = jnp.where(lane == k, jnp.sum(d[:, k * size : (k + 1) * size]), acc)
        squares[...] = acc

    return pl.pallas_call(
        body,
        in_specs=[
            pl.BlockSpec(memory_space=pltpu.SMEM),
            pl.BlockSpec(memory_space=pltpu.VMEM),
            pl.BlockSpec(memory_space=pltpu.VMEM),
        ],
        out_shape=(
            jax.ShapeDtypeStruct((rows, width), f32),
            jax.ShapeDtypeStruct((8, 128), f32),
        ),
        compiler_params=params(),
        name="adam_part",
    )(correction, summed, moment)


def left_product(left, columns, squares, my_block, members, blocks):
    out_rows, size = left.shape

    def body(block, lref, cref, sref, out):
        prod = jnp.dot(lref[...], cref[...], preferred_element_type=f32)
        lane = lax.broadcasted_iota(jnp.int32, (8, 128), 1)
        row = lax.broadcasted_iota(jnp.int32, (8, 128), 0)
        norms = jnp.where(lane == blocks + block[0], jnp.sum(prod * prod), sref[...])
        high = norms.astype(bf16).astype(f32)
        rest = norms - high
        mid = rest.astype(bf16).astype(f32)
        low = rest - mid
        tail = jnp.where(row == 0, high, jnp.where(row == 1, mid, jnp.where(row == 2, low, 0.0)))
        out[:, :8, :] = prod.reshape(members, 8, 128).astype(bf16)
        out[:, 8:, :] = jnp.broadcast_to(tail[None], (members, 8, 128)).astype(bf16)

    return pl.pallas_call(
        body,
        in_specs=[pl.BlockSpec(memory_space=pltpu.SMEM)]
        + [pl.BlockSpec(memory_space=pltpu.VMEM)] * 3,
        out_shape=jax.ShapeDtypeStruct((members, 16, 128), bf16),
        compiler_params=params(),
        name="left_product",
    )(my_block, left, columns, squares)


def finish(returned, rows, width, blocks):
    members = returned.shape[0]
    tiles = members // blocks // 2

    def body(got, out):
        sums = jnp.sum(got[:, 8:, :].astype(f32), axis=0)
        sums = jnp.sum(sums, axis=0, keepdims=True)
        lane = lax.broadcasted_iota(jnp.int32, (1, 128), 1)
        for k in range(blocks):
            adam = jnp.sum(jnp.where(lane == k, sums, 0.0), axis=1, keepdims=True)
            shampoo = jnp.sum(jnp.where(lane == blocks + k, sums, 0.0), axis=1, keepdims=True)
            ratio = jnp.sqrt(adam / (shampoo + 1e-06))
            for x in range(tiles):
                d = (k * tiles + x) * 2
                both = jnp.concatenate([got[d, :8, :].astype(f32), got[d + 1, :8, :].astype(f32)], 0)
                col = (k * tiles + x) * 128
                out[:, col : col + 128] = (both * ratio).astype(bf16)

    return pl.pallas_call(
        body,
        out_shape=jax.ShapeDtypeStruct((rows, width), bf16),
        compiler_params=params(),
        name="finish",
    )(returned)


def local(gradients, second_moment, left_rows, right_root, owner_table, step_count):
    ny, nz = lax.axis_size("y"), lax.axis_size("z_hi")
    yi = lax.axis_index("y")
    group_id = lax.axis_index(REP)
    member = lax.axis_index(FS)
    members = lax.axis_size(FS)
    rows, width = gradients.shape[3], gradients.shape[4]
    blocks, size = right_root.shape[1], right_root.shape[3]
    team = members // blocks
    share = rows // team
    my_block = member // team

    gathered = lax.all_gather(left_rows[0, 0], FS, axis=0, tiled=True)
    owner_row = lax.dynamic_index_in_dim(owner_table, group_id, 0, keepdims=False)
    half = team // 2
    first = my_block * team + (member % 2) * half
    owners = lax.dynamic_slice_in_dim(owner_row, first, half, 0)
    source = (
        owners[None, :, None] * (members * share)
        + jnp.arange(members)[:, None, None] * share
        + jnp.arange(share)[None, None, :]
    ).reshape(members * half * share)
    pick = (source[:, None] == jnp.arange(members * members * share)[None, :]).astype(bf16)
    left = jnp.dot(pick, gathered, preferred_element_type=f32).astype(bf16)

    chunks = gradients.reshape(ny, nz, rows, width)
    up = [(j, (j + 1) % ny) for j in range(ny)]
    down = [(j, (j - 1) % ny) for j in range(ny)]

    def at(offset):
        return lax.rem(yi + offset + ny, ny).astype(jnp.int32).reshape(1)

    far = lax.dynamic_index_in_dim(chunks, at(4)[0], 0, keepdims=False)
    above = lax.ppermute(far[: nz // 2], "y", up)
    below = lax.ppermute(far[nz // 2 :], "y", down)
    above = ring_first(chunks, at(3), above, True)
    above = lax.ppermute(above, "y", up)
    below = ring_first(chunks, at(-3), below, False)
    below = lax.ppermute(below, "y", down)
    for s in (2, 1):
        above = lax.ppermute(ring_add(chunks, at(s), above), "y", up)
        below = lax.ppermute(ring_add(chunks, at(-s), below), "y", down)
    part = ring_add(chunks, at(0), above, below)

    parts = lax.all_to_all(part, "z_hi", 0, 0, tiled=True)
    summed, pieces = right_product(parts, right_root[0])
    columns = lax.all_to_all(pieces, FS, 0, 0, tiled=True)

    correction = 1.0 - jnp.power(f32(beta_two), step_count.astype(f32))
    new_moment, squares = adam_part(summed, second_moment[0, 0], correction, blocks)

    sent = left_product(
        left,
        columns.reshape(members * rows, 128),
        squares,
        my_block.astype(jnp.int32).reshape(1),
        members,
        blocks,
    )
    returned = lax.all_to_all(sent, FS, 0, 0, tiled=True)
    update = finish(returned, rows, width, blocks)
    return (update[None, None], new_moment[None, None])


def solution(mesh):
    fine = Mesh(mesh.devices.reshape(4, 4, 2, 8, 4), FS + REP)
    return jax.shard_map(
        local,
        mesh=fine,
        in_specs=(
            P(REP, FS, None, None, None),
            P(FS, REP, None, None),
            P(REP, FS, None, None),
            P(REP, None, None, None),
            P(),
            P(),
        ),
        out_specs=(P(FS, REP, None, None), P(FS, REP, None, None)),
        check_vma=False,
    )
```

time: 394 us -> 130 us (0.33)
  waiting for transfers between devices: 282 us -> 32.7 us
  blocking collectives: 66.4 us -> 12.1 us
  starting transfers between devices: 18.2 us -> 57.6 us
  Pallas kernels: 0 us -> 4.11 us
    reduce_scatter x1 -> x0, waiting for transfers between devices: 262 us -> none  [local(): lax.psum_scatter(gradients, 'rep', scatter_dimension=2, tiled=True)]
    psum x1 -> x0, blocking collectives: 66.4 us -> none  [local(): lax.psum((adam_sq, block_pick * precond_sq), 'fsdp')]
    ppermute x0 -> x8, starting transfers between devices: none -> 27.5 us  [the longest x2 9.15 us: local(): below = lax.ppermute(ring_add(chunks, at(-s), below), 'y', down)]
    all_to_all x0 -> x1, blocking collectives: none -> 12.1 us  [local(): returned = lax.all_to_all(sent, FS, 0, 0, tiled=True)]
    all_to_all x2, starting transfers between devices: 18.2 us -> 30.1 us  [the longest x1 19.3 us: local(): parts = lax.all_to_all(part, 'z_hi', 0, 0, tiled=True)]
    ppermute x0 -> x8, waiting for transfers between devices: none -> 9.08 us  [the longest x2 3.72 us: local(): above = lax.ppermute(ring_add(chunks, at(s), above), 'y', up)]
    all_to_all x2, waiting for transfers between devices: 18.5 us -> 22.9 us  [the longest x1 18.4 us: local(): parts = lax.all_to_all(part, 'z_hi', 0, 0, tiled=True)]
    pallas_call x0 -> x11, Pallas kernels: none -> 4.11 us  [the longest x5 1.17 us: ring_add(): pl.pallas_call(body, grid_spec=pltpu.PrefetchScalarGridSpec(num_scalar_pr...]
  transfers between devices with their start and end apart: 3 -> 11, of which waited for: 3 -> 7; matrix products, arithmetic and copies ran while one was open for 1% -> 3% of each run, Pallas kernels for 0% -> 2%
where the time goes in v1:
time: 130 us; the launch traced here: 129 us
  starting transfers between devices  57.6 us (44%)
  waiting for transfers between devices  32.7 us (25%)
  between operations  14.9 us (11%)
  blocking collectives  12.1 us (9%)
  local copies, waits for them, and re-layouts  4.33 us (3%)
  Pallas kernels  4.11 us (3%)
  matrix products  2.34 us (2%)
    all_to_all x1, starting transfers between devices, local(): parts = lax.all_to_all(part, 'z_hi', 0, 0, tiled=True)  19.3 us
    all_to_all x1, waiting for transfers between devices, local(): parts = lax.all_to_all(part, 'z_hi', 0, 0, tiled=True)  18.4 us
    all_to_all x1, blocking collectives, local(): returned = lax.all_to_all(sent, FS, 0, 0, tiled=True)  12.1 us
    all_to_all x1, starting transfers between devices, local(): columns = lax.all_to_all(pieces, FS, 0, 0, tiled=True)  10.8 us
    ppermute x2, starting transfers between devices, local(): below = lax.ppermute(ring_add(chunks, at(-s), below), 'y', down)  9.15 us
    ppermute x1, starting transfers between devices, local(): below = lax.ppermute(below, 'y', down)  4.57 us
    all_to_all x1, waiting for transfers between devices, local(): columns = lax.all_to_all(pieces, FS, 0, 0, tiled=True)  4.52 us
    ppermute x1, starting transfers between devices, local(): above = lax.ppermute(far[:nz // 2], 'y', up)  4.03 us
  transfers between devices with their start and end apart: 11, of which 7 were waited for; matrix products, arithmetic and copies ran while one was open for 3% of the time, Pallas kernels for 2%

profile of v1, /device:TPU:1, one launch (start us, length us, event | category | flops | bytes accessed | tf_op | source)
XLA Modules:
  0.0 129.1 jit_solution(6646118252663621136)
XLA Ops:
  7.2 0.0 all-gather.3.cloned.1.call-start
  7.2 0.7 all-gather.3.cloned.1.call-update
  7.9 1.0 dynamic-slice_bitcast_fusion
  8.9 4.0 %collective-permute-start = (bf16[2,16,2048]{2,1,0:T(8,128)(2,1)S(1)}, bf16[2,16,2048]{2,1,0:T(8,128)(2,1)S(1)}, u32[]{:S(2)}, u32[]{:S(2)}) collective-permute-start(bf16[2,16,2048]{2,1,0:T(8,128)(2,1)S(1)} %get-tuple-element.11), channel_id=1, source_target_pairs={{0,4},{4,8},{8,12},{12,16},{16,20},{20,24},{24,28},{28,0},{1,5},{5... | collective-permute-start | bytes 393224 | tf_op jit(solution)/shard_map/ppermute | solution.py:224
  12.9 3.8 %collective-permute-start.4 = (bf16[2,16,2048]{2,1,0:T(8,128)(2,1)S(1)}, bf16[2,16,2048]{2,1,0:T(8,128)(2,1)S(1)}, u32[]{:S(2)}, u32[]{:S(2)}) collective-permute-start(bf16[2,16,2048]{2,1,0:T(8,128)(2,1)S(1)} %get-tuple-element.10), channel_id=1, source_target_pairs={{0,28},{4,0},{8,4},{12,8},{16,12},{20,16},{24,20},{28,24},{1,29},{... | collective-permute-start | bytes 393224 | tf_op jit(solution)/shard_map/ppermute | solution.py:225
  16.8 0.4 collective-permute-done.got
  17.2 0.0 copy-start
  17.2 1.6 %copy-done = bf16[1,1,32,16,2048]{4,3,2,1,0:T(8,128)(2,1)S(1)} copy-done((bf16[1,1,32,16,2048]{4,3,2,1,0:T(8,128)(2,1)S(1)}, bf16[1,1,32,16,2048]{4,3,2,1,0:T(8,128)(2,1)}, u32[]{:S(2)}) %copy-start) | copy-done | bytes 2097176
  18.8 0.0 copy-start.1
  18.8 2.1 %collective-permute-start.1 = (bf16[4,16,2048]{2,1,0:T(8,128)(2,1)S(1)}, bf16[4,16,2048]{2,1,0:T(8,128)(2,1)S(1)}, u32[]{:S(2)}, u32[]{:S(2)}) collective-permute-start(bf16[4,16,2048]{2,1,0:T(8,128)(2,1)S(1)} %ring_first.2), channel_id=1, source_target_pairs={{0,4},{4,8},{8,12},{12,16},{16,20},{20,24},{24,28},{28,0},{1,5},{5... | collective-permute-start | bytes 786440 | tf_op jit(solution)/shard_map/ppermute | solution.py:227
  20.9 0.0 collective-permute-done.4.got
  20.9 0.0 copy-done.1
  20.9 4.6 %collective-permute-start.5 = (bf16[4,16,2048]{2,1,0:T(8,128)(2,1)S(1)}, bf16[4,16,2048]{2,1,0:T(8,128)(2,1)S(1)}, u32[]{:S(2)}, u32[]{:S(2)}) collective-permute-start(bf16[4,16,2048]{2,1,0:T(8,128)(2,1)S(1)} %ring_first.3), channel_id=1, source_target_pairs={{0,28},{4,0},{8,4},{12,8},{16,12},{20,16},{24,20},{28,24},{1,29},{... | collective-permute-start | bytes 786440 | tf_op jit(solution)/shard_map/ppermute | solution.py:229
  25.5 1.7 %collective-permute-done.1.refs_0_ = bf16[4,16,2048]{2,1,0:T(8,128)(2,1)S(1)} collective-permute-done((bf16[4,16,2048]{2,1,0:T(8,128)(2,1)S(1)}, bf16[4,16,2048]{2,1,0:T(8,128)(2,1)S(1)}, u32[]{:S(2)}, u32[]{:S(2)}) %collective-permute-start.1) | collective-permute-done | bytes 262176 | tf_op jit(solution)/shard_map/ppermute | solution.py:227
  27.3 0.1 ring_add.5
  27.4 1.9 %collective-permute-start.2 = (bf16[4,16,2048]{2,1,0:T(8,128)(2,1)S(1)}, bf16[4,16,2048]{2,1,0:T(8,128)(2,1)S(1)}, u32[]{:S(2)}, u32[]{:S(2)}) collective-permute-start(bf16[4,16,2048]{2,1,0:T(8,128)(2,1)S(1)} %ring_add.5), channel_id=1, source_target_pairs={{0,4},{4,8},{8,12},{12,16},{16,20},{20,24},{24,28},{28,0},{1,5},{5... | collective-permute-start | bytes 786440 | tf_op jit(solution)/shard_map/ppermute | solution.py:231
  29.3 0.0 collective-permute-done.5.refs_0_
  29.3 0.1 ring_add.7
  29.4 4.6 %collective-permute-start.6 = (bf16[4,16,2048]{2,1,0:T(8,128)(2,1)S(1)}, bf16[4,16,2048]{2,1,0:T(8,128)(2,1)S(1)}, u32[]{:S(2)}, u32[]{:S(2)}) collective-permute-start(bf16[4,16,2048]{2,1,0:T(8,128)(2,1)S(1)} %ring_add.7), channel_id=1, source_target_pairs={{0,28},{4,0},{8,4},{12,8},{16,12},{20,16},{24,20},{28,24},{1,29},{... | collective-permute-start | bytes 786440 | tf_op jit(solution)/shard_map/ppermute | solution.py:232
  34.0 1.7 %collective-permute-done.2.refs_0_ = bf16[4,16,2048]{2,1,0:T(8,128)(2,1)S(1)} collective-permute-done((bf16[4,16,2048]{2,1,0:T(8,128)(2,1)S(1)}, bf16[4,16,2048]{2,1,0:T(8,128)(2,1)S(1)}, u32[]{:S(2)}, u32[]{:S(2)}) %collective-permute-start.2) | collective-permute-done | bytes 262176 | tf_op jit(solution)/shard_map/ppermute | solution.py:231
  35.7 0.1 ring_add.6
  35.8 1.9 %collective-permute-start.3 = (bf16[4,16,2048]{2,1,0:T(8,128)(2,1)S(1)}, bf16[4,16,2048]{2,1,0:T(8,128)(2,1)S(1)}, u32[]{:S(2)}, u32[]{:S(2)}) collective-permute-start(bf16[4,16,2048]{2,1,0:T(8,128)(2,1)S(1)} %ring_add.6), channel_id=1, source_target_pairs={{0,4},{4,8},{8,12},{12,16},{16,20},{20,24},{24,28},{28,0},{1,5},{5... | collective-permute-start | bytes 786440 | tf_op jit(solution)/shard_map/ppermute | solution.py:231
  37.7 0.0 collective-permute-done.6.refs_0_
  37.7 0.1 ring_add.8
  37.9 4.6 %collective-permute-start.7 = (bf16[4,16,2048]{2,1,0:T(8,128)(2,1)S(1)}, bf16[4,16,2048]{2,1,0:T(8,128)(2,1)S(1)}, u32[]{:S(2)}, u32[]{:S(2)}) collective-permute-start(bf16[4,16,2048]{2,1,0:T(8,128)(2,1)S(1)} %ring_add.8), channel_id=1, source_target_pairs={{0,28},{4,0},{8,4},{12,8},{16,12},{20,16},{24,20},{28,24},{1,29},{... | collective-permute-start | bytes 786440 | tf_op jit(solution)/shard_map/ppermute | solution.py:232
  42.4 2.0 %collective-permute-done.3.refs_0_ = bf16[4,16,2048]{2,1,0:T(8,128)(2,1)S(1)} collective-permute-done((bf16[4,16,2048]{2,1,0:T(8,128)(2,1)S(1)}, bf16[4,16,2048]{2,1,0:T(8,128)(2,1)S(1)}, u32[]{:S(2)}, u32[]{:S(2)}) %collective-permute-start.3) | collective-permute-done | bytes 262176 | tf_op jit(solution)/shard_map/ppermute | solution.py:231
  44.5 3.2 %collective-permute-done.7.refs_1_ = bf16[4,16,2048]{2,1,0:T(8,128)(2,1)S(1)} collective-permute-done((bf16[4,16,2048]{2,1,0:T(8,128)(2,1)S(1)}, bf16[4,16,2048]{2,1,0:T(8,128)(2,1)S(1)}, u32[]{:S(2)}, u32[]{:S(2)}) %collective-permute-start.7) | collective-permute-done | bytes 262176 | tf_op jit(solution)/shard_map/ppermute | solution.py:232
  47.7 0.8 ring_add.9
  48.4 0.0 copy-start.3
  48.4 19.3 %all-to-all-start = ((bf16[4,16,2048]{2,1,0:T(8,128)(2,1)}), bf16[4,16,2048]{2,1,0:T(8,128)(2,1)S(1)}, u32[]{:S(2)}, u32[]{:S(2)}) async-start(bf16[4,16,2048]{2,1,0:T(8,128)(2,1)} %ring_add.9), calls=%async_computation | async-start | bytes 524288 | tf_op jit(solution)/shard_map/all_to_all | solution.py:235
  67.7 0.8 multiply_bitcast_fusion
  68.5 0.1 broadcast_add_fusion
  68.5 18.4 %all-to-all-done.got = bf16[4,16,2048]{2,1,0:T(8,128)(2,1)S(1)} async-done(((bf16[4,16,2048]{2,1,0:T(8,128)(2,1)}), bf16[4,16,2048]{2,1,0:T(8,128)(2,1)S(1)}, u32[]{:S(2)}, u32[]{:S(2)}) %all-to-all-start) | async-done | bytes 262176 | tf_op jit(solution)/shard_map/all_to_all | solution.py:235
  86.9 0.0 copy-start.2
  86.9 1.6 %copy-done.2 = bf16[1,4,512,512]{3,2,1,0:T(8,128)(2,1)S(1)} copy-done((bf16[1,4,512,512]{3,2,1,0:T(8,128)(2,1)S(1)}, bf16[1,4,512,512]{3,2,1,0:T(8,128)(2,1)}, u32[]{:S(2)}) %copy-start.2) | copy-done | bytes 2097176
  88.5 1.0 right_product.1
  89.6 10.8 %all-to-all-start.1 = ((bf16[32,16,128]{2,1,0:T(8,128)(2,1)}), bf16[32,16,128]{2,1,0:T(8,128)(2,1)S(1)}, u32[]{:S(2)}, u32[]{:S(2)}) async-start(bf16[32,16,128]{2,1,0:T(8,128)(2,1)} %get-tuple-element.6), calls=%async_computation.1 | async-start | bytes 262144 | tf_op jit(solution)/shard_map/all_to_all | solution.py:237
  100.4 0.1 iota_add_fusion
  100.5 0.1 add.126
  101.4 0.0 copy-done.3
  101.4 0.7 adam_part.1
  102.1 0.0 all-gather.3.cloned.1.call-done
  102.1 2.3 %fusion.2.lref = bf16[256,512]{1,0:T(8,128)(2,1)S(1)} fusion(bf16[1,1,2048,512]{3,2,1,0:T(8,128)(2,1)} %all-gather.3.cloned.1.call-done, s32[256]{0:T(256)S(1)} %add.126), kind=kOutput, calls=%fused_computation.3 | convolution fusion | flops 537526272 | bytes 2360320 | tf_op jit(solution)/shard_map/dot_general | solution.py:214
  104.4 4.5 %all-to-all-done.1 = bf16[32,16,128]{2,1,0:T(8,128)(2,1)S(1)} async-done(((bf16[32,16,128]{2,1,0:T(8,128)(2,1)}), bf16[32,16,128]{2,1,0:T(8,128)(2,1)S(1)}, u32[]{:S(2)}, u32[]{:S(2)}) %all-to-all-start.1) | async-done | bytes 131104 | tf_op jit(solution)/shard_map/all_to_all | solution.py:237
  109.0 0.3 left_product.1
  109.3 12.1 %all_to_all.15.got = bf16[32,16,128]{2,1,0:T(8,128)(2,1)S(1)} all-to-all(bf16[32,16,128]{2,1,0:T(8,128)(2,1)S(1)} %left_product.1), channel_id=1, replica_groups=mesh['z_lo'=4,'x'=4,'core'=2,'y'=8,'z_hi'=4] {'z_lo','x','core'}, dimensions={0} | all-to-all | bytes 262144 | tf_op jit(solution)/shard_map/all_to_all | solution.py:250
  121.4 0.8 finish.1
  (3 shorter events, 0.1 us)
Async XLA Ops:
  7.2 94.9 %all-gather.3.cloned.1.call-start = ((), (), s32[]{:S(2)}) async-start(), calls=%async_computation.3 | async-start | bytes 2162688 | tf_op jit(solution)/shard_map/all_gather | solution.py:203
  8.9 8.3 %collective-permute-start = (bf16[2,16,2048]{2,1,0:T(8,128)(2,1)S(1)}, bf16[2,16,2048]{2,1,0:T(8,128)(2,1)S(1)}, u32[]{:S(2)}, u32[]{:S(2)}) collective-permute-start(bf16[2,16,2048]{2,1,0:T(8,128)(2,1)S(1)} %get-tuple-element.11), channel_id=1, source_target_pairs={{0,4},{4,8},{8,12},{12,16},{16,20},{20,24},{24,28},{28,0},{1,5},{5... | collective-permute-start | bytes 393224 | tf_op jit(solution)/shard_map/ppermute | solution.py:224
  12.9 7.9 %collective-permute-start.4 = (bf16[2,16,2048]{2,1,0:T(8,128)(2,1)S(1)}, bf16[2,16,2048]{2,1,0:T(8,128)(2,1)S(1)}, u32[]{:S(2)}, u32[]{:S(2)}) collective-permute-start(bf16[2,16,2048]{2,1,0:T(8,128)(2,1)S(1)} %get-tuple-element.10), channel_id=1, source_target_pairs={{0,28},{4,0},{8,4},{12,8},{16,12},{20,16},{24,20},{28,24},{1,29},{... | collective-permute-start | bytes 393224 | tf_op jit(solution)/shard_map/ppermute | solution.py:225
  17.2 1.6 %copy-start = (bf16[1,1,32,16,2048]{4,3,2,1,0:T(8,128)(2,1)S(1)}, bf16[1,1,32,16,2048]{4,3,2,1,0:T(8,128)(2,1)}, u32[]{:S(2)}) copy-start(bf16[1,1,32,16,2048]{4,3,2,1,0:T(8,128)(2,1)} %param.6) | copy-start | bytes 6291460
  18.8 2.1 %copy-start.1 = (bf16[1,1,32,16,2048]{4,3,2,1,0:T(8,128)(2,1)S(1)}, bf16[1,1,32,16,2048]{4,3,2,1,0:T(8,128)(2,1)}, u32[]{:S(2)}) copy-start(bf16[1,1,32,16,2048]{4,3,2,1,0:T(8,128)(2,1)} %param.6) | copy-start | bytes 6291460
  18.8 8.5 %collective-permute-start.1 = (bf16[4,16,2048]{2,1,0:T(8,128)(2,1)S(1)}, bf16[4,16,2048]{2,1,0:T(8,128)(2,1)S(1)}, u32[]{:S(2)}, u32[]{:S(2)}) collective-permute-start(bf16[4,16,2048]{2,1,0:T(8,128)(2,1)S(1)} %ring_first.2), channel_id=1, source_target_pairs={{0,4},{4,8},{8,12},{12,16},{16,20},{20,24},{24,28},{28,0},{1,5},{5... | collective-permute-start | bytes 786440 | tf_op jit(solution)/shard_map/ppermute | solution.py:227
  20.9 8.4 %collective-permute-start.5 = (bf16[4,16,2048]{2,1,0:T(8,128)(2,1)S(1)}, bf16[4,16,2048]{2,1,0:T(8,128)(2,1)S(1)}, u32[]{:S(2)}, u32[]{:S(2)}) collective-permute-start(bf16[4,16,2048]{2,1,0:T(8,128)(2,1)S(1)} %ring_first.3), channel_id=1, source_target_pairs={{0,28},{4,0},{8,4},{12,8},{16,12},{20,16},{24,20},{28,24},{1,29},{... | collective-permute-start | bytes 786440 | tf_op jit(solution)/shard_map/ppermute | solution.py:229
  27.4 8.3 %collective-permute-start.2 = (bf16[4,16,2048]{2,1,0:T(8,128)(2,1)S(1)}, bf16[4,16,2048]{2,1,0:T(8,128)(2,1)S(1)}, u32[]{:S(2)}, u32[]{:S(2)}) collective-permute-start(bf16[4,16,2048]{2,1,0:T(8,128)(2,1)S(1)} %ring_add.5), channel_id=1, source_target_pairs={{0,4},{4,8},{8,12},{12,16},{16,20},{20,24},{24,28},{28,0},{1,5},{5... | collective-permute-start | bytes 786440 | tf_op jit(solution)/shard_map/ppermute | solution.py:231
  29.4 8.3 %collective-permute-start.6 = (bf16[4,16,2048]{2,1,0:T(8,128)(2,1)S(1)}, bf16[4,16,2048]{2,1,0:T(8,128)(2,1)S(1)}, u32[]{:S(2)}, u32[]{:S(2)}) collective-permute-start(bf16[4,16,2048]{2,1,0:T(8,128)(2,1)S(1)} %ring_add.7), channel_id=1, source_target_pairs={{0,28},{4,0},{8,4},{12,8},{16,12},{20,16},{24,20},{28,24},{1,29},{... | collective-permute-start | bytes 786440 | tf_op jit(solution)/shard_map/ppermute | solution.py:232
  35.8 8.7 %collective-permute-start.3 = (bf16[4,16,2048]{2,1,0:T(8,128)(2,1)S(1)}, bf16[4,16,2048]{2,1,0:T(8,128)(2,1)S(1)}, u32[]{:S(2)}, u32[]{:S(2)}) collective-permute-start(bf16[4,16,2048]{2,1,0:T(8,128)(2,1)S(1)} %ring_add.6), channel_id=1, source_target_pairs={{0,4},{4,8},{8,12},{12,16},{16,20},{20,24},{24,28},{28,0},{1,5},{5... | collective-permute-start | bytes 786440 | tf_op jit(solution)/shard_map/ppermute | solution.py:231
  37.9 9.8 %collective-permute-start.7 = (bf16[4,16,2048]{2,1,0:T(8,128)(2,1)S(1)}, bf16[4,16,2048]{2,1,0:T(8,128)(2,1)S(1)}, u32[]{:S(2)}, u32[]{:S(2)}) collective-permute-start(bf16[4,16,2048]{2,1,0:T(8,128)(2,1)S(1)} %ring_add.8), channel_id=1, source_target_pairs={{0,28},{4,0},{8,4},{12,8},{16,12},{20,16},{24,20},{28,24},{1,29},{... | collective-permute-start | bytes 786440 | tf_op jit(solution)/shard_map/ppermute | solution.py:232
  48.4 52.9 %copy-start.3 = (f32[1,1,16,2048]{3,2,1,0:T(8,128)S(1)}, f32[1,1,16,2048]{3,2,1,0:T(8,128)}, u32[]{:S(2)}) copy-start(f32[1,1,16,2048]{3,2,1,0:T(8,128)} %param.7) | copy-start | bytes 393220
  48.4 38.5 %all-to-all-start = ((bf16[4,16,2048]{2,1,0:T(8,128)(2,1)}), bf16[4,16,2048]{2,1,0:T(8,128)(2,1)S(1)}, u32[]{:S(2)}, u32[]{:S(2)}) async-start(bf16[4,16,2048]{2,1,0:T(8,128)(2,1)} %ring_add.9), calls=%async_computation | async-start | bytes 524288 | tf_op jit(solution)/shard_map/all_to_all | solution.py:235
  86.9 1.6 %copy-start.2 = (bf16[1,4,512,512]{3,2,1,0:T(8,128)(2,1)S(1)}, bf16[1,4,512,512]{3,2,1,0:T(8,128)(2,1)}, u32[]{:S(2)}) copy-start(bf16[1,4,512,512]{3,2,1,0:T(8,128)(2,1)} %param.9) | copy-start | bytes 6291460
  89.6 19.4 %all-to-all-start.1 = ((bf16[32,16,128]{2,1,0:T(8,128)(2,1)}), bf16[32,16,128]{2,1,0:T(8,128)(2,1)S(1)}, u32[]{:S(2)}, u32[]{:S(2)}) async-start(bf16[32,16,128]{2,1,0:T(8,128)(2,1)} %get-tuple-element.6), calls=%async_computation.1 | async-start | bytes 262144 | tf_op jit(solution)/shard_map/all_to_all | solution.py:237
Sparse Core Ops, SparseCore 0:
  10.7 81.8 all-gather.2

commit v2 on v1

v2 whole, which is shorter than its diff:
```python
import jax
import jax.numpy as jnp
from jax import lax
from jax.experimental import pallas as pl
from jax.experimental.pallas import tpu as pltpu
from jax.sharding import Mesh, PartitionSpec as P

beta_two = 0.95
adam_eps = 1e-08
FS = ("z_lo", "x", "core")
REP = ("y", "z_hi")
f32 = jnp.float32
bf16 = jnp.bfloat16
VMEM_LIMIT = 24 * 1024 * 1024
SMEM = pl.BlockSpec(memory_space=pltpu.SMEM)
VMEM = pl.BlockSpec(memory_space=pltpu.VMEM)


def call(body, name, ins, outs, scratch=()):
    return pl.pallas_call(
        body,
        in_specs=ins,
        out_specs=jax.tree.map(lambda _: VMEM, outs),
        out_shape=outs,
        scratch_shapes=scratch,
        compiler_params=pltpu.CompilerParams(vmem_limit_bytes=VMEM_LIMIT),
        name=name,
    )


def for_sibling(chunks, index):
    _, parts, rows, width = chunks.shape

    def body(idx, own, out):
        for n in range(3):
            out[n * parts : (n + 1) * parts] = own[idx[n]]

    shape = jax.ShapeDtypeStruct((3 * parts, rows, width), bf16)
    return call(body, "for_sibling", [SMEM, VMEM], shape)(index, chunks)


def add_own(chunks, index, received):
    _, parts, rows, width = chunks.shape

    def body(idx, own, got, out):
        out[...] = (own[idx[0]].astype(f32) + got[...].astype(f32)).astype(bf16)

    shape = jax.ShapeDtypeStruct((parts, rows, width), bf16)
    return call(body, "add_own", [SMEM, VMEM, VMEM], shape)(index, chunks, received)


def add_other(others, place, received):
    parts, rows, width = received.shape

    def body(own, got, out):
        mine = own[place * parts : (place + 1) * parts]
        out[...] = (mine.astype(f32) + got[...].astype(f32)).astype(bf16)

    shape = jax.ShapeDtypeStruct((parts, rows, width), bf16)
    return call(body, "add_other", [VMEM, VMEM], shape)(others, received)


def add_last(chunks, index, one, two):
    _, parts, rows, width = chunks.shape

    def body(idx, own, a, b, *outs):
        for d in range(parts):
            p = idx[1 + d]
            total = own[idx[0], p].astype(f32) + a[p].astype(f32) + b[p].astype(f32)
            outs[d][...] = total.astype(outs[d].dtype)

    shapes = [jax.ShapeDtypeStruct((rows, width), f32 if d == 0 else bf16) for d in range(parts)]
    return call(body, "add_last", [SMEM, VMEM, VMEM, VMEM], shapes)(index, chunks, one, two)


def add_pair(one, two):
    def body(a, b, out):
        out[...] = (a[...].astype(f32) + b[...].astype(f32)).astype(bf16)

    return call(body, "add_pair", [VMEM, VMEM], jax.ShapeDtypeStruct(one.shape, bf16))(one, two)


def right_product(own, one, two, right, owners):
    rows, width = own.shape
    blocks, size, _ = right.shape
    members = owners.shape[0]
    team = members // blocks

    def body(owner, a, b, c, root, summed, pieces):
        total = a[...] + b[...].astype(f32) + c[...].astype(f32)
        summed[...] = total
        grad = total.astype(bf16)
        for k in range(blocks):
            prod = jnp.dot(
                grad[:, k * size : (k + 1) * size], root[k], preferred_element_type=f32
            ).astype(bf16)
            for i in range(team):
                pieces[owner[k * team + i]] = prod

    shapes = (
        jax.ShapeDtypeStruct((rows, width), f32),
        jax.ShapeDtypeStruct((members, rows, size), bf16),
    )
    return call(body, "right_product", [SMEM, VMEM, VMEM, VMEM, VMEM], shapes)(
        owners, own, one, two, right
    )


def adam_part(summed, moment, correction, blocks):
    rows, width = summed.shape
    size = width // blocks

    def body(corr, grad, old, new, squares):
        g = grad[...]
        m = beta_two * old[...] + (1.0 - beta_two) * g * g
        new[...] = m
        d = g / (jnp.sqrt(m / corr[0]) + adam_eps)
        d = d * d
        lane = lax.broadcasted_iota(jnp.int32, (8, 128), 1)
        acc = jnp.zeros((8, 128), f32)
        for k in range(blocks):
            acc = jnp.where(lane == k, jnp.sum(d[:, k * size : (k + 1) * size]), acc)
        squares[...] = acc

    shapes = (
        jax.ShapeDtypeStruct((rows, width), f32),
        jax.ShapeDtypeStruct((8, 128), f32),
    )
    return call(body, "adam_part", [SMEM, VMEM, VMEM], shapes)(correction, summed, moment)


def left_product(left, columns, squares, my_block, blocks):
    held, size = left.shape
    tiles = size // 128
    share = 8 // tiles
    members = held // share

    def body(block, lref, cref, sref, out):
        prod = jnp.dot(lref[...], cref[...], preferred_element_type=f32)
        lane = lax.broadcasted_iota(jnp.int32, (8, 128), 1)
        row = lax.broadcasted_iota(jnp.int32, (8, 128), 0)
        norms = jnp.where(lane == blocks + block[0], jnp.sum(prod * prod), sref[...])
        high = norms.astype(bf16).astype(f32)
        rest = norms - high
        mid = rest.astype(bf16).astype(f32)
        low = rest - mid
        tail = jnp.where(row == 0, high, jnp.where(row == 1, mid, jnp.where(row == 2, low, 0.0)))
        small = prod.astype(bf16)
        to = lax.broadcasted_iota(jnp.int32, (members * 8, held), 0)
        of = lax.broadcasted_iota(jnp.int32, (members * 8, held), 1)
        base = (of // share) * 8 + lax.rem(of, share)
        placed = jnp.zeros((members * 8, 128), f32)
        for x in range(tiles):
            pick = (to == base + x * share).astype(bf16)
            placed += jnp.dot(
                pick, small[:, x * 128 : (x + 1) * 128], preferred_element_type=f32
            )
        out[:, :8, :] = placed.reshape(members, 8, 128).astype(bf16)
        out[:, 8:, :] = jnp.broadcast_to(tail[None], (members, 8, 128)).astype(bf16)

    return call(
        body,
        "left_product",
        [SMEM, VMEM, VMEM, VMEM],
        jax.ShapeDtypeStruct((members, 16, 128), bf16),
    )(my_block, left, columns, squares)


def finish(returned, source, rows, width, blocks):
    members = returned.shape[0]
    tiles = width // blocks // 128

    def body(got, src, out):
        sums = jnp.sum(got[:, 8:, :].astype(f32), axis=0)
        sums = jnp.sum(sums, axis=0, keepdims=True)
        lane = lax.broadcasted_iota(jnp.int32, (1, 128), 1)
        count = members * 8
        ids = lax.broadcasted_iota(jnp.int32, (count, count), 1)
        pick = (src[...] == ids).astype(bf16)
        flat = got[:, :8, :].astype(f32).reshape(count, 128).astype(bf16)
        moved = jnp.dot(pick, flat, preferred_element_type=f32)
        for k in range(blocks):
            adam = jnp.sum(jnp.where(lane == k, sums, 0.0), axis=1, keepdims=True)
            shampoo = jnp.sum(jnp.where(lane == blocks + k, sums, 0.0), axis=1, keepdims=True)
            ratio = jnp.sqrt(adam / (shampoo + 1e-06))
            for x in range(tiles):
                n = k * tiles + x
                tile = moved[n * rows : (n + 1) * rows] * ratio
                out[:, n * 128 : (n + 1) * 128] = tile.astype(bf16)

    return call(body, "finish", [VMEM, VMEM], jax.ShapeDtypeStruct((rows, width), bf16))(
        returned, source
    )


def local(gradients, second_moment, left_rows, right_root, owner_table, step_count):
    ny, nz = lax.axis_size("y"), lax.axis_size("z_hi")
    yi, zi, core = lax.axis_index("y"), lax.axis_index("z_hi"), lax.axis_index("core")
    group_id = lax.axis_index(REP)
    member = lax.axis_index(FS)
    members = lax.axis_size(FS)
    rows, width = gradients.shape[3], gradients.shape[4]
    blocks, size = right_root.shape[1], right_root.shape[3]
    team = members // blocks
    share = rows // team
    tiles = size // 128
    sign = 1 - 2 * core

    def ring(n, turn):
        steps = (turn, -turn)
        return [(c * n + j, c * n + (j + steps[c]) % n) for j in range(n) for c in range(2)]

    def along_y(value):
        return lax.ppermute(value, ("core", "y"), ring(ny, 1))

    def along_z(value, turn):
        return lax.ppermute(value, ("core", "z_hi"), ring(nz, turn))

    def swap(value):
        return lax.ppermute(value, "core", [(0, 1), (1, 0)])

    def y_at(*offsets):
        return jnp.stack([jnp.bitwise_and(yi + sign * o + ny, ny - 1) for o in offsets]).astype(
            jnp.int32
        )

    chunks = gradients.reshape(ny, nz, rows, width)
    far = lax.dynamic_index_in_dim(chunks, jnp.bitwise_and(yi + 4, ny - 1), 0, keepdims=False)
    own = along_y(far)
    others = swap(for_sibling(chunks, y_at(-3, -2, -1)))
    own = along_y(add_own(chunks, y_at(3), own))
    other = along_y(others[:nz])
    own = along_y(add_own(chunks, y_at(2), own))
    other = along_y(add_other(others, 1, other))
    own = along_y(add_own(chunks, y_at(1), own))
    other = along_y(add_other(others, 2, other))
    back = swap(other)

    z_at = [jnp.bitwise_and(zi + sign * o + nz, nz - 1) for o in (0, 2, 1, -1)]
    index = jnp.stack([yi] + z_at).astype(jnp.int32)
    here, farthest, ahead, behind = add_last(chunks, index, own, back)
    farthest = along_z(farthest, 1)
    behind = along_z(behind, -1)
    ahead = along_z(add_pair(ahead, farthest), 1)

    owners = lax.dynamic_index_in_dim(owner_table, group_id, 0, keepdims=False)
    summed, pieces = right_product(here, ahead, behind, right_root[0], owners)
    columns = lax.all_to_all(pieces, FS, 0, 0, tiled=True)

    correction = 1.0 - jnp.power(f32(beta_two), step_count.astype(f32))
    new_moment, squares = adam_part(summed, second_moment[0, 0], correction, blocks)

    items = lax.broadcasted_iota(jnp.int32, (members,), 0)
    my_block = jnp.sum(jnp.where(owners == member, items // team, 0)).reshape(1)
    sent = left_product(
        left_rows[0, 0], columns.reshape(members * rows, size), squares, my_block, blocks
    )
    returned = lax.all_to_all(sent, FS, 0, 0, tiled=True)
    source = (
        owners.reshape(blocks, 1, team, 1) * 8
        + jnp.arange(tiles).reshape(1, tiles, 1, 1) * share
        + jnp.arange(share).reshape(1, 1, 1, share)
    ).reshape(members * 8, 1)
    update = finish(returned, source, rows, width, blocks)
    return (update[None, None], new_moment[None, None])


def solution(mesh):
    fine = Mesh(mesh.devices.reshape(4, 4, 2, 8, 4), FS + REP)
    return jax.shard_map(
        local,
        mesh=fine,
        in_specs=(
            P(REP, FS, None, None, None),
            P(FS, REP, None, None),
            P(REP, FS, None, None),
            P(REP, None, None, None),
            P(),
            P(),
        ),
        out_specs=(P(FS, REP, None, None), P(FS, REP, None, None)),
        check_vma=False,
    )
```

time: 130 us -> 130 us (level)
  starting transfers between devices: 57.6 us -> 74.5 us
  between operations: 14.9 us -> 1.65 us
  blocking collectives: 12.1 us -> 0 us
  Pallas kernels: 4.11 us -> 10.8 us
  waiting for transfers between devices: 32.7 us -> 35.3 us
  matrix products: 2.34 us -> 0 us
  other arithmetic: 0.93 us -> 2.28 us
    ppermute x8 -> x12, starting transfers between devices: 27.5 us -> 55.9 us  [the longest x2 21.4 us: swap(): return lax.ppermute(value, 'core', [(0, 1), (1, 0)])]
    all_to_all x1, starting transfers between devices: 19.3 us -> 4.15 us  [local(): returned = lax.all_to_all(sent, FS, 0, 0, tiled=True)]
    all_to_all x1 -> x0, blocking collectives: 12.1 us -> none  [local(): returned = lax.all_to_all(sent, FS, 0, 0, tiled=True)]
    all_to_all x1, waiting for transfers between devices: 18.4 us -> 8.29 us  [local(): returned = lax.all_to_all(sent, FS, 0, 0, tiled=True)]
    all_to_all x1, waiting for transfers between devices: 4.52 us -> 14.2 us  [local(): columns = lax.all_to_all(pieces, FS, 0, 0, tiled=True)]
    pallas_call x11 -> x12, Pallas kernels: 4.11 us -> 10.8 us  [the longest x3 3.47 us: add_own(): call(body, 'add_own', [SMEM, VMEM, VMEM], shape)(index, chunks, received)]
    ppermute x8 -> x12, waiting for transfers between devices: 9.08 us -> 12.9 us  [the longest x7 7.11 us: along_y(): return lax.ppermute(value, ('core', 'y'), ring(ny, 1))]
    all_to_all x1, starting transfers between devices: 10.8 us -> 14.5 us  [local(): columns = lax.all_to_all(pieces, FS, 0, 0, tiled=True)]
  transfers between devices with their start and end apart: 11 -> 14, of which waited for: 7 -> 7; matrix products, arithmetic and copies ran while one was open for 3% -> 3% of each run, Pallas kernels for 2% -> 3%
where the time goes in v2:
time: 130 us; the launch traced here: 129 us
  starting transfers between devices  74.5 us (57%)
  waiting for transfers between devices  35.3 us (27%)
  Pallas kernels  10.8 us (8%)
  local copies, waits for them, and re-layouts  4.88 us (4%)
  other arithmetic  2.28 us (2%)
  between operations  1.65 us (1%)
    ppermute x2, starting transfers between devices, swap(): return lax.ppermute(value, 'core', [(0, 1), (1, 0)])  21.4 us
    ppermute x7, starting transfers between devices, along_y(): return lax.ppermute(value, ('core', 'y'), ring(ny, 1))  19.7 us
    ppermute x3, starting transfers between devices, along_z(): return lax.ppermute(value, ('core', 'z_hi'), ring(nz, turn))  14.8 us
    all_to_all x1, starting transfers between devices, local(): columns = lax.all_to_all(pieces, FS, 0, 0, tiled=True)  14.5 us
    all_to_all x1, waiting for transfers between devices, local(): columns = lax.all_to_all(pieces, FS, 0, 0, tiled=True)  14.2 us
    all_to_all x1, waiting for transfers between devices, local(): returned = lax.all_to_all(sent, FS, 0, 0, tiled=True)  8.29 us
    ppermute x7, waiting for transfers between devices, along_y(): return lax.ppermute(value, ('core', 'y'), ring(ny, 1))  7.11 us
    ppermute x3, waiting for transfers between devices, along_z(): return lax.ppermute(value, ('core', 'z_hi'), ring(nz, turn))  4.51 us
  transfers between devices with their start and end apart: 14, of which 7 were waited for; matrix products, arithmetic and copies ran while one was open for 3% of the time, Pallas kernels for 3%

profile of v2, /device:TPU:1, one launch (start us, length us, event | category | flops | bytes accessed | tf_op | source)
XLA Modules:
  0.0 129.5 jit_solution(7408563274354612947)
XLA Ops:
  0.6 0.1 pad_add_fusion.idx
  0.7 1.6 %copy-done = bf16[1,1,32,16,2048]{4,3,2,1,0:T(8,128)(2,1)S(1)} copy-done((bf16[1,1,32,16,2048]{4,3,2,1,0:T(8,128)(2,1)S(1)}, bf16[1,1,32,16,2048]{4,3,2,1,0:T(8,128)(2,1)}, u32[]{:S(2)}) %copy-start) | copy-done | bytes 2097176
  2.3 1.5 %for_sibling.1 = bf16[12,16,2048]{2,1,0:T(8,128)(2,1)} custom-call(s32[3]{0:T(128)S(1)} %pad_add_fusion.idx, bf16[8,4,16,2048]{3,2,1,0:T(8,128)(2,1)S(1)} %bitcast.26), custom_call_target="tpu_custom_call" | custom-call | tf_op jit(solution)/shard_map/for_sibling/pallas_call | solution.py:39
  3.8 16.1 %collective-permute-start.4 = (bf16[12,16,2048]{2,1,0:T(8,128)(2,1)}, bf16[12,16,2048]{2,1,0:T(8,128)(2,1)S(1)}, u32[]{:S(2)}, u32[]{:S(2)}) collective-permute-start(bf16[12,16,2048]{2,1,0:T(8,128)(2,1)} %for_sibling.1), channel_id=1, source_target_pairs={{0,32},{32,0},{1,33},{33,1},{2,34},{34,2},{3,35},{35,3},{4,36},{36... | collective-permute-start | bytes 2359304 | tf_op jit(solution)/shard_map/ppermute | solution.py:220
  19.9 0.7 dynamic-slice_bitcast_fusion
  20.6 1.9 %collective-permute-start = (bf16[4,16,2048]{2,1,0:T(8,128)(2,1)}, bf16[4,16,2048]{2,1,0:T(8,128)(2,1)S(1)}, u32[]{:S(2)}, u32[]{:S(2)}) collective-permute-start(bf16[4,16,2048]{2,1,0:T(8,128)(2,1)} %dynamic-slice_bitcast_fusion), channel_id=1, source_target_pairs={{0,4},{32,60},{4,8},{36,32},{8,12},{40,36},{12,16},{44,40},{16,20}... | collective-permute-start | bytes 786440 | tf_op jit(solution)/shard_map/ppermute | solution.py:214
  22.5 0.0 collective-permute-done.4.own
  22.5 0.7 slice.4
  23.2 1.9 %collective-permute-start.5 = (bf16[4,16,2048]{2,1,0:T(8,128)(2,1)}, bf16[4,16,2048]{2,1,0:T(8,128)(2,1)S(1)}, u32[]{:S(2)}, u32[]{:S(2)}) collective-permute-start(bf16[4,16,2048]{2,1,0:T(8,128)(2,1)} %slice.4), channel_id=1, source_target_pairs={{0,4},{32,60},{4,8},{36,32},{8,12},{40,36},{12,16},{44,40},{16,20}... | collective-permute-start | bytes 786440 | tf_op jit(solution)/shard_map/ppermute | solution.py:214
  25.2 3.0 %collective-permute-done.got = bf16[4,16,2048]{2,1,0:T(8,128)(2,1)S(1)} collective-permute-done((bf16[4,16,2048]{2,1,0:T(8,128)(2,1)}, bf16[4,16,2048]{2,1,0:T(8,128)(2,1)S(1)}, u32[]{:S(2)}, u32[]{:S(2)}) %collective-permute-start) | collective-permute-done | bytes 262176 | tf_op jit(solution)/shard_map/ppermute | solution.py:214
  28.2 0.8 add_own.3
  29.0 2.8 %collective-permute-start.1 = (bf16[4,16,2048]{2,1,0:T(8,128)(2,1)}, bf16[4,16,2048]{2,1,0:T(8,128)(2,1)}, u32[]{:S(2)}, u32[]{:S(2)}) collective-permute-start(bf16[4,16,2048]{2,1,0:T(8,128)(2,1)} %add_own.3), channel_id=1, source_target_pairs={{0,4},{32,60},{4,8},{36,32},{8,12},{40,36},{12,16},{44,40},{16,20}... | collective-permute-start | bytes 786440 | tf_op jit(solution)/shard_map/ppermute | solution.py:214
  31.8 0.0 collective-permute-done.5.got
  31.8 0.1 add_other.2
  31.9 2.0 %collective-permute-start.6 = (bf16[4,16,2048]{2,1,0:T(8,128)(2,1)S(1)}, bf16[4,16,2048]{2,1,0:T(8,128)(2,1)S(1)}, u32[]{:S(2)}, u32[]{:S(2)}) collective-permute-start(bf16[4,16,2048]{2,1,0:T(8,128)(2,1)S(1)} %add_other.2), channel_id=1, source_target_pairs={{0,4},{32,60},{4,8},{36,32},{8,12},{40,36},{12,16},{44,40},{16,20}... | collective-permute-start | bytes 786440 | tf_op jit(solution)/shard_map/ppermute | solution.py:214
  33.9 2.5 %collective-permute-done.1.got = bf16[4,16,2048]{2,1,0:T(8,128)(2,1)} collective-permute-done((bf16[4,16,2048]{2,1,0:T(8,128)(2,1)}, bf16[4,16,2048]{2,1,0:T(8,128)(2,1)}, u32[]{:S(2)}, u32[]{:S(2)}) %collective-permute-start.1) | collective-permute-done | bytes 262176 | tf_op jit(solution)/shard_map/ppermute | solution.py:214
  36.4 1.7 %add_own.4 = bf16[4,16,2048]{2,1,0:T(8,128)(2,1)} custom-call(s32[1]{0:T(128)} %bitcast.10.idx, bf16[8,4,16,2048]{3,2,1,0:T(8,128)(2,1)S(1)} %bitcast.29, bf16[4,16,2048]{2,1,0:T(8,128)(2,1)} %collective-permute-done.1.got), custom_call_target="tpu_custom_call" | custom-call | tf_op jit(solution)/shard_map/add_own/pallas_call | solution.py:49
  38.1 4.0 %collective-permute-start.2 = (bf16[4,16,2048]{2,1,0:T(8,128)(2,1)}, bf16[4,16,2048]{2,1,0:T(8,128)(2,1)}, u32[]{:S(2)}, u32[]{:S(2)}) collective-permute-start(bf16[4,16,2048]{2,1,0:T(8,128)(2,1)} %add_own.4), channel_id=1, source_target_pairs={{0,4},{32,60},{4,8},{36,32},{8,12},{40,36},{12,16},{44,40},{16,20}... | collective-permute-start | bytes 786440 | tf_op jit(solution)/shard_map/ppermute | solution.py:214
  42.1 0.1 add_other.3
  42.2 1.9 %collective-permute-start.7 = (bf16[4,16,2048]{2,1,0:T(8,128)(2,1)S(1)}, bf16[4,16,2048]{2,1,0:T(8,128)(2,1)}, u32[]{:S(2)}, u32[]{:S(2)}) collective-permute-start(bf16[4,16,2048]{2,1,0:T(8,128)(2,1)S(1)} %add_other.3), channel_id=1, source_target_pairs={{0,4},{32,60},{4,8},{36,32},{8,12},{40,36},{12,16},{44,40},{16,20}... | collective-permute-start | bytes 786440 | tf_op jit(solution)/shard_map/ppermute | solution.py:214
  44.1 1.6 %collective-permute-done.2.got = bf16[4,16,2048]{2,1,0:T(8,128)(2,1)} collective-permute-done((bf16[4,16,2048]{2,1,0:T(8,128)(2,1)}, bf16[4,16,2048]{2,1,0:T(8,128)(2,1)}, u32[]{:S(2)}, u32[]{:S(2)}) %collective-permute-start.2) | collective-permute-done | bytes 262176 | tf_op jit(solution)/shard_map/ppermute | solution.py:214
  45.7 1.0 add_own.5
  46.8 5.0 %collective-permute-start.3 = (bf16[4,16,2048]{2,1,0:T(8,128)(2,1)S(1)}, bf16[4,16,2048]{2,1,0:T(8,128)(2,1)S(1)}, u32[]{:S(2)}, u32[]{:S(2)}) collective-permute-start(bf16[4,16,2048]{2,1,0:T(8,128)(2,1)S(1)} %add_own.5), channel_id=1, source_target_pairs={{0,4},{32,60},{4,8},{36,32},{8,12},{40,36},{12,16},{44,40},{16,20}... | collective-permute-start | bytes 786440 | tf_op jit(solution)/shard_map/ppermute | solution.py:214
  51.8 5.4 %collective-permute-start.8 = (bf16[4,16,2048]{2,1,0:T(8,128)(2,1)}, bf16[4,16,2048]{2,1,0:T(8,128)(2,1)S(1)}, u32[]{:S(2)}, u32[]{:S(2)}) collective-permute-start(bf16[4,16,2048]{2,1,0:T(8,128)(2,1)} %collective-permute-done.7), channel_id=1, source_target_pairs={{0,32},{32,0},{1,33},{33,1},{2,34},{34,2},{3,35},{35,3},{4,36},{36... | collective-permute-start | bytes 786440 | tf_op jit(solution)/shard_map/ppermute | solution.py:220
  57.2 0.1 stack.44.idx
  57.3 1.2 collective-permute-done.8.b
  58.5 0.6 add_last.1
  59.2 0.0 copy-start.3
  59.2 0.0 copy-start.4
  59.2 5.6 %collective-permute-start.9 = (bf16[16,2048]{1,0:T(8,128)(2,1)S(1)}, bf16[16,2048]{1,0:T(8,128)(2,1)S(1)}, u32[]{:S(2)}, u32[]{:S(2)}) collective-permute-start(bf16[16,2048]{1,0:T(8,128)(2,1)S(1)} %get-tuple-element.12), channel_id=1, source_target_pairs={{0,1},{32,35},{1,2},{33,32},{2,3},{34,33},{3,0},{35,34},{4,5},{36,... | collective-permute-start | bytes 196616 | tf_op jit(solution)/shard_map/ppermute | solution.py:217
  64.9 3.7 %collective-permute-start.11 = (bf16[16,2048]{1,0:T(8,128)(2,1)S(1)}, bf16[16,2048]{1,0:T(8,128)(2,1)S(1)}, u32[]{:S(2)}, u32[]{:S(2)}) collective-permute-start(bf16[16,2048]{1,0:T(8,128)(2,1)S(1)} %get-tuple-element.13), channel_id=1, source_target_pairs={{0,3},{32,33},{1,0},{33,34},{2,1},{34,35},{3,2},{35,32},{4,7},{36,... | collective-permute-start | bytes 196616 | tf_op jit(solution)/shard_map/ppermute | solution.py:217
  68.6 5.5 %collective-permute-start.10 = (bf16[16,2048]{1,0:T(8,128)(2,1)S(1)}, bf16[16,2048]{1,0:T(8,128)(2,1)S(1)}, u32[]{:S(2)}, u32[]{:S(2)}) collective-permute-start(bf16[16,2048]{1,0:T(8,128)(2,1)S(1)} %add_pair.1), channel_id=1, source_target_pairs={{0,1},{32,35},{1,2},{33,32},{2,3},{34,33},{3,0},{35,34},{4,5},{36,... | collective-permute-start | bytes 196616 | tf_op jit(solution)/shard_map/ppermute | solution.py:217
  74.1 1.3 %fusion = (s32[]{:T(128)}, s32[32]{0:T(128)S(1)}) fusion(s32[]{:T(128)S(6)} %add.122, s32[32,32]{1,0:T(8,128)} %param.10, s32[]{:T(128)S(6)} %select_n.17), kind=kLoop, calls=%fused_computation.8 | loop fusion | flops 351 | bytes 268 | tf_op jit(solution)/shard_map/reduce_sum | solution.py:254
  75.4 4.5 %collective-permute-done.10.b = bf16[16,2048]{1,0:T(8,128)(2,1)S(1)} collective-permute-done((bf16[16,2048]{1,0:T(8,128)(2,1)S(1)}, bf16[16,2048]{1,0:T(8,128)(2,1)S(1)}, u32[]{:S(2)}, u32[]{:S(2)}) %collective-permute-start.10) | collective-permute-done | bytes 65568 | tf_op jit(solution)/shard_map/ppermute | solution.py:217
  79.9 1.6 %copy-done.2 = bf16[1,4,512,512]{3,2,1,0:T(8,128)(2,1)S(1)} copy-done((bf16[1,4,512,512]{3,2,1,0:T(8,128)(2,1)S(1)}, bf16[1,4,512,512]{3,2,1,0:T(8,128)(2,1)}, u32[]{:S(2)}) %copy-start.2) | copy-done | bytes 2097176
  81.5 1.7 %right_product.1 = (f32[16,2048]{1,0:T(8,128)S(1)}, bf16[32,16,512]{2,1,0:T(8,128)(2,1)}) custom-call(s32[32]{0:T(128)S(1)} %get-tuple-element.19.owner, f32[16,2048]{1,0:T(8,128)S(1)} %get-tuple-element.10.a, bf16[16,2048]{1,0:T(8,128)(2,1)S(1)} %collective-permute-done.10.b, bf16[16,2048]{1,0:T(8,128)(2,1)S(1)} %collective-permute-done.11.c, ...), custom_call_target="tpu_custom_call" | custom-call | tf_op jit(solution)/shard_map/right_product/pallas_call | solution.py:104
  83.3 14.5 %all-to-all-start = ((bf16[32,16,512]{2,1,0:T(8,128)(2,1)}), bf16[32,16,512]{2,1,0:T(8,128)(2,1)S(1)}, u32[]{:S(2)}, u32[]{:S(2)}) async-start(bf16[32,16,512]{2,1,0:T(8,128)(2,1)} %get-tuple-element.14), calls=%async_computation | async-start | bytes 1048576 | tf_op jit(solution)/shard_map/all_to_all | solution.py:248
  98.4 0.7 multiply_reduce_fusion
  99.1 0.1 mul.62
  99.3 0.7 adam_part.1
  100.0 14.2 %all-to-all-done = bf16[32,16,512]{2,1,0:T(8,128)(2,1)S(1)} async-done(((bf16[32,16,512]{2,1,0:T(8,128)(2,1)}), bf16[32,16,512]{2,1,0:T(8,128)(2,1)S(1)}, u32[]{:S(2)}, u32[]{:S(2)}) %all-to-all-start) | async-done | bytes 524320 | tf_op jit(solution)/shard_map/all_to_all | solution.py:248
  114.2 1.8 %left_product.1 = bf16[32,16,128]{2,1,0:T(8,128)(2,1)} custom-call(s32[1]{0:T(128)} %bitcast.1.block, bf16[64,512]{1,0:T(8,128)(2,1)S(1)} %bitcast.35, bf16[512,512]{1,0:T(8,128)(2,1)S(1)} %bitcast.33, f32[8,128]{1,0:T(8,128)S(1)} %get-tuple-element.16.sref), custom_call_target="tpu_custom_call" | custom-call | tf_op jit(solution)/shard_map/left_product/pallas_call | solution.py:161
  115.9 4.1 %all-to-all-start.1 = ((bf16[32,16,128]{2,1,0:T(8,128)(2,1)}), bf16[32,16,128]{2,1,0:T(8,128)(2,1)S(1)}, u32[]{:S(2)}, u32[]{:S(2)}) async-start(bf16[32,16,128]{2,1,0:T(8,128)(2,1)} %left_product.1), calls=%async_computation.1 | async-start | bytes 262144 | tf_op jit(solution)/shard_map/all_to_all | solution.py:258
  120.1 0.1 broadcast_add_fusion
  120.2 0.1 iota_add_fusion
  120.3 0.1 add.151.src
  120.3 8.3 %all-to-all-done.1.got = bf16[32,16,128]{2,1,0:T(8,128)(2,1)S(1)} async-done(((bf16[32,16,128]{2,1,0:T(8,128)(2,1)}), bf16[32,16,128]{2,1,0:T(8,128)(2,1)S(1)}, u32[]{:S(2)}, u32[]{:S(2)}) %all-to-all-start.1) | async-done | bytes 131104 | tf_op jit(solution)/shard_map/all_to_all | solution.py:258
  128.6 0.9 finish.1
  (13 shorter events, 0.0 us)
Async XLA Ops:
  0.7 1.6 %copy-start = (bf16[1,1,32,16,2048]{4,3,2,1,0:T(8,128)(2,1)S(1)}, bf16[1,1,32,16,2048]{4,3,2,1,0:T(8,128)(2,1)}, u32[]{:S(2)}) copy-start(bf16[1,1,32,16,2048]{4,3,2,1,0:T(8,128)(2,1)} %param.6) | copy-start | bytes 6291460
  2.3 17.5 %copy-start.1 = (bf16[1,1,32,16,2048]{4,3,2,1,0:T(8,128)(2,1)S(1)}, bf16[1,1,32,16,2048]{4,3,2,1,0:T(8,128)(2,1)}, u32[]{:S(2)}) copy-start(bf16[1,1,32,16,2048]{4,3,2,1,0:T(8,128)(2,1)} %param.6) | copy-start | bytes 6291460
  3.8 18.7 %collective-permute-start.4 = (bf16[12,16,2048]{2,1,0:T(8,128)(2,1)}, bf16[12,16,2048]{2,1,0:T(8,128)(2,1)S(1)}, u32[]{:S(2)}, u32[]{:S(2)}) collective-permute-start(bf16[12,16,2048]{2,1,0:T(8,128)(2,1)} %for_sibling.1), channel_id=1, source_target_pairs={{0,32},{32,0},{1,33},{33,1},{2,34},{34,2},{3,35},{35,3},{4,36},{36... | collective-permute-start | bytes 2359304 | tf_op jit(solution)/shard_map/ppermute | solution.py:220
  20.6 7.6 %collective-permute-start = (bf16[4,16,2048]{2,1,0:T(8,128)(2,1)}, bf16[4,16,2048]{2,1,0:T(8,128)(2,1)S(1)}, u32[]{:S(2)}, u32[]{:S(2)}) collective-permute-start(bf16[4,16,2048]{2,1,0:T(8,128)(2,1)} %dynamic-slice_bitcast_fusion), channel_id=1, source_target_pairs={{0,4},{32,60},{4,8},{36,32},{8,12},{40,36},{12,16},{44,40},{16,20}... | collective-permute-start | bytes 786440 | tf_op jit(solution)/shard_map/ppermute | solution.py:214
  23.2 8.6 %collective-permute-start.5 = (bf16[4,16,2048]{2,1,0:T(8,128)(2,1)}, bf16[4,16,2048]{2,1,0:T(8,128)(2,1)S(1)}, u32[]{:S(2)}, u32[]{:S(2)}) collective-permute-start(bf16[4,16,2048]{2,1,0:T(8,128)(2,1)} %slice.4), channel_id=1, source_target_pairs={{0,4},{32,60},{4,8},{36,32},{8,12},{40,36},{12,16},{44,40},{16,20}... | collective-permute-start | bytes 786440 | tf_op jit(solution)/shard_map/ppermute | solution.py:214
  29.0 7.4 %collective-permute-start.1 = (bf16[4,16,2048]{2,1,0:T(8,128)(2,1)}, bf16[4,16,2048]{2,1,0:T(8,128)(2,1)}, u32[]{:S(2)}, u32[]{:S(2)}) collective-permute-start(bf16[4,16,2048]{2,1,0:T(8,128)(2,1)} %add_own.3), channel_id=1, source_target_pairs={{0,4},{32,60},{4,8},{36,32},{8,12},{40,36},{12,16},{44,40},{16,20}... | collective-permute-start | bytes 786440 | tf_op jit(solution)/shard_map/ppermute | solution.py:214
  31.9 10.3 %collective-permute-start.6 = (bf16[4,16,2048]{2,1,0:T(8,128)(2,1)S(1)}, bf16[4,16,2048]{2,1,0:T(8,128)(2,1)S(1)}, u32[]{:S(2)}, u32[]{:S(2)}) collective-permute-start(bf16[4,16,2048]{2,1,0:T(8,128)(2,1)S(1)} %add_other.2), channel_id=1, source_target_pairs={{0,4},{32,60},{4,8},{36,32},{8,12},{40,36},{12,16},{44,40},{16,20}... | collective-permute-start | bytes 786440 | tf_op jit(solution)/shard_map/ppermute | solution.py:214
  38.1 7.7 %collective-permute-start.2 = (bf16[4,16,2048]{2,1,0:T(8,128)(2,1)}, bf16[4,16,2048]{2,1,0:T(8,128)(2,1)}, u32[]{:S(2)}, u32[]{:S(2)}) collective-permute-start(bf16[4,16,2048]{2,1,0:T(8,128)(2,1)} %add_own.4), channel_id=1, source_target_pairs={{0,4},{32,60},{4,8},{36,32},{8,12},{40,36},{12,16},{44,40},{16,20}... | collective-permute-start | bytes 786440 | tf_op jit(solution)/shard_map/ppermute | solution.py:214
  42.2 9.6 %collective-permute-start.7 = (bf16[4,16,2048]{2,1,0:T(8,128)(2,1)S(1)}, bf16[4,16,2048]{2,1,0:T(8,128)(2,1)}, u32[]{:S(2)}, u32[]{:S(2)}) collective-permute-start(bf16[4,16,2048]{2,1,0:T(8,128)(2,1)S(1)} %add_other.3), channel_id=1, source_target_pairs={{0,4},{32,60},{4,8},{36,32},{8,12},{40,36},{12,16},{44,40},{16,20}... | collective-permute-start | bytes 786440 | tf_op jit(solution)/shard_map/ppermute | solution.py:214
  46.8 10.5 %collective-permute-start.3 = (bf16[4,16,2048]{2,1,0:T(8,128)(2,1)S(1)}, bf16[4,16,2048]{2,1,0:T(8,128)(2,1)S(1)}, u32[]{:S(2)}, u32[]{:S(2)}) collective-permute-start(bf16[4,16,2048]{2,1,0:T(8,128)(2,1)S(1)} %add_own.5), channel_id=1, source_target_pairs={{0,4},{32,60},{4,8},{36,32},{8,12},{40,36},{12,16},{44,40},{16,20}... | collective-permute-start | bytes 786440 | tf_op jit(solution)/shard_map/ppermute | solution.py:214
  51.8 6.7 %collective-permute-start.8 = (bf16[4,16,2048]{2,1,0:T(8,128)(2,1)}, bf16[4,16,2048]{2,1,0:T(8,128)(2,1)S(1)}, u32[]{:S(2)}, u32[]{:S(2)}) collective-permute-start(bf16[4,16,2048]{2,1,0:T(8,128)(2,1)} %collective-permute-done.7), channel_id=1, source_target_pairs={{0,32},{32,0},{1,33},{33,1},{2,34},{34,2},{3,35},{35,3},{4,36},{36... | collective-permute-start | bytes 786440 | tf_op jit(solution)/shard_map/ppermute | solution.py:220
  59.2 40.1 %copy-start.3 = (f32[1,1,16,2048]{3,2,1,0:T(8,128)S(1)}, f32[1,1,16,2048]{3,2,1,0:T(8,128)}, u32[]{:S(2)}) copy-start(f32[1,1,16,2048]{3,2,1,0:T(8,128)} %param.7) | copy-start | bytes 393220
  59.2 55.0 %copy-start.4 = (bf16[1,1,64,512]{3,2,1,0:T(8,128)(2,1)S(1)}, bf16[1,1,64,512]{3,2,1,0:T(8,128)(2,1)}, u32[]{:S(2)}) copy-start(bf16[1,1,64,512]{3,2,1,0:T(8,128)(2,1)} %param.8) | copy-start | bytes 196612
  59.2 9.4 %collective-permute-start.9 = (bf16[16,2048]{1,0:T(8,128)(2,1)S(1)}, bf16[16,2048]{1,0:T(8,128)(2,1)S(1)}, u32[]{:S(2)}, u32[]{:S(2)}) collective-permute-start(bf16[16,2048]{1,0:T(8,128)(2,1)S(1)} %get-tuple-element.12), channel_id=1, source_target_pairs={{0,1},{32,35},{1,2},{33,32},{2,3},{34,33},{3,0},{35,34},{4,5},{36,... | collective-permute-start | bytes 196616 | tf_op jit(solution)/shard_map/ppermute | solution.py:217
  64.9 10.6 %collective-permute-start.11 = (bf16[16,2048]{1,0:T(8,128)(2,1)S(1)}, bf16[16,2048]{1,0:T(8,128)(2,1)S(1)}, u32[]{:S(2)}, u32[]{:S(2)}) collective-permute-start(bf16[16,2048]{1,0:T(8,128)(2,1)S(1)} %get-tuple-element.13), channel_id=1, source_target_pairs={{0,3},{32,33},{1,0},{33,34},{2,1},{34,35},{3,2},{35,32},{4,7},{36,... | collective-permute-start | bytes 196616 | tf_op jit(solution)/shard_map/ppermute | solution.py:217
  68.6 11.4 %collective-permute-start.10 = (bf16[16,2048]{1,0:T(8,128)(2,1)S(1)}, bf16[16,2048]{1,0:T(8,128)(2,1)S(1)}, u32[]{:S(2)}, u32[]{:S(2)}) collective-permute-start(bf16[16,2048]{1,0:T(8,128)(2,1)S(1)} %add_pair.1), channel_id=1, source_target_pairs={{0,1},{32,35},{1,2},{33,32},{2,3},{34,33},{3,0},{35,34},{4,5},{36,... | collective-permute-start | bytes 196616 | tf_op jit(solution)/shard_map/ppermute | solution.py:217
  79.9 1.6 %copy-start.2 = (bf16[1,4,512,512]{3,2,1,0:T(8,128)(2,1)S(1)}, bf16[1,4,512,512]{3,2,1,0:T(8,128)(2,1)}, u32[]{:S(2)}) copy-start(bf16[1,4,512,512]{3,2,1,0:T(8,128)(2,1)} %param.9) | copy-start | bytes 6291460
  83.3 30.9 %all-to-all-start = ((bf16[32,16,512]{2,1,0:T(8,128)(2,1)}), bf16[32,16,512]{2,1,0:T(8,128)(2,1)S(1)}, u32[]{:S(2)}, u32[]{:S(2)}) async-start(bf16[32,16,512]{2,1,0:T(8,128)(2,1)} %get-tuple-element.14), calls=%async_computation | async-start | bytes 1048576 | tf_op jit(solution)/shard_map/all_to_all | solution.py:248
  115.9 12.7 %all-to-all-start.1 = ((bf16[32,16,128]{2,1,0:T(8,128)(2,1)}), bf16[32,16,128]{2,1,0:T(8,128)(2,1)S(1)}, u32[]{:S(2)}, u32[]{:S(2)}) async-start(bf16[32,16,128]{2,1,0:T(8,128)(2,1)} %left_product.1), calls=%async_computation.1 | async-start | bytes 262144 | tf_op jit(solution)/shard_map/all_to_all | solution.py:258

commit v3 on v2

v3 whole, which is shorter than its diff:
```python
import math

import jax
import jax.numpy as jnp
from jax import lax
from jax.experimental import pallas as pl
from jax.experimental.pallas import tpu as pltpu
from jax.sharding import Mesh, PartitionSpec as P

beta_two = 0.95
adam_eps = 1e-08
log_beta = math.log(beta_two)
FS = ("z_lo", "x", "core")
REP = ("y", "z_hi")
f32 = jnp.float32
bf16 = jnp.bfloat16
VMEM_LIMIT = 24 * 1024 * 1024
SMEM = pl.BlockSpec(memory_space=pltpu.SMEM)
VMEM = pl.BlockSpec(memory_space=pltpu.VMEM)


def call(body, name, ins, outs, scratch=()):
    return pl.pallas_call(
        body,
        in_specs=ins,
        out_specs=jax.tree.map(lambda _: VMEM, outs),
        out_shape=outs,
        scratch_shapes=scratch,
        compiler_params=pltpu.CompilerParams(vmem_limit_bytes=VMEM_LIMIT),
        name=name,
    )


def far_halves(chunks, index):
    _, parts, rows, width = chunks.shape
    half = parts // 2

    def body(idx, own, low, high):
        low[...] = own[0, :half]
        high[...] = own[0, half:]

    shape = jax.ShapeDtypeStruct((half, rows, width), bf16)
    block = pl.BlockSpec((half, rows, width), lambda i, idx: (0, 0, 0))
    return pl.pallas_call(
        body,
        grid_spec=pltpu.PrefetchScalarGridSpec(
            num_scalar_prefetch=1,
            grid=(1,),
            in_specs=[pl.BlockSpec((1, parts, rows, width), lambda i, idx: (idx[0], 0, 0, 0))],
            out_specs=[block, block],
        ),
        out_shape=[shape, shape],
        compiler_params=pltpu.CompilerParams(vmem_limit_bytes=VMEM_LIMIT),
        name="far_halves",
    )(index, chunks)


def ring_add(chunks, scalars, place, *received, covers=None):
    _, parts, rows, width = chunks.shape
    half = parts // 2

    def body(idx, own, *refs):
        if covers is None:
            total = own[0].astype(f32)
            for got in refs[:-1]:
                total = total + got[...].astype(f32)
            refs[-1][...] = total.astype(bf16)
        else:
            i = pl.program_id(0)

            @pl.when(i == covers)
            def _():
                refs[1][...] = (own[0].astype(f32) + refs[0][...].astype(f32)).astype(bf16)

            @pl.when(i != covers)
            def _():
                refs[1][...] = own[0]

    block = pl.BlockSpec((half, rows, width), lambda i, idx: (i, 0, 0))
    if covers is not None:
        got_block = pl.BlockSpec((half, rows, width), lambda i, idx: (0, 0, 0))
    else:
        got_block = block
    return pl.pallas_call(
        body,
        grid_spec=pltpu.PrefetchScalarGridSpec(
            num_scalar_prefetch=1,
            grid=(2,),
            in_specs=[
                pl.BlockSpec((1, half, rows, width), lambda i, idx: (idx[place], i, 0, 0))
            ]
            + [got_block] * len(received),
            out_specs=block,
        ),
        out_shape=jax.ShapeDtypeStruct((parts, rows, width), bf16),
        compiler_params=pltpu.CompilerParams(vmem_limit_bytes=VMEM_LIMIT),
        name="ring_add",
    )(scalars, chunks, *received)


def right_and_adam(parts, right, moment, scalars, step_count, owners_at, members):
    count, rows, width = parts.shape
    blocks, size, _ = right.shape
    team = members // blocks

    def body(idx, step, got, root, old, pieces, new, squares):
        total = got[0].astype(f32)
        for i in range(1, count):
            total = total + got[i].astype(f32)
        grad = total.astype(bf16)
        for k in range(blocks):
            prod = jnp.dot(
                grad[:, k * size : (k + 1) * size], root[k], preferred_element_type=f32
            ).astype(bf16)
            for i in range(team):
                pieces[idx[owners_at + k * team + i]] = prod
        steps = jnp.full((8, 128), step[0], jnp.int32).astype(f32)
        correction = (1.0 - jnp.exp(steps * log_beta))[:1, :1]
        m = beta_two * old[...] + (1.0 - beta_two) * total * total
        new[...] = m
        d = total / (jnp.sqrt(m / correction) + adam_eps)
        d = d * d
        lane = lax.broadcasted_iota(jnp.int32, (8, 128), 1)
        acc = jnp.zeros((8, 128), f32)
        for k in range(blocks):
            acc = jnp.where(lane == k, jnp.sum(d[:, k * size : (k + 1) * size]), acc)
        squares[...] = acc

    shapes = (
        jax.ShapeDtypeStruct((members, rows, size), bf16),
        jax.ShapeDtypeStruct((rows, width), f32),
        jax.ShapeDtypeStruct((8, 128), f32),
    )
    return call(body, "right_and_adam", [SMEM, SMEM, VMEM, VMEM, VMEM], shapes)(
        scalars, step_count, parts, right, moment
    )


def left_product(left, columns, squares, scalars, member_at, owners_at, blocks):
    held, size = left.shape
    tiles = size // 128
    share = 8 // tiles
    members = held // share
    team = members // blocks

    def body(idx, lref, cref, sref, out):
        prod = jnp.dot(lref[...], cref[...], preferred_element_type=f32)
        my_block = jnp.int32(0)
        for m in range(team, members):
            my_block = jnp.where(idx[owners_at + m] == idx[member_at], m // team, my_block)
        lane = lax.broadcasted_iota(jnp.int32, (8, 128), 1)
        row = lax.broadcasted_iota(jnp.int32, (8, 128), 0)
        norms = jnp.where(lane == blocks + my_block, jnp.sum(prod * prod), sref[...])
        high = norms.astype(bf16).astype(f32)
        rest = norms - high
        mid = rest.astype(bf16).astype(f32)
        low = rest - mid
        tail = jnp.where(row == 0, high, jnp.where(row == 1, mid, jnp.where(row == 2, low, 0.0)))
        small = prod.astype(bf16)
        to = lax.broadcasted_iota(jnp.int32, (members * 8, held), 0)
        of = lax.broadcasted_iota(jnp.int32, (members * 8, held), 1)
        base = (of // share) * 8 + lax.rem(of, share)
        placed = jnp.zeros((members * 8, 128), f32)
        for x in range(tiles):
            pick = (to == base + x * share).astype(bf16)
            placed += jnp.dot(
                pick, small[:, x * 128 : (x + 1) * 128], preferred_element_type=f32
            )
        out[:, :8, :] = placed.reshape(members, 8, 128).astype(bf16)
        out[:, 8:, :] = jnp.broadcast_to(tail[None], (members, 8, 128)).astype(bf16)

    return call(
        body,
        "left_product",
        [SMEM, VMEM, VMEM, VMEM],
        jax.ShapeDtypeStruct((members, 16, 128), bf16),
    )(scalars, left, columns, squares)


def finish(returned, scalars, owners_at, rows, width, blocks):
    members = returned.shape[0]
    tiles = width // blocks // 128
    team = members // blocks
    share = rows // team
    count = team * 8

    def body(idx, got, out, held):
        sums = jnp.sum(got[:, 8:, :].astype(f32), axis=0)
        sums = jnp.sum(sums, axis=0, keepdims=True)
        lane = lax.broadcasted_iota(jnp.int32, (1, 128), 1)
        to = lax.broadcasted_iota(jnp.int32, (count, count), 0)
        of = lax.broadcasted_iota(jnp.int32, (count, count), 1)
        inner = lax.rem(to, rows)
        pick = (of == (inner // share) * 8 + (to // rows) * share + lax.rem(inner, share)).astype(f32)
        for k in range(blocks):
            for i in range(team):
                m = k * team + i
                held[m] = got[idx[owners_at + m], :8, :].astype(f32)
            adam = jnp.sum(jnp.where(lane == k, sums, 0.0), axis=1, keepdims=True)
            shampoo = jnp.sum(jnp.where(lane == blocks + k, sums, 0.0), axis=1, keepdims=True)
            ratio = jnp.sqrt(adam / (shampoo + 1e-06))
            flat = held[k * team : (k + 1) * team].reshape(count, 128).astype(bf16)
            moved = jnp.dot(pick.astype(bf16), flat, preferred_element_type=f32)
            for x in range(tiles):
                n = k * tiles + x
                tile = moved[x * rows : (x + 1) * rows] * ratio
                out[:, n * 128 : (n + 1) * 128] = tile.astype(bf16)

    return call(
        body,
        "finish",
        [SMEM, VMEM],
        jax.ShapeDtypeStruct((rows, width), bf16),
        [pltpu.VMEM((members, 8, 128), f32)],
    )(scalars, returned)


def local(gradients, second_moment, left_rows, right_root, owner_table, step_count):
    ny, nz = lax.axis_size("y"), lax.axis_size("z_hi")
    yi = lax.axis_index("y")
    members = lax.axis_size(FS)
    rows, width = gradients.shape[3], gradients.shape[4]
    size = right_root.shape[3]
    blocks = right_root.shape[1]
    up = [(j, (j + 1) % ny) for j in range(ny)]
    down = [(j, (j - 1) % ny) for j in range(ny)]

    places = jnp.bitwise_and(yi + jnp.arange(ny), ny - 1)
    owners = lax.dynamic_index_in_dim(owner_table, lax.axis_index(REP), 0, keepdims=False)
    scalars = jnp.concatenate([places, lax.axis_index(FS).reshape(1), owners]).astype(jnp.int32)
    member_at, owners_at = ny, ny + 1

    chunks = gradients.reshape(ny, nz, rows, width)
    far = jnp.bitwise_and(yi + 4, ny - 1).astype(jnp.int32).reshape(1)
    above, below = far_halves(chunks, far)
    above = lax.ppermute(above, "y", up)
    below = lax.ppermute(below, "y", down)
    above = lax.ppermute(ring_add(chunks, scalars, 3, above, covers=0), "y", up)
    below = lax.ppermute(ring_add(chunks, scalars, 5, below, covers=1), "y", down)
    for s in (2, 1):
        above = lax.ppermute(ring_add(chunks, scalars, s, above), "y", up)
        below = lax.ppermute(ring_add(chunks, scalars, ny - s, below), "y", down)
    part = ring_add(chunks, scalars, 0, above, below)

    parts = lax.all_to_all(part, "z_hi", 0, 0, tiled=True)
    pieces, new_moment, squares = right_and_adam(
        parts, right_root[0], second_moment[0, 0], scalars, step_count, owners_at, members
    )
    columns = lax.all_to_all(pieces, FS, 0, 0, tiled=True).reshape(members * rows, size)
    sent = left_product(
        left_rows[0, 0], columns, squares, scalars, member_at, owners_at, blocks
    )
    returned = lax.all_to_all(sent, FS, 0, 0, tiled=True)
    update = finish(returned, scalars, owners_at, rows, width, blocks)
    return (update[None, None], new_moment[None, None])


def solution(mesh):
    fine = Mesh(mesh.devices.reshape(4, 4, 2, 8, 4), FS + REP)
    return jax.shard_map(
        local,
        mesh=fine,
        in_specs=(
            P(REP, FS, None, None, None),
            P(FS, REP, None, None),
            P(REP, FS, None, None),
            P(REP, None, None, None),
            P(),
            P(),
        ),
        out_specs=(P(FS, REP, None, None), P(FS, REP, None, None)),
        check_vma=False,
    )
```

time: 130 us -> 130 us (level)
  blocking collectives: 0 us -> 42.1 us
  starting transfers between devices: 74.5 us -> 49.8 us
  waiting for transfers between devices: 35.3 us -> 24.1 us
  other arithmetic: 2.28 us -> 0.08 us
  Pallas kernels: 10.8 us -> 9.05 us
  local copies, waits for them, and re-layouts: 4.88 us -> 3.21 us
    all_to_all x0 -> x2, blocking collectives: none -> 42.1 us  [the longest x1 29.6 us: local(): lax.all_to_all(pieces, FS, 0, 0, tiled=True).reshape(members * rows, size)]
    ppermute x12 -> x8, starting transfers between devices: 55.9 us -> 29.6 us  [the longest x2 10 us: local(): below = lax.ppermute(ring_add(chunks, scalars, ny - s, below), 'y', down)]
    all_to_all x2 -> x1, waiting for transfers between devices: 22.5 us -> 15.2 us  [local(): parts = lax.all_to_all(part, 'z_hi', 0, 0, tiled=True)]
    ppermute x12 -> x8, waiting for transfers between devices: 12.9 us -> 8.91 us  [the longest x2 4.41 us: local(): above = lax.ppermute(ring_add(chunks, scalars, s, above), 'y', up)]
    all_to_all x2 -> x1, starting transfers between devices: 18.6 us -> 20.1 us  [local(): parts = lax.all_to_all(part, 'z_hi', 0, 0, tiled=True)]
    reduce_sum x1 -> x0, other arithmetic: 1.33 us -> none  [local(): my_block = jnp.sum(jnp.where(owners == member, items // team, 0)).reshape(1)]
    pallas_call x11 -> x10, Pallas kernels: 9.06 us -> 8.05 us  [the longest x7 5.22 us: ring_add(): pl.pallas_call(body, grid_spec=pltpu.PrefetchScalarGridSpec(num_scalar_pr...]
    unnamed x10 -> x12, local copies, waits for them, and re-layouts: 3.2 us -> 3.2 us
  transfers between devices with their start and end apart: 14 -> 9, of which waited for: 7 -> 6; matrix products, arithmetic and copies ran while one was open for 3% -> 0% of each run, Pallas kernels for 3% -> 3%
where the time goes in v3:
time: 130 us
  starting transfers between devices  49.8 us (38%)
  blocking collectives  42.1 us (32%)
  waiting for transfers between devices  24.1 us (19%)
  Pallas kernels  9.05 us (7%)
  local copies, waits for them, and re-layouts  3.21 us (2%)
  between operations  1.49 us (1%)
    all_to_all x1, blocking collectives, local(): lax.all_to_all(pieces, FS, 0, 0, tiled=True).reshape(members * rows, size)  29.6 us
    all_to_all x1, starting transfers between devices, local(): parts = lax.all_to_all(part, 'z_hi', 0, 0, tiled=True)  20.1 us
    all_to_all x1, waiting for transfers between devices, local(): parts = lax.all_to_all(part, 'z_hi', 0, 0, tiled=True)  15.2 us
    all_to_all x1, blocking collectives, local(): returned = lax.all_to_all(sent, FS, 0, 0, tiled=True)  12.5 us
    ppermute x2, starting transfers between devices, local(): below = lax.ppermute(ring_add(chunks, scalars, ny - s, below), 'y', down)  10 us
    pallas_call x7, Pallas kernels, ring_add(): pl.pallas_call(body, grid_spec=pltpu.PrefetchScalarGridSpec(num_scalar_pr...  5.22 us
    ppermute x1, starting transfers between devices, local(): lax.ppermute(ring_add(chunks, scalars, 5, below, covers=1), 'y', down)  4.99 us
    ppermute x2, starting transfers between devices, local(): above = lax.ppermute(ring_add(chunks, scalars, s, above), 'y', up)  4.67 us
  transfers between devices with their start and end apart: 9, of which 6 were waited for; matrix products, arithmetic and copies ran while one was open for 0% of the time, Pallas kernels for 3%

profile of v3, /device:TPU:1, one launch (start us, length us, event | category | flops | bytes accessed | tf_op | source)
XLA Modules:
  0.0 129.8 jit_solution(1985992037592850833)
XLA Ops:
  0.6 0.0 copy-start
  0.7 0.0 copy-start.1
  0.7 1.6 %copy-done.1 = bf16[1,1,32,16,2048]{4,3,2,1,0:T(8,128)(2,1)S(1)} copy-done((bf16[1,1,32,16,2048]{4,3,2,1,0:T(8,128)(2,1)S(1)}, bf16[1,1,32,16,2048]{4,3,2,1,0:T(8,128)(2,1)}, u32[]{:S(2)}) %copy-start.1) | copy-done | bytes 2097176
  2.2 0.0 copy-start.2
  2.3 4.2 %collective-permute-start = (bf16[2,16,2048]{2,1,0:T(8,128)(2,1)S(1)}, bf16[2,16,2048]{2,1,0:T(8,128)(2,1)S(1)}, u32[]{:S(2)}, u32[]{:S(2)}) collective-permute-start(bf16[2,16,2048]{2,1,0:T(8,128)(2,1)S(1)} %get-tuple-element.7), channel_id=1, source_target_pairs={{0,4},{4,8},{8,12},{12,16},{16,20},{20,24},{24,28},{28,0},{1,5},{5... | collective-permute-start | bytes 393224 | tf_op jit(solution)/shard_map/ppermute | solution.py:236
  6.4 3.8 %collective-permute-start.4 = (bf16[2,16,2048]{2,1,0:T(8,128)(2,1)S(1)}, bf16[2,16,2048]{2,1,0:T(8,128)(2,1)S(1)}, u32[]{:S(2)}, u32[]{:S(2)}) collective-permute-start(bf16[2,16,2048]{2,1,0:T(8,128)(2,1)S(1)} %get-tuple-element.8), channel_id=1, source_target_pairs={{0,28},{4,0},{8,4},{12,8},{16,12},{20,16},{24,20},{28,24},{1,29},{... | collective-permute-start | bytes 393224 | tf_op jit(solution)/shard_map/ppermute | solution.py:237
  10.3 0.0 copy-done
  10.3 0.1 pad_add_fusion.idx
  10.4 1.8 %collective-permute-done.4.refs_0_ = bf16[2,16,2048]{2,1,0:T(8,128)(2,1)S(1)} collective-permute-done((bf16[2,16,2048]{2,1,0:T(8,128)(2,1)S(1)}, bf16[2,16,2048]{2,1,0:T(8,128)(2,1)S(1)}, u32[]{:S(2)}, u32[]{:S(2)}) %collective-permute-start.4) | collective-permute-done | bytes 131104 | tf_op jit(solution)/shard_map/ppermute | solution.py:237
  12.2 0.0 copy-done.2
  12.2 0.6 ring_add.10
  12.8 5.0 %collective-permute-start.5 = (bf16[4,16,2048]{2,1,0:T(8,128)(2,1)S(1)}, bf16[4,16,2048]{2,1,0:T(8,128)(2,1)S(1)}, u32[]{:S(2)}, u32[]{:S(2)}) collective-permute-start(bf16[4,16,2048]{2,1,0:T(8,128)(2,1)S(1)} %ring_add.10), channel_id=1, source_target_pairs={{0,28},{4,0},{8,4},{12,8},{16,12},{20,16},{24,20},{28,24},{1,29},{... | collective-permute-start | bytes 786440 | tf_op jit(solution)/shard_map/ppermute | solution.py:239
  17.8 0.0 collective-permute-done.refs_0_
  17.8 0.6 ring_add.7
  18.5 1.9 %collective-permute-start.1 = (bf16[4,16,2048]{2,1,0:T(8,128)(2,1)S(1)}, bf16[4,16,2048]{2,1,0:T(8,128)(2,1)S(1)}, u32[]{:S(2)}, u32[]{:S(2)}) collective-permute-start(bf16[4,16,2048]{2,1,0:T(8,128)(2,1)S(1)} %ring_add.7), channel_id=1, source_target_pairs={{0,4},{4,8},{8,12},{12,16},{16,20},{20,24},{24,28},{28,0},{1,5},{5... | collective-permute-start | bytes 786440 | tf_op jit(solution)/shard_map/ppermute | solution.py:238
  20.4 0.7 collective-permute-done.5.refs_0_
  21.1 0.7 ring_add.11
  21.8 5.0 %collective-permute-start.6 = (bf16[4,16,2048]{2,1,0:T(8,128)(2,1)S(1)}, bf16[4,16,2048]{2,1,0:T(8,128)(2,1)S(1)}, u32[]{:S(2)}, u32[]{:S(2)}) collective-permute-start(bf16[4,16,2048]{2,1,0:T(8,128)(2,1)S(1)} %ring_add.11), channel_id=1, source_target_pairs={{0,28},{4,0},{8,4},{12,8},{16,12},{20,16},{24,20},{28,24},{1,29},{... | collective-permute-start | bytes 786440 | tf_op jit(solution)/shard_map/ppermute | solution.py:242
  26.8 0.0 collective-permute-done.1.refs_0_
  26.8 0.7 ring_add.8
  27.5 1.9 %collective-permute-start.2 = (bf16[4,16,2048]{2,1,0:T(8,128)(2,1)S(1)}, bf16[4,16,2048]{2,1,0:T(8,128)(2,1)S(1)}, u32[]{:S(2)}, u32[]{:S(2)}) collective-permute-start(bf16[4,16,2048]{2,1,0:T(8,128)(2,1)S(1)} %ring_add.8), channel_id=1, source_target_pairs={{0,4},{4,8},{8,12},{12,16},{16,20},{20,24},{24,28},{28,0},{1,5},{5... | collective-permute-start | bytes 786440 | tf_op jit(solution)/shard_map/ppermute | solution.py:241
  29.4 0.7 collective-permute-done.6.refs_0_
  30.1 0.7 ring_add.12
  30.8 5.0 %collective-permute-start.7 = (bf16[4,16,2048]{2,1,0:T(8,128)(2,1)S(1)}, bf16[4,16,2048]{2,1,0:T(8,128)(2,1)S(1)}, u32[]{:S(2)}, u32[]{:S(2)}) collective-permute-start(bf16[4,16,2048]{2,1,0:T(8,128)(2,1)S(1)} %ring_add.12), channel_id=1, source_target_pairs={{0,28},{4,0},{8,4},{12,8},{16,12},{20,16},{24,20},{28,24},{1,29},{... | collective-permute-start | bytes 786440 | tf_op jit(solution)/shard_map/ppermute | solution.py:242
  35.8 0.0 collective-permute-done.2.refs_0_
  35.8 0.7 ring_add.9
  36.5 0.0 copy-start.4
  36.5 2.8 %collective-permute-start.3 = (bf16[4,16,2048]{2,1,0:T(8,128)(2,1)S(1)}, bf16[4,16,2048]{2,1,0:T(8,128)(2,1)S(1)}, u32[]{:S(2)}, u32[]{:S(2)}) collective-permute-start(bf16[4,16,2048]{2,1,0:T(8,128)(2,1)S(1)} %ring_add.9), channel_id=1, source_target_pairs={{0,4},{4,8},{8,12},{12,16},{16,20},{20,24},{24,28},{28,0},{1,5},{5... | collective-permute-start | bytes 786440 | tf_op jit(solution)/shard_map/ppermute | solution.py:241
  39.3 1.3 collective-permute-done.7.refs_1_
  40.6 4.4 %collective-permute-done.3.refs_0_ = bf16[4,16,2048]{2,1,0:T(8,128)(2,1)S(1)} collective-permute-done((bf16[4,16,2048]{2,1,0:T(8,128)(2,1)S(1)}, bf16[4,16,2048]{2,1,0:T(8,128)(2,1)S(1)}, u32[]{:S(2)}, u32[]{:S(2)}) %collective-permute-start.3) | collective-permute-done | bytes 262176 | tf_op jit(solution)/shard_map/ppermute | solution.py:241
  45.0 1.3 %ring_add.13 = bf16[4,16,2048]{2,1,0:T(8,128)(2,1)} custom-call(s32[41]{0:T(128)S(1)} %pad_add_fusion.idx, bf16[8,4,16,2048]{3,2,1,0:T(8,128)(2,1)S(1)} %bitcast.18, bf16[4,16,2048]{2,1,0:T(8,128)(2,1)S(1)} %collective-permute-done.3.refs_0_, bf16[4,16,2048]{2,1,0:T(8,128)(2,1)S(1)} %collective-permute-done.7.refs_1_), custom_call_target="tpu_custom_call" | custom-call | tf_op jit(solution)/shard_map/ring_add/pallas_call | solution.py:84
  46.3 0.0 copy-start.5
  46.3 20.1 %all-to-all-start = ((bf16[4,16,2048]{2,1,0:T(8,128)(2,1)}), bf16[4,16,2048]{2,1,0:T(8,128)(2,1)S(1)}, u32[]{:S(2)}, u32[]{:S(2)}) async-start(bf16[4,16,2048]{2,1,0:T(8,128)(2,1)} %ring_add.13), calls=%async_computation | async-start | bytes 524288 | tf_op jit(solution)/shard_map/all_to_all | solution.py:245
  67.1 15.2 %all-to-all-done.got = bf16[4,16,2048]{2,1,0:T(8,128)(2,1)S(1)} async-done(((bf16[4,16,2048]{2,1,0:T(8,128)(2,1)}), bf16[4,16,2048]{2,1,0:T(8,128)(2,1)S(1)}, u32[]{:S(2)}, u32[]{:S(2)}) %all-to-all-start) | async-done | bytes 262176 | tf_op jit(solution)/shard_map/all_to_all | solution.py:245
  82.3 0.0 copy-done.4
  82.3 0.0 copy-start.3
  82.3 1.6 %copy-done.3 = bf16[1,4,512,512]{3,2,1,0:T(8,128)(2,1)S(1)} copy-done((bf16[1,4,512,512]{3,2,1,0:T(8,128)(2,1)S(1)}, bf16[1,4,512,512]{3,2,1,0:T(8,128)(2,1)}, u32[]{:S(2)}) %copy-start.3) | copy-done | bytes 2097176
  83.9 1.5 %right_and_adam.1 = (bf16[32,16,512]{2,1,0:T(8,128)(2,1)S(1)}, f32[16,2048]{1,0:T(8,128)}, f32[8,128]{1,0:T(8,128)S(1)}) custom-call(s32[41]{0:T(128)S(1)} %pad_add_fusion.idx, s32[1]{0:T(128)S(6)} %copy.8.step, bf16[4,16,2048]{2,1,0:T(8,128)(2,1)S(1)} %all-to-all-done.got, bf16[4,512,512]{2,1,0:T(8,128)(2,1)S(1)} %bitcast.19, f32[16,2048]{1,0:T(8,128)S(1)} %bitcast.21), custom_call_target="tpu_custom_call" | custom-call | tf_op jit(solution)/shard_map/right_and_adam/pallas_call | solution.py:134
  85.3 29.6 %all_to_all.15 = bf16[32,16,512]{2,1,0:T(8,128)(2,1)S(1)} all-to-all(bf16[32,16,512]{2,1,0:T(8,128)(2,1)S(1)} %get-tuple-element.9), channel_id=1, replica_groups=mesh['z_lo'=4,'x'=4,'core'=2,'y'=8,'z_hi'=4] {'z_lo','x','core'}, dimensions={0} | all-to-all | bytes 1048576 | tf_op jit(solution)/shard_map/all_to_all | solution.py:249
  114.9 0.0 copy-done.5
  114.9 1.0 left_product.1
  115.9 12.5 %all_to_all.16.got = bf16[32,16,128]{2,1,0:T(8,128)(2,1)S(1)} all-to-all(bf16[32,16,128]{2,1,0:T(8,128)(2,1)S(1)} %left_product.1), channel_id=1, replica_groups=mesh['z_lo'=4,'x'=4,'core'=2,'y'=8,'z_hi'=4] {'z_lo','x','core'}, dimensions={0} | all-to-all | bytes 262144 | tf_op jit(solution)/shard_map/all_to_all | solution.py:253
  128.4 1.3 %finish.1 = bf16[16,2048]{1,0:T(8,128)(2,1)} custom-call(s32[41]{0:T(128)S(1)} %pad_add_fusion.idx, bf16[32,16,128]{2,1,0:T(8,128)(2,1)S(1)} %all_to_all.16.got), custom_call_target="tpu_custom_call" | custom-call | tf_op jit(solution)/shard_map/finish/pallas_call | solution.py:209
  (3 shorter events, 0.0 us)
Async XLA Ops:
  0.6 9.7 %copy-start = (s32[32,32]{1,0:T(8,128)S(1)}, s32[32,32]{1,0:T(8,128)}, u32[]{:S(2)}) copy-start(s32[32,32]{1,0:T(8,128)} %param.10) | copy-start | bytes 12292
  0.7 1.6 %copy-start.1 = (bf16[1,1,32,16,2048]{4,3,2,1,0:T(8,128)(2,1)S(1)}, bf16[1,1,32,16,2048]{4,3,2,1,0:T(8,128)(2,1)}, u32[]{:S(2)}) copy-start(bf16[1,1,32,16,2048]{4,3,2,1,0:T(8,128)(2,1)} %param.6) | copy-start | bytes 6291460
  2.2 9.9 %copy-start.2 = (bf16[1,1,32,16,2048]{4,3,2,1,0:T(8,128)(2,1)S(1)}, bf16[1,1,32,16,2048]{4,3,2,1,0:T(8,128)(2,1)}, u32[]{:S(2)}) copy-start(bf16[1,1,32,16,2048]{4,3,2,1,0:T(8,128)(2,1)} %param.6) | copy-start | bytes 6291460
  2.3 15.6 %collective-permute-start = (bf16[2,16,2048]{2,1,0:T(8,128)(2,1)S(1)}, bf16[2,16,2048]{2,1,0:T(8,128)(2,1)S(1)}, u32[]{:S(2)}, u32[]{:S(2)}) collective-permute-start(bf16[2,16,2048]{2,1,0:T(8,128)(2,1)S(1)} %get-tuple-element.7), channel_id=1, source_target_pairs={{0,4},{4,8},{8,12},{12,16},{16,20},{20,24},{24,28},{28,0},{1,5},{5... | collective-permute-start | bytes 393224 | tf_op jit(solution)/shard_map/ppermute | solution.py:236
  6.4 5.7 %collective-permute-start.4 = (bf16[2,16,2048]{2,1,0:T(8,128)(2,1)S(1)}, bf16[2,16,2048]{2,1,0:T(8,128)(2,1)S(1)}, u32[]{:S(2)}, u32[]{:S(2)}) collective-permute-start(bf16[2,16,2048]{2,1,0:T(8,128)(2,1)S(1)} %get-tuple-element.8), channel_id=1, source_target_pairs={{0,28},{4,0},{8,4},{12,8},{16,12},{20,16},{24,20},{28,24},{1,29},{... | collective-permute-start | bytes 393224 | tf_op jit(solution)/shard_map/ppermute | solution.py:237
  12.8 8.3 %collective-permute-start.5 = (bf16[4,16,2048]{2,1,0:T(8,128)(2,1)S(1)}, bf16[4,16,2048]{2,1,0:T(8,128)(2,1)S(1)}, u32[]{:S(2)}, u32[]{:S(2)}) collective-permute-start(bf16[4,16,2048]{2,1,0:T(8,128)(2,1)S(1)} %ring_add.10), channel_id=1, source_target_pairs={{0,28},{4,0},{8,4},{12,8},{16,12},{20,16},{24,20},{28,24},{1,29},{... | collective-permute-start | bytes 786440 | tf_op jit(solution)/shard_map/ppermute | solution.py:239
  18.5 8.3 %collective-permute-start.1 = (bf16[4,16,2048]{2,1,0:T(8,128)(2,1)S(1)}, bf16[4,16,2048]{2,1,0:T(8,128)(2,1)S(1)}, u32[]{:S(2)}, u32[]{:S(2)}) collective-permute-start(bf16[4,16,2048]{2,1,0:T(8,128)(2,1)S(1)} %ring_add.7), channel_id=1, source_target_pairs={{0,4},{4,8},{8,12},{12,16},{16,20},{20,24},{24,28},{28,0},{1,5},{5... | collective-permute-start | bytes 786440 | tf_op jit(solution)/shard_map/ppermute | solution.py:238
  21.8 8.3 %collective-permute-start.6 = (bf16[4,16,2048]{2,1,0:T(8,128)(2,1)S(1)}, bf16[4,16,2048]{2,1,0:T(8,128)(2,1)S(1)}, u32[]{:S(2)}, u32[]{:S(2)}) collective-permute-start(bf16[4,16,2048]{2,1,0:T(8,128)(2,1)S(1)} %ring_add.11), channel_id=1, source_target_pairs={{0,28},{4,0},{8,4},{12,8},{16,12},{20,16},{24,20},{28,24},{1,29},{... | collective-permute-start | bytes 786440 | tf_op jit(solution)/shard_map/ppermute | solution.py:242
  27.5 8.3 %collective-permute-start.2 = (bf16[4,16,2048]{2,1,0:T(8,128)(2,1)S(1)}, bf16[4,16,2048]{2,1,0:T(8,128)(2,1)S(1)}, u32[]{:S(2)}, u32[]{:S(2)}) collective-permute-start(bf16[4,16,2048]{2,1,0:T(8,128)(2,1)S(1)} %ring_add.8), channel_id=1, source_target_pairs={{0,4},{4,8},{8,12},{12,16},{16,20},{20,24},{24,28},{28,0},{1,5},{5... | collective-permute-start | bytes 786440 | tf_op jit(solution)/shard_map/ppermute | solution.py:241
  30.8 9.8 %collective-permute-start.7 = (bf16[4,16,2048]{2,1,0:T(8,128)(2,1)S(1)}, bf16[4,16,2048]{2,1,0:T(8,128)(2,1)S(1)}, u32[]{:S(2)}, u32[]{:S(2)}) collective-permute-start(bf16[4,16,2048]{2,1,0:T(8,128)(2,1)S(1)} %ring_add.12), channel_id=1, source_target_pairs={{0,28},{4,0},{8,4},{12,8},{16,12},{20,16},{24,20},{28,24},{1,29},{... | collective-permute-start | bytes 786440 | tf_op jit(solution)/shard_map/ppermute | solution.py:242
  36.5 45.8 %copy-start.4 = (f32[1,1,16,2048]{3,2,1,0:T(8,128)S(1)}, f32[1,1,16,2048]{3,2,1,0:T(8,128)}, u32[]{:S(2)}) copy-start(f32[1,1,16,2048]{3,2,1,0:T(8,128)} %param.7) | copy-start | bytes 393220
  36.5 8.5 %collective-permute-start.3 = (bf16[4,16,2048]{2,1,0:T(8,128)(2,1)S(1)}, bf16[4,16,2048]{2,1,0:T(8,128)(2,1)S(1)}, u32[]{:S(2)}, u32[]{:S(2)}) collective-permute-start(bf16[4,16,2048]{2,1,0:T(8,128)(2,1)S(1)} %ring_add.9), channel_id=1, source_target_pairs={{0,4},{4,8},{8,12},{12,16},{16,20},{20,24},{24,28},{28,0},{1,5},{5... | collective-permute-start | bytes 786440 | tf_op jit(solution)/shard_map/ppermute | solution.py:241
  46.3 68.7 %copy-start.5 = (bf16[1,1,64,512]{3,2,1,0:T(8,128)(2,1)S(1)}, bf16[1,1,64,512]{3,2,1,0:T(8,128)(2,1)}, u32[]{:S(2)}) copy-start(bf16[1,1,64,512]{3,2,1,0:T(8,128)(2,1)} %param.8) | copy-start | bytes 196612
  46.3 36.0 %all-to-all-start = ((bf16[4,16,2048]{2,1,0:T(8,128)(2,1)}), bf16[4,16,2048]{2,1,0:T(8,128)(2,1)S(1)}, u32[]{:S(2)}, u32[]{:S(2)}) async-start(bf16[4,16,2048]{2,1,0:T(8,128)(2,1)} %ring_add.13), calls=%async_computation | async-start | bytes 524288 | tf_op jit(solution)/shard_map/all_to_all | solution.py:245
  82.3 1.6 %copy-start.3 = (bf16[1,4,512,512]{3,2,1,0:T(8,128)(2,1)S(1)}, bf16[1,4,512,512]{3,2,1,0:T(8,128)(2,1)}, u32[]{:S(2)}) copy-start(bf16[1,4,512,512]{3,2,1,0:T(8,128)(2,1)} %param.9) | copy-start | bytes 6291460

commit v4 on v3

--- a/solution.py
+++ b/solution.py
@@ -31,79 +31,67 @@
     )
 
 
-def far_halves(chunks, index):
+def take(chunks, one, two):
     _, parts, rows, width = chunks.shape
-    half = parts // 2
-
-    def body(idx, own, low, high):
-        low[...] = own[0, :half]
-        high[...] = own[0, half:]
-
-    shape = jax.ShapeDtypeStruct((half, rows, width), bf16)
-    block = pl.BlockSpec((half, rows, width), lambda i, idx: (0, 0, 0))
+
+    def body(i, j, a, b, first, second):
+        first[...] = a[0]
+        second[...] = b[0]
+
+    shape = jax.ShapeDtypeStruct((parts, rows, width), bf16)
+    block = pl.BlockSpec((parts, rows, width), lambda g, i, j: (0, 0, 0))
     return pl.pallas_call(
         body,
         grid_spec=pltpu.PrefetchScalarGridSpec(
-            num_scalar_prefetch=1,
+            num_scalar_prefetch=2,
             grid=(1,),
-            in_specs=[pl.BlockSpec((1, parts, rows, width), lambda i, idx: (idx[0], 0, 0, 0))],
+            in_specs=[
+                pl.BlockSpec((1, parts, rows, width), lambda g, i, j: (i[0], 0, 0, 0)),
+                pl.BlockSpec((1, parts, rows, width), lambda g, i, j: (j[0], 0, 0, 0)),
+            ],
             out_specs=[block, block],
         ),
         out_shape=[shape, shape],
         compiler_params=pltpu.CompilerParams(vmem_limit_bytes=VMEM_LIMIT),
-        name="far_halves",
-    )(index, chunks)
-
-
-def ring_add(chunks, scalars, place, *received, covers=None):
+        name="take",
+    )(one, two, chunks, chunks)
+
+
+def ring_add(chunks, index, *received, after=None):
     _, parts, rows, width = chunks.shape
     half = parts // 2
+    count = len(received)
 
     def body(idx, own, *refs):
-        if covers is None:
-            total = own[0].astype(f32)
-            for got in refs[:-1]:
-                total = total + got[...].astype(f32)
-            refs[-1][...] = total.astype(bf16)
-        else:
-            i = pl.program_id(0)
-
-            @pl.when(i == covers)
-            def _():
-                refs[1][...] = (own[0].astype(f32) + refs[0][...].astype(f32)).astype(bf16)
-
-            @pl.when(i != covers)
-            def _():
-                refs[1][...] = own[0]
+        total = own[0].astype(f32)
+        for got in refs[:count]:
+            total = total + got[...].astype(f32)
+        refs[-1][...] = total.astype(bf16)
 
     block = pl.BlockSpec((half, rows, width), lambda i, idx: (i, 0, 0))
-    if covers is not None:
-        got_block = pl.BlockSpec((half, rows, width), lambda i, idx: (0, 0, 0))
-    else:
-        got_block = block
+    extra = [] if after is None else [after]
     return pl.pallas_call(
         body,
         grid_spec=pltpu.PrefetchScalarGridSpec(
             num_scalar_prefetch=1,
             grid=(2,),
-            in_specs=[
-                pl.BlockSpec((1, half, rows, width), lambda i, idx: (idx[place], i, 0, 0))
-            ]
-            + [got_block] * len(received),
+            in_specs=[pl.BlockSpec((1, half, rows, width), lambda i, idx: (idx[0], i, 0, 0))]
+            + [block] * count
+            + [SMEM] * len(extra),
             out_specs=block,
         ),
         out_shape=jax.ShapeDtypeStruct((parts, rows, width), bf16),
         compiler_params=pltpu.CompilerParams(vmem_limit_bytes=VMEM_LIMIT),
         name="ring_add",
-    )(scalars, chunks, *received)
-
-
-def right_and_adam(parts, right, moment, scalars, step_count, owners_at, members):
+    )(index, chunks, *received, *extra)
+
+
+def right_and_adam(parts, right, moment, scalars, step_at, owners_at, members):
     count, rows, width = parts.shape
     blocks, size, _ = right.shape
     team = members // blocks
 
-    def body(idx, step, got, root, old, pieces, new, squares):
+    def body(idx, got, root, old, pieces, new, squares):
         total = got[0].astype(f32)
         for i in range(1, count):
             total = total + got[i].astype(f32)
@@ -114,7 +102,7 @@
             ).astype(bf16)
             for i in range(team):
                 pieces[idx[owners_at + k * team + i]] = prod
-        steps = jnp.full((8, 128), step[0], jnp.int32).astype(f32)
+        steps = jnp.full((8, 128), idx[step_at], jnp.int32).astype(f32)
         correction = (1.0 - jnp.exp(steps * log_beta))[:1, :1]
         m = beta_two * old[...] + (1.0 - beta_two) * total * total
         new[...] = m
@@ -131,8 +119,8 @@
         jax.ShapeDtypeStruct((rows, width), f32),
         jax.ShapeDtypeStruct((8, 128), f32),
     )
-    return call(body, "right_and_adam", [SMEM, SMEM, VMEM, VMEM, VMEM], shapes)(
-        scalars, step_count, parts, right, moment
+    return call(body, "right_and_adam", [SMEM, VMEM, VMEM, VMEM], shapes)(
+        scalars, parts, right, moment
     )
 
 
@@ -222,29 +210,34 @@
     rows, width = gradients.shape[3], gradients.shape[4]
     size = right_root.shape[3]
     blocks = right_root.shape[1]
-    up = [(j, (j + 1) % ny) for j in range(ny)]
-    down = [(j, (j - 1) % ny) for j in range(ny)]
-
-    places = jnp.bitwise_and(yi + jnp.arange(ny), ny - 1)
+    sign = 1 - 2 * lax.axis_index("core")
+
+    def along(value, turn):
+        steps = (turn, -turn)
+        pairs = [(c * ny + j, c * ny + (j + steps[c]) % ny) for c in range(2) for j in range(ny)]
+        return lax.ppermute(value, ("core", "y"), pairs)
+
+    def at(offset):
+        return jnp.bitwise_and(yi + sign * offset + ny, ny - 1).astype(jnp.int32).reshape(1)
+
     owners = lax.dynamic_index_in_dim(owner_table, lax.axis_index(REP), 0, keepdims=False)
-    scalars = jnp.concatenate([places, lax.axis_index(FS).reshape(1), owners]).astype(jnp.int32)
-    member_at, owners_at = ny, ny + 1
+    scalars = jnp.concatenate([lax.axis_index(FS).reshape(1), step_count, owners]).astype(jnp.int32)
+    member_at, step_at, owners_at = 0, 1, 2
 
     chunks = gradients.reshape(ny, nz, rows, width)
-    far = jnp.bitwise_and(yi + 4, ny - 1).astype(jnp.int32).reshape(1)
-    above, below = far_halves(chunks, far)
-    above = lax.ppermute(above, "y", up)
-    below = lax.ppermute(below, "y", down)
-    above = lax.ppermute(ring_add(chunks, scalars, 3, above, covers=0), "y", up)
-    below = lax.ppermute(ring_add(chunks, scalars, 5, below, covers=1), "y", down)
-    for s in (2, 1):
-        above = lax.ppermute(ring_add(chunks, scalars, s, above), "y", up)
-        below = lax.ppermute(ring_add(chunks, scalars, ny - s, below), "y", down)
-    part = ring_add(chunks, scalars, 0, above, below)
+    long_way, short_way = take(chunks, at(4), at(-3))
+    long_way = along(long_way, 1)
+    short_way = along(short_way, -1)
+    long_way = along(ring_add(chunks, at(3), long_way, after=scalars), 1)
+    short_way = along(ring_add(chunks, at(-2), short_way), -1)
+    long_way = along(ring_add(chunks, at(2), long_way), 1)
+    short_way = along(ring_add(chunks, at(-1), short_way), -1)
+    long_way = along(ring_add(chunks, at(1), long_way), 1)
+    part = ring_add(chunks, at(0), long_way, short_way)
 
     parts = lax.all_to_all(part, "z_hi", 0, 0, tiled=True)
     pieces, new_moment, squares = right_and_adam(
-        parts, right_root[0], second_moment[0, 0], scalars, step_count, owners_at, members
+        parts, right_root[0], second_moment[0, 0], scalars, step_at, owners_at, members
     )
     columns = lax.all_to_all(pieces, FS, 0, 0, tiled=True).reshape(members * rows, size)
     sent = left_product(

time: 130 us -> 123 us (0.946)
  the two profiles are of different devices: /device:TPU:1 before, /device:TPU:33 now
where the time goes in v4:
time: 123 us; the launch traced here: 122 us
  blocking collectives  80.3 us (65%)
  starting transfers between devices  21.7 us (18%)
  waiting for transfers between devices  12.1 us (10%)
  Pallas kernels  4.96 us (4%)
  local copies, waits for them, and re-layouts  1.63 us (1%)
  between operations  1.51 us (1%)
    all_to_all x1, blocking collectives, local(): parts = lax.all_to_all(part, 'z_hi', 0, 0, tiled=True)  34.2 us
    all_to_all x1, blocking collectives, local(): lax.all_to_all(pieces, FS, 0, 0, tiled=True).reshape(members * rows, size)  33.6 us
    ppermute x7, starting transfers between devices, along(): return lax.ppermute(value, ('core', 'y'), pairs)  21.7 us
    all_to_all x1, blocking collectives, local(): returned = lax.all_to_all(sent, FS, 0, 0, tiled=True)  12.5 us
    ppermute x7, waiting for transfers between devices, along(): return lax.ppermute(value, ('core', 'y'), pairs)  12.1 us
  transfers between devices with their start and end apart: 7, of which 7 were waited for; matrix products, arithmetic and copies ran while one was open for 0% of the time, Pallas kernels for 1%

profile of v4, /device:TPU:33, one launch (start us, length us, event | category | flops | bytes accessed | tf_op | source)
XLA Modules:
  0.0 122.3 jit_solution(15208780625758375046)
XLA Ops:
  0.6 0.0 copy-start
  0.7 0.0 copy-start.1
  0.7 1.6 %copy-done.1 = bf16[1,1,32,16,2048]{4,3,2,1,0:T(8,128)(2,1)S(1)} copy-done((bf16[1,1,32,16,2048]{4,3,2,1,0:T(8,128)(2,1)S(1)}, bf16[1,1,32,16,2048]{4,3,2,1,0:T(8,128)(2,1)}, u32[]{:S(2)}) %copy-start.1) | copy-done | bytes 2097176
  2.3 0.0 copy-start.2
  2.3 2.2 %collective-permute-start = (bf16[4,16,2048]{2,1,0:T(8,128)(2,1)S(1)}, bf16[4,16,2048]{2,1,0:T(8,128)(2,1)S(1)}, u32[]{:S(2)}, u32[]{:S(2)}) collective-permute-start(bf16[4,16,2048]{2,1,0:T(8,128)(2,1)S(1)} %get-tuple-element.7), channel_id=1, source_target_pairs={{0,4},{4,8},{8,12},{12,16},{16,20},{20,24},{24,28},{28,0},{32,60},... | collective-permute-start | bytes 786440 | tf_op jit(solution)/shard_map/ppermute | solution.py:218
  4.5 3.2 %collective-permute-start.4 = (bf16[4,16,2048]{2,1,0:T(8,128)(2,1)S(1)}, bf16[4,16,2048]{2,1,0:T(8,128)(2,1)S(1)}, u32[]{:S(2)}, u32[]{:S(2)}) collective-permute-start(bf16[4,16,2048]{2,1,0:T(8,128)(2,1)S(1)} %get-tuple-element.8), channel_id=1, source_target_pairs={{0,28},{4,0},{8,4},{12,8},{16,12},{20,16},{24,20},{28,24},{32,36},... | collective-permute-start | bytes 786440 | tf_op jit(solution)/shard_map/ppermute | solution.py:218
  8.4 0.0 copy-done
  8.4 0.1 pad_add_fusion.refs_1_.idx
  8.5 1.3 %collective-permute-done.refs_0_ = bf16[4,16,2048]{2,1,0:T(8,128)(2,1)S(1)} collective-permute-done((bf16[4,16,2048]{2,1,0:T(8,128)(2,1)S(1)}, bf16[4,16,2048]{2,1,0:T(8,128)(2,1)S(1)}, u32[]{:S(2)}, u32[]{:S(2)}) %collective-permute-start) | collective-permute-done | bytes 262176 | tf_op jit(solution)/shard_map/ppermute | solution.py:218
  9.8 0.0 copy-done.2
  9.8 0.6 ring_add.6
  10.5 3.0 %collective-permute-start.1 = (bf16[4,16,2048]{2,1,0:T(8,128)(2,1)S(1)}, bf16[4,16,2048]{2,1,0:T(8,128)(2,1)S(1)}, u32[]{:S(2)}, u32[]{:S(2)}) collective-permute-start(bf16[4,16,2048]{2,1,0:T(8,128)(2,1)S(1)} %ring_add.6), channel_id=1, source_target_pairs={{0,4},{4,8},{8,12},{12,16},{16,20},{20,24},{24,28},{28,0},{32,60},... | collective-permute-start | bytes 786440 | tf_op jit(solution)/shard_map/ppermute | solution.py:218
  13.5 1.2 collective-permute-done.4.refs_0_
  14.7 0.1 ring_add.9
  14.8 1.9 %collective-permute-start.5 = (bf16[4,16,2048]{2,1,0:T(8,128)(2,1)S(1)}, bf16[4,16,2048]{2,1,0:T(8,128)(2,1)S(1)}, u32[]{:S(2)}, u32[]{:S(2)}) collective-permute-start(bf16[4,16,2048]{2,1,0:T(8,128)(2,1)S(1)} %ring_add.9), channel_id=1, source_target_pairs={{0,28},{4,0},{8,4},{12,8},{16,12},{20,16},{24,20},{28,24},{32,36},... | collective-permute-start | bytes 786440 | tf_op jit(solution)/shard_map/ppermute | solution.py:218
  16.7 0.9 collective-permute-done.1.refs_0_
  17.6 0.1 ring_add.7
  17.7 4.2 %collective-permute-start.2 = (bf16[4,16,2048]{2,1,0:T(8,128)(2,1)S(1)}, bf16[4,16,2048]{2,1,0:T(8,128)(2,1)S(1)}, u32[]{:S(2)}, u32[]{:S(2)}) collective-permute-start(bf16[4,16,2048]{2,1,0:T(8,128)(2,1)S(1)} %ring_add.7), channel_id=1, source_target_pairs={{0,4},{4,8},{8,12},{12,16},{16,20},{20,24},{24,28},{28,0},{32,60},... | collective-permute-start | bytes 786440 | tf_op jit(solution)/shard_map/ppermute | solution.py:218
  22.0 3.5 %collective-permute-done.5.refs_0_ = bf16[4,16,2048]{2,1,0:T(8,128)(2,1)S(1)} collective-permute-done((bf16[4,16,2048]{2,1,0:T(8,128)(2,1)S(1)}, bf16[4,16,2048]{2,1,0:T(8,128)(2,1)S(1)}, u32[]{:S(2)}, u32[]{:S(2)}) %collective-permute-start.5) | collective-permute-done | bytes 262176 | tf_op jit(solution)/shard_map/ppermute | solution.py:218
  25.5 0.1 ring_add.10
  25.6 1.9 %collective-permute-start.6 = (bf16[4,16,2048]{2,1,0:T(8,128)(2,1)S(1)}, bf16[4,16,2048]{2,1,0:T(8,128)(2,1)S(1)}, u32[]{:S(2)}, u32[]{:S(2)}) collective-permute-start(bf16[4,16,2048]{2,1,0:T(8,128)(2,1)S(1)} %ring_add.10), channel_id=1, source_target_pairs={{0,28},{4,0},{8,4},{12,8},{16,12},{20,16},{24,20},{28,24},{32,36},... | collective-permute-start | bytes 786440 | tf_op jit(solution)/shard_map/ppermute | solution.py:218
  27.5 0.3 collective-permute-done.2.refs_0_
  27.8 0.1 ring_add.8
  27.9 0.0 copy-start.4
  27.9 5.3 %collective-permute-start.3 = (bf16[4,16,2048]{2,1,0:T(8,128)(2,1)S(1)}, bf16[4,16,2048]{2,1,0:T(8,128)(2,1)S(1)}, u32[]{:S(2)}, u32[]{:S(2)}) collective-permute-start(bf16[4,16,2048]{2,1,0:T(8,128)(2,1)S(1)} %ring_add.8), channel_id=1, source_target_pairs={{0,4},{4,8},{8,12},{12,16},{16,20},{20,24},{24,28},{28,0},{32,60},... | collective-permute-start | bytes 786440 | tf_op jit(solution)/shard_map/ppermute | solution.py:218
  33.1 0.0 copy-start.3
  33.2 2.2 %collective-permute-done.6.refs_1_ = bf16[4,16,2048]{2,1,0:T(8,128)(2,1)S(1)} collective-permute-done((bf16[4,16,2048]{2,1,0:T(8,128)(2,1)S(1)}, bf16[4,16,2048]{2,1,0:T(8,128)(2,1)S(1)}, u32[]{:S(2)}, u32[]{:S(2)}) %collective-permute-start.6) | collective-permute-done | bytes 262176 | tf_op jit(solution)/shard_map/ppermute | solution.py:218
  35.4 2.7 %collective-permute-done.3.refs_0_ = bf16[4,16,2048]{2,1,0:T(8,128)(2,1)S(1)} collective-permute-done((bf16[4,16,2048]{2,1,0:T(8,128)(2,1)S(1)}, bf16[4,16,2048]{2,1,0:T(8,128)(2,1)S(1)}, u32[]{:S(2)}, u32[]{:S(2)}) %collective-permute-start.3) | collective-permute-done | bytes 262176 | tf_op jit(solution)/shard_map/ppermute | solution.py:218
  38.0 0.1 ring_add.11
  38.2 0.0 copy-start.5
  38.2 34.2 %all_to_all.15.got = bf16[4,16,2048]{2,1,0:T(8,128)(2,1)S(1)} all-to-all(bf16[4,16,2048]{2,1,0:T(8,128)(2,1)S(1)} %ring_add.11), channel_id=1, replica_groups=mesh['z_lo'=4,'x'=4,'core'=2,'y'=8,'z_hi'=4] {'z_hi'}, dimensions={0} | all-to-all | bytes 524288 | tf_op jit(solution)/shard_map/all_to_all | solution.py:238
  72.4 0.0 copy-done.4
  72.4 0.0 copy-done.3
  72.4 1.5 %right_and_adam.1 = (bf16[32,16,512]{2,1,0:T(8,128)(2,1)S(1)}, f32[16,2048]{1,0:T(8,128)}, f32[8,128]{1,0:T(8,128)S(1)}) custom-call(s32[34]{0:T(128)S(1)} %pad_add_fusion.refs_1_.idx, bf16[4,16,2048]{2,1,0:T(8,128)(2,1)S(1)} %all_to_all.15.got, bf16[4,512,512]{2,1,0:T(8,128)(2,1)S(1)} %bitcast.26, f32[16,2048]{1,0:T(8,128)S(1)} %bitcast.28), custom_call_target="tpu_custom_call" | custom-call | tf_op jit(solution)/shard_map/right_and_adam/pallas_call | solution.py:122
  73.9 33.6 %all_to_all.16 = bf16[32,16,512]{2,1,0:T(8,128)(2,1)S(1)} all-to-all(bf16[32,16,512]{2,1,0:T(8,128)(2,1)S(1)} %get-tuple-element.9), channel_id=1, replica_groups=mesh['z_lo'=4,'x'=4,'core'=2,'y'=8,'z_hi'=4] {'z_lo','x','core'}, dimensions={0} | all-to-all | bytes 1048576 | tf_op jit(solution)/shard_map/all_to_all | solution.py:242
  107.5 0.0 copy-done.5
  107.5 1.0 left_product.1
  108.5 12.5 %all_to_all.17.got = bf16[32,16,128]{2,1,0:T(8,128)(2,1)S(1)} all-to-all(bf16[32,16,128]{2,1,0:T(8,128)(2,1)S(1)} %left_product.1), channel_id=1, replica_groups=mesh['z_lo'=4,'x'=4,'core'=2,'y'=8,'z_hi'=4] {'z_lo','x','core'}, dimensions={0} | all-to-all | bytes 262144 | tf_op jit(solution)/shard_map/all_to_all | solution.py:246
  121.0 1.3 %finish.1 = bf16[16,2048]{1,0:T(8,128)(2,1)} custom-call(s32[34]{0:T(128)S(1)} %pad_add_fusion.refs_1_.idx, bf16[32,16,128]{2,1,0:T(8,128)(2,1)S(1)} %all_to_all.17.got), custom_call_target="tpu_custom_call" | custom-call | tf_op jit(solution)/shard_map/finish/pallas_call | solution.py:197
  (2 shorter events, 0.0 us)
Async XLA Ops:
  0.6 7.8 %copy-start = (s32[32,32]{1,0:T(8,128)S(1)}, s32[32,32]{1,0:T(8,128)}, u32[]{:S(2)}) copy-start(s32[32,32]{1,0:T(8,128)} %param.10) | copy-start | bytes 12292
  0.7 1.6 %copy-start.1 = (bf16[1,1,32,16,2048]{4,3,2,1,0:T(8,128)(2,1)S(1)}, bf16[1,1,32,16,2048]{4,3,2,1,0:T(8,128)(2,1)}, u32[]{:S(2)}) copy-start(bf16[1,1,32,16,2048]{4,3,2,1,0:T(8,128)(2,1)} %param.6) | copy-start | bytes 6291460
  2.3 7.6 %copy-start.2 = (bf16[1,1,32,16,2048]{4,3,2,1,0:T(8,128)(2,1)S(1)}, bf16[1,1,32,16,2048]{4,3,2,1,0:T(8,128)(2,1)}, u32[]{:S(2)}) copy-start(bf16[1,1,32,16,2048]{4,3,2,1,0:T(8,128)(2,1)} %param.6) | copy-start | bytes 6291460
  2.3 7.5 %collective-permute-start = (bf16[4,16,2048]{2,1,0:T(8,128)(2,1)S(1)}, bf16[4,16,2048]{2,1,0:T(8,128)(2,1)S(1)}, u32[]{:S(2)}, u32[]{:S(2)}) collective-permute-start(bf16[4,16,2048]{2,1,0:T(8,128)(2,1)S(1)} %get-tuple-element.7), channel_id=1, source_target_pairs={{0,4},{4,8},{8,12},{12,16},{16,20},{20,24},{24,28},{28,0},{32,60},... | collective-permute-start | bytes 786440 | tf_op jit(solution)/shard_map/ppermute | solution.py:218
  4.5 10.2 %collective-permute-start.4 = (bf16[4,16,2048]{2,1,0:T(8,128)(2,1)S(1)}, bf16[4,16,2048]{2,1,0:T(8,128)(2,1)S(1)}, u32[]{:S(2)}, u32[]{:S(2)}) collective-permute-start(bf16[4,16,2048]{2,1,0:T(8,128)(2,1)S(1)} %get-tuple-element.8), channel_id=1, source_target_pairs={{0,28},{4,0},{8,4},{12,8},{16,12},{20,16},{24,20},{28,24},{32,36},... | collective-permute-start | bytes 786440 | tf_op jit(solution)/shard_map/ppermute | solution.py:218
  10.5 7.1 %collective-permute-start.1 = (bf16[4,16,2048]{2,1,0:T(8,128)(2,1)S(1)}, bf16[4,16,2048]{2,1,0:T(8,128)(2,1)S(1)}, u32[]{:S(2)}, u32[]{:S(2)}) collective-permute-start(bf16[4,16,2048]{2,1,0:T(8,128)(2,1)S(1)} %ring_add.6), channel_id=1, source_target_pairs={{0,4},{4,8},{8,12},{12,16},{16,20},{20,24},{24,28},{28,0},{32,60},... | collective-permute-start | bytes 786440 | tf_op jit(solution)/shard_map/ppermute | solution.py:218
  14.8 10.7 %collective-permute-start.5 = (bf16[4,16,2048]{2,1,0:T(8,128)(2,1)S(1)}, bf16[4,16,2048]{2,1,0:T(8,128)(2,1)S(1)}, u32[]{:S(2)}, u32[]{:S(2)}) collective-permute-start(bf16[4,16,2048]{2,1,0:T(8,128)(2,1)S(1)} %ring_add.9), channel_id=1, source_target_pairs={{0,28},{4,0},{8,4},{12,8},{16,12},{20,16},{24,20},{28,24},{32,36},... | collective-permute-start | bytes 786440 | tf_op jit(solution)/shard_map/ppermute | solution.py:218
  17.7 10.1 %collective-permute-start.2 = (bf16[4,16,2048]{2,1,0:T(8,128)(2,1)S(1)}, bf16[4,16,2048]{2,1,0:T(8,128)(2,1)S(1)}, u32[]{:S(2)}, u32[]{:S(2)}) collective-permute-start(bf16[4,16,2048]{2,1,0:T(8,128)(2,1)S(1)} %ring_add.7), channel_id=1, source_target_pairs={{0,4},{4,8},{8,12},{12,16},{16,20},{20,24},{24,28},{28,0},{32,60},... | collective-permute-start | bytes 786440 | tf_op jit(solution)/shard_map/ppermute | solution.py:218
  25.6 9.8 %collective-permute-start.6 = (bf16[4,16,2048]{2,1,0:T(8,128)(2,1)S(1)}, bf16[4,16,2048]{2,1,0:T(8,128)(2,1)S(1)}, u32[]{:S(2)}, u32[]{:S(2)}) collective-permute-start(bf16[4,16,2048]{2,1,0:T(8,128)(2,1)S(1)} %ring_add.10), channel_id=1, source_target_pairs={{0,28},{4,0},{8,4},{12,8},{16,12},{20,16},{24,20},{28,24},{32,36},... | collective-permute-start | bytes 786440 | tf_op jit(solution)/shard_map/ppermute | solution.py:218
  27.9 44.5 %copy-start.4 = (f32[1,1,16,2048]{3,2,1,0:T(8,128)S(1)}, f32[1,1,16,2048]{3,2,1,0:T(8,128)}, u32[]{:S(2)}) copy-start(f32[1,1,16,2048]{3,2,1,0:T(8,128)} %param.7) | copy-start | bytes 393220
  27.9 10.2 %collective-permute-start.3 = (bf16[4,16,2048]{2,1,0:T(8,128)(2,1)S(1)}, bf16[4,16,2048]{2,1,0:T(8,128)(2,1)S(1)}, u32[]{:S(2)}, u32[]{:S(2)}) collective-permute-start(bf16[4,16,2048]{2,1,0:T(8,128)(2,1)S(1)} %ring_add.8), channel_id=1, source_target_pairs={{0,4},{4,8},{8,12},{12,16},{16,20},{20,24},{24,28},{28,0},{32,60},... | collective-permute-start | bytes 786440 | tf_op jit(solution)/shard_map/ppermute | solution.py:218
  33.1 39.3 %copy-start.3 = (bf16[1,4,512,512]{3,2,1,0:T(8,128)(2,1)S(1)}, bf16[1,4,512,512]{3,2,1,0:T(8,128)(2,1)}, u32[]{:S(2)}) copy-start(bf16[1,4,512,512]{3,2,1,0:T(8,128)(2,1)} %param.9) | copy-start | bytes 6291460
  38.2 69.3 %copy-start.5 = (bf16[1,1,64,512]{3,2,1,0:T(8,128)(2,1)S(1)}, bf16[1,1,64,512]{3,2,1,0:T(8,128)(2,1)}, u32[]{:S(2)}) copy-start(bf16[1,1,64,512]{3,2,1,0:T(8,128)(2,1)} %param.8) | copy-start | bytes 196612

commit v5 on v4

--- a/solution.py
+++ b/solution.py
@@ -31,59 +31,68 @@
     )
 
 
-def take(chunks, one, two):
+def take(chunks, *places):
     _, parts, rows, width = chunks.shape
-
-    def body(i, j, a, b, first, second):
-        first[...] = a[0]
-        second[...] = b[0]
+    count = len(places)
+
+    def body(*refs):
+        ins, outs = refs[count : 2 * count], refs[2 * count :]
+        for got, out in zip(ins, outs):
+            out[...] = got[0]
+
+    def block_at(n):
+        return pl.BlockSpec((1, parts, rows, width), lambda g, *idx: (idx[n][0], 0, 0, 0))
 
     shape = jax.ShapeDtypeStruct((parts, rows, width), bf16)
-    block = pl.BlockSpec((parts, rows, width), lambda g, i, j: (0, 0, 0))
     return pl.pallas_call(
         body,
         grid_spec=pltpu.PrefetchScalarGridSpec(
-            num_scalar_prefetch=2,
+            num_scalar_prefetch=count,
             grid=(1,),
-            in_specs=[
-                pl.BlockSpec((1, parts, rows, width), lambda g, i, j: (i[0], 0, 0, 0)),
-                pl.BlockSpec((1, parts, rows, width), lambda g, i, j: (j[0], 0, 0, 0)),
-            ],
-            out_specs=[block, block],
+            in_specs=[block_at(n) for n in range(count)],
+            out_specs=[pl.BlockSpec((parts, rows, width), lambda g, *idx: (0, 0, 0))] * count,
         ),
-        out_shape=[shape, shape],
+        out_shape=[shape] * count,
         compiler_params=pltpu.CompilerParams(vmem_limit_bytes=VMEM_LIMIT),
         name="take",
-    )(one, two, chunks, chunks)
-
-
-def ring_add(chunks, index, *received, after=None):
+    )(*places, *[chunks] * count)
+
+
+def ring_add(chunks, index, *received, also=None, after=None):
     _, parts, rows, width = chunks.shape
     half = parts // 2
     count = len(received)
-
-    def body(idx, own, *refs):
-        total = own[0].astype(f32)
-        for got in refs[:count]:
+    places = [index] + ([] if also is None else [also])
+    wanted = len(places)
+
+    def body(*refs):
+        own = refs[wanted : 2 * wanted]
+        outs = refs[-wanted:]
+        total = own[0][0].astype(f32)
+        for got in refs[2 * wanted : 2 * wanted + count]:
             total = total + got[...].astype(f32)
-        refs[-1][...] = total.astype(bf16)
-
-    block = pl.BlockSpec((half, rows, width), lambda i, idx: (i, 0, 0))
+        outs[0][...] = total.astype(bf16)
+        if wanted == 2:
+            outs[1][...] = own[1][0]
+
+    def block_at(n):
+        return pl.BlockSpec((1, half, rows, width), lambda i, *idx: (idx[n][0], i, 0, 0))
+
+    block = pl.BlockSpec((half, rows, width), lambda i, *idx: (i, 0, 0))
     extra = [] if after is None else [after]
-    return pl.pallas_call(
+    out = pl.pallas_call(
         body,
         grid_spec=pltpu.PrefetchScalarGridSpec(
-            num_scalar_prefetch=1,
+            num_scalar_prefetch=wanted,
             grid=(2,),
-            in_specs=[pl.BlockSpec((1, half, rows, width), lambda i, idx: (idx[0], i, 0, 0))]
-            + [block] * count
-            + [SMEM] * len(extra),
-            out_specs=block,
+            in_specs=[block_at(n) for n in range(wanted)] + [block] * count + [SMEM] * len(extra),
+            out_specs=[block] * wanted,
         ),
-        out_shape=jax.ShapeDtypeStruct((parts, rows, width), bf16),
+        out_shape=[jax.ShapeDtypeStruct((parts, rows, width), bf16)] * wanted,
         compiler_params=pltpu.CompilerParams(vmem_limit_bytes=VMEM_LIMIT),
         name="ring_add",
-    )(index, chunks, *received, *extra)
+    )(*places, *[chunks] * wanted, *received, *extra)
+    return out[0] if also is None else out
 
 
 def right_and_adam(parts, right, moment, scalars, step_at, owners_at, members):
@@ -225,15 +234,16 @@
     member_at, step_at, owners_at = 0, 1, 2
 
     chunks = gradients.reshape(ny, nz, rows, width)
-    long_way, short_way = take(chunks, at(4), at(-3))
-    long_way = along(long_way, 1)
-    short_way = along(short_way, -1)
-    long_way = along(ring_add(chunks, at(3), long_way, after=scalars), 1)
-    short_way = along(ring_add(chunks, at(-2), short_way), -1)
-    long_way = along(ring_add(chunks, at(2), long_way), 1)
-    short_way = along(ring_add(chunks, at(-1), short_way), -1)
-    long_way = along(ring_add(chunks, at(1), long_way), 1)
-    part = ring_add(chunks, at(0), long_way, short_way)
+    four = along(lax.dynamic_index_in_dim(chunks, at(4)[0], 0, keepdims=False), 1)
+    minus_two, two = take(chunks, at(-2), at(2))
+    minus_two = along(minus_two, -1)
+    two = along(two, 1)
+    three = along(ring_add(chunks, at(3), four), 2)
+    minus_one, minus_three = ring_add(chunks, at(-1), minus_two, also=at(-3), after=scalars)
+    minus_one = along(minus_one, -1)
+    minus_three = along(minus_three, -3)
+    one = along(ring_add(chunks, at(1), two, three), 1)
+    part = ring_add(chunks, at(0), minus_one, minus_three, one)
 
     parts = lax.all_to_all(part, "z_hi", 0, 0, tiled=True)
     pieces, new_moment, squares = right_and_adam(

time: 123 us -> 125 us (1.016)
  the two profiles are of different devices: /device:TPU:33 before, /device:TPU:1 now
where the time goes in v5:
time: 125 us; the launch traced here: 123 us
  blocking collectives  74.1 us (59%)
  starting transfers between devices  25.4 us (20%)
  waiting for transfers between devices  13.4 us (11%)
  Pallas kernels  6.36 us (5%)
  local copies, waits for them, and re-layouts  2.6 us (2%)
  between operations  1.52 us (1%)
    all_to_all x1, blocking collectives, local(): parts = lax.all_to_all(part, 'z_hi', 0, 0, tiled=True)  32.6 us
    all_to_all x1, blocking collectives, local(): lax.all_to_all(pieces, FS, 0, 0, tiled=True).reshape(members * rows, size)  29 us
    ppermute x7, starting transfers between devices, along(): return lax.ppermute(value, ('core', 'y'), pairs)  25.4 us
    ppermute x7, waiting for transfers between devices, along(): return lax.ppermute(value, ('core', 'y'), pairs)  13.4 us
    all_to_all x1, blocking collectives, local(): returned = lax.all_to_all(sent, FS, 0, 0, tiled=True)  12.5 us
  transfers between devices with their start and end apart: 7, of which 2 were waited for; matrix products, arithmetic and copies ran while one was open for 0% of the time, Pallas kernels for 2%

profile of v5, /device:TPU:1, one launch (start us, length us, event | category | flops | bytes accessed | tf_op | source)
XLA Modules:
  0.0 123.4 jit_solution(2149162072661427094)
XLA Ops:
  0.6 0.0 copy-start
  0.7 1.0 dynamic-slice_bitcast_fusion
  1.6 5.9 %collective-permute-start.4 = (bf16[4,16,2048]{2,1,0:T(8,128)(2,1)S(1)}, bf16[4,16,2048]{2,1,0:T(8,128)(2,1)S(1)}, u32[]{:S(2)}, u32[]{:S(2)}) collective-permute-start(bf16[4,16,2048]{2,1,0:T(8,128)(2,1)S(1)} %dynamic-slice_bitcast_fusion), channel_id=1, source_target_pairs={{0,4},{4,8},{8,12},{12,16},{16,20},{20,24},{24,28},{28,0},{32,60},... | collective-permute-start | bytes 786440 | tf_op jit(solution)/shard_map/ppermute | solution.py:227
  7.6 0.0 copy-start.1
  7.6 1.6 %copy-done.1 = bf16[1,1,32,16,2048]{4,3,2,1,0:T(8,128)(2,1)S(1)} copy-done((bf16[1,1,32,16,2048]{4,3,2,1,0:T(8,128)(2,1)S(1)}, bf16[1,1,32,16,2048]{4,3,2,1,0:T(8,128)(2,1)}, u32[]{:S(2)}) %copy-start.1) | copy-done | bytes 2097176
  9.2 0.0 copy-start.2
  9.2 0.7 take.1
  9.9 3.0 %collective-permute-start.3 = (bf16[4,16,2048]{2,1,0:T(8,128)(2,1)}, bf16[4,16,2048]{2,1,0:T(8,128)(2,1)S(1)}, u32[]{:S(2)}, u32[]{:S(2)}) collective-permute-start(bf16[4,16,2048]{2,1,0:T(8,128)(2,1)} %get-tuple-element.12), channel_id=1, source_target_pairs={{0,4},{4,8},{8,12},{12,16},{16,20},{20,24},{24,28},{28,0},{32,60},... | collective-permute-start | bytes 786440 | tf_op jit(solution)/shard_map/ppermute | solution.py:227
  12.9 2.3 %collective-permute-start = (bf16[4,16,2048]{2,1,0:T(8,128)(2,1)S(1)}, bf16[4,16,2048]{2,1,0:T(8,128)(2,1)S(1)}, u32[]{:S(2)}, u32[]{:S(2)}) collective-permute-start(bf16[4,16,2048]{2,1,0:T(8,128)(2,1)S(1)} %get-tuple-element.9), channel_id=1, source_target_pairs={{0,28},{4,0},{8,4},{12,8},{16,12},{20,16},{24,20},{28,24},{32,36},... | collective-permute-start | bytes 786440 | tf_op jit(solution)/shard_map/ppermute | solution.py:227
  15.2 0.0 collective-permute-done.4.refs_2_
  15.2 0.0 copy-done.2
  15.2 0.1 ring_add.5
  15.3 3.8 %collective-permute-start.5 = (bf16[4,16,2048]{2,1,0:T(8,128)(2,1)S(1)}, bf16[4,16,2048]{2,1,0:T(8,128)(2,1)S(1)}, u32[]{:S(2)}, u32[]{:S(2)}) collective-permute-start(bf16[4,16,2048]{2,1,0:T(8,128)(2,1)S(1)} %ring_add.5), channel_id=1, source_target_pairs={{0,8},{4,12},{8,16},{12,20},{16,24},{20,28},{24,0},{28,4},{32,56},... | collective-permute-start | bytes 786440 | tf_op jit(solution)/shard_map/ppermute | solution.py:227
  19.8 0.0 copy-done
  19.8 0.1 pad_add_fusion.refs_5_.idx
  19.9 1.3 %collective-permute-done.refs_4_ = bf16[4,16,2048]{2,1,0:T(8,128)(2,1)S(1)} collective-permute-done((bf16[4,16,2048]{2,1,0:T(8,128)(2,1)S(1)}, bf16[4,16,2048]{2,1,0:T(8,128)(2,1)S(1)}, u32[]{:S(2)}, u32[]{:S(2)}) %collective-permute-start) | collective-permute-done | bytes 262176 | tf_op jit(solution)/shard_map/ppermute | solution.py:227
  21.2 1.4 %ring_add.4 = (bf16[4,16,2048]{2,1,0:T(8,128)(2,1)}, bf16[4,16,2048]{2,1,0:T(8,128)(2,1)}) custom-call(s32[1]{0:T(128)} %bitcast.5.refs_0_, s32[1]{0:T(128)} %bitcast.6.refs_1_, bf16[8,4,16,2048]{3,2,1,0:T(8,128)(2,1)S(1)} %bitcast.23, bf16[8,4,16,2048]{3,2,1,0:T(8,128)(2,1)S(1)} %bitcast.24, bf16[4,16,2048]{2,1,0:T(8,128)(2,1)S(1)} %collective-permute-done.refs_4_, ...), custom_call_target="tpu_custom_call" | custom-call | tf_op jit(solution)/shard_map/ring_add/pallas_call | solution.py:83
  22.6 2.2 %collective-permute-start.1 = (bf16[4,16,2048]{2,1,0:T(8,128)(2,1)}, bf16[4,16,2048]{2,1,0:T(8,128)(2,1)S(1)}, u32[]{:S(2)}, u32[]{:S(2)}) collective-permute-start(bf16[4,16,2048]{2,1,0:T(8,128)(2,1)} %get-tuple-element.10), channel_id=1, source_target_pairs={{0,28},{4,0},{8,4},{12,8},{16,12},{20,16},{24,20},{28,24},{32,36},... | collective-permute-start | bytes 786440 | tf_op jit(solution)/shard_map/ppermute | solution.py:227
  24.8 6.2 %collective-permute-start.2 = (bf16[4,16,2048]{2,1,0:T(8,128)(2,1)}, bf16[4,16,2048]{2,1,0:T(8,128)(2,1)S(1)}, u32[]{:S(2)}, u32[]{:S(2)}) collective-permute-start(bf16[4,16,2048]{2,1,0:T(8,128)(2,1)} %get-tuple-element.11), channel_id=1, source_target_pairs={{0,20},{4,24},{8,28},{12,0},{16,4},{20,8},{24,12},{28,16},{32,44},... | collective-permute-start | bytes 786440 | tf_op jit(solution)/shard_map/ppermute | solution.py:227
  31.0 0.0 collective-permute-done.3.refs_2_
  31.0 0.0 collective-permute-done.5.refs_3_
  31.0 0.2 ring_add.6
  31.1 0.0 copy-start.4
  31.2 2.1 %collective-permute-start.6 = (bf16[4,16,2048]{2,1,0:T(8,128)(2,1)S(1)}, bf16[4,16,2048]{2,1,0:T(8,128)(2,1)S(1)}, u32[]{:S(2)}, u32[]{:S(2)}) collective-permute-start(bf16[4,16,2048]{2,1,0:T(8,128)(2,1)S(1)} %ring_add.6), channel_id=1, source_target_pairs={{0,4},{4,8},{8,12},{12,16},{16,20},{20,24},{24,28},{28,0},{32,60},... | collective-permute-start | bytes 786440 | tf_op jit(solution)/shard_map/ppermute | solution.py:227
  33.2 0.0 copy-start.3
  33.2 0.0 collective-permute-done.1.refs_2_
  33.2 12.0 %collective-permute-done.2.refs_3_ = bf16[4,16,2048]{2,1,0:T(8,128)(2,1)S(1)} collective-permute-done((bf16[4,16,2048]{2,1,0:T(8,128)(2,1)}, bf16[4,16,2048]{2,1,0:T(8,128)(2,1)S(1)}, u32[]{:S(2)}, u32[]{:S(2)}) %collective-permute-start.2) | collective-permute-done | bytes 262176 | tf_op jit(solution)/shard_map/ppermute | solution.py:227
  45.3 0.0 collective-permute-done.6.refs_4_
  45.3 0.2 ring_add.7
  45.5 0.0 copy-start.5
  45.5 32.6 %all_to_all.15.got = bf16[4,16,2048]{2,1,0:T(8,128)(2,1)S(1)} all-to-all(bf16[4,16,2048]{2,1,0:T(8,128)(2,1)S(1)} %ring_add.7), channel_id=1, replica_groups=mesh['z_lo'=4,'x'=4,'core'=2,'y'=8,'z_hi'=4] {'z_hi'}, dimensions={0} | all-to-all | bytes 524288 | tf_op jit(solution)/shard_map/all_to_all | solution.py:248
  78.1 0.0 copy-done.4
  78.1 0.0 copy-done.3
  78.1 1.5 %right_and_adam.1 = (bf16[32,16,512]{2,1,0:T(8,128)(2,1)S(1)}, f32[16,2048]{1,0:T(8,128)}, f32[8,128]{1,0:T(8,128)S(1)}) custom-call(s32[34]{0:T(128)S(1)} %pad_add_fusion.refs_5_.idx, bf16[4,16,2048]{2,1,0:T(8,128)(2,1)S(1)} %all_to_all.15.got, bf16[4,512,512]{2,1,0:T(8,128)(2,1)S(1)} %bitcast.27, f32[16,2048]{1,0:T(8,128)S(1)} %bitcast.29), custom_call_target="tpu_custom_call" | custom-call | tf_op jit(solution)/shard_map/right_and_adam/pallas_call | solution.py:131
  79.5 29.0 %all_to_all.16 = bf16[32,16,512]{2,1,0:T(8,128)(2,1)S(1)} all-to-all(bf16[32,16,512]{2,1,0:T(8,128)(2,1)S(1)} %get-tuple-element.13), channel_id=1, replica_groups=mesh['z_lo'=4,'x'=4,'core'=2,'y'=8,'z_hi'=4] {'z_lo','x','core'}, dimensions={0} | all-to-all | bytes 1048576 | tf_op jit(solution)/shard_map/all_to_all | solution.py:252
  108.5 0.0 copy-done.5
  108.6 1.0 left_product.1
  109.6 12.5 %all_to_all.17.got = bf16[32,16,128]{2,1,0:T(8,128)(2,1)S(1)} all-to-all(bf16[32,16,128]{2,1,0:T(8,128)(2,1)S(1)} %left_product.1), channel_id=1, replica_groups=mesh['z_lo'=4,'x'=4,'core'=2,'y'=8,'z_hi'=4] {'z_lo','x','core'}, dimensions={0} | all-to-all | bytes 262144 | tf_op jit(solution)/shard_map/all_to_all | solution.py:256
  122.0 1.3 %finish.1 = bf16[16,2048]{1,0:T(8,128)(2,1)} custom-call(s32[34]{0:T(128)S(1)} %pad_add_fusion.refs_5_.idx, bf16[32,16,128]{2,1,0:T(8,128)(2,1)S(1)} %all_to_all.17.got), custom_call_target="tpu_custom_call" | custom-call | tf_op jit(solution)/shard_map/finish/pallas_call | solution.py:206
  (1 shorter events, 0.0 us)
Async XLA Ops:
  0.6 19.2 %copy-start = (s32[32,32]{1,0:T(8,128)S(1)}, s32[32,32]{1,0:T(8,128)}, u32[]{:S(2)}) copy-start(s32[32,32]{1,0:T(8,128)} %param.10) | copy-start | bytes 12292
  1.6 13.6 %collective-permute-start.4 = (bf16[4,16,2048]{2,1,0:T(8,128)(2,1)S(1)}, bf16[4,16,2048]{2,1,0:T(8,128)(2,1)S(1)}, u32[]{:S(2)}, u32[]{:S(2)}) collective-permute-start(bf16[4,16,2048]{2,1,0:T(8,128)(2,1)S(1)} %dynamic-slice_bitcast_fusion), channel_id=1, source_target_pairs={{0,4},{4,8},{8,12},{12,16},{16,20},{20,24},{24,28},{28,0},{32,60},... | collective-permute-start | bytes 786440 | tf_op jit(solution)/shard_map/ppermute | solution.py:227
  7.6 1.6 %copy-start.1 = (bf16[1,1,32,16,2048]{4,3,2,1,0:T(8,128)(2,1)S(1)}, bf16[1,1,32,16,2048]{4,3,2,1,0:T(8,128)(2,1)}, u32[]{:S(2)}) copy-start(bf16[1,1,32,16,2048]{4,3,2,1,0:T(8,128)(2,1)} %param.6) | copy-start | bytes 6291460
  9.2 6.0 %copy-start.2 = (bf16[1,1,32,16,2048]{4,3,2,1,0:T(8,128)(2,1)S(1)}, bf16[1,1,32,16,2048]{4,3,2,1,0:T(8,128)(2,1)}, u32[]{:S(2)}) copy-start(bf16[1,1,32,16,2048]{4,3,2,1,0:T(8,128)(2,1)} %param.6) | copy-start | bytes 6291460
  9.9 21.1 %collective-permute-start.3 = (bf16[4,16,2048]{2,1,0:T(8,128)(2,1)}, bf16[4,16,2048]{2,1,0:T(8,128)(2,1)S(1)}, u32[]{:S(2)}, u32[]{:S(2)}) collective-permute-start(bf16[4,16,2048]{2,1,0:T(8,128)(2,1)} %get-tuple-element.12), channel_id=1, source_target_pairs={{0,4},{4,8},{8,12},{12,16},{16,20},{20,24},{24,28},{28,0},{32,60},... | collective-permute-start | bytes 786440 | tf_op jit(solution)/shard_map/ppermute | solution.py:227
  12.9 8.3 %collective-permute-start = (bf16[4,16,2048]{2,1,0:T(8,128)(2,1)S(1)}, bf16[4,16,2048]{2,1,0:T(8,128)(2,1)S(1)}, u32[]{:S(2)}, u32[]{:S(2)}) collective-permute-start(bf16[4,16,2048]{2,1,0:T(8,128)(2,1)S(1)} %get-tuple-element.9), channel_id=1, source_target_pairs={{0,28},{4,0},{8,4},{12,8},{16,12},{20,16},{24,20},{28,24},{32,36},... | collective-permute-start | bytes 786440 | tf_op jit(solution)/shard_map/ppermute | solution.py:227
  15.3 15.6 %collective-permute-start.5 = (bf16[4,16,2048]{2,1,0:T(8,128)(2,1)S(1)}, bf16[4,16,2048]{2,1,0:T(8,128)(2,1)S(1)}, u32[]{:S(2)}, u32[]{:S(2)}) collective-permute-start(bf16[4,16,2048]{2,1,0:T(8,128)(2,1)S(1)} %ring_add.5), channel_id=1, source_target_pairs={{0,8},{4,12},{8,16},{12,20},{16,24},{20,28},{24,0},{28,4},{32,56},... | collective-permute-start | bytes 786440 | tf_op jit(solution)/shard_map/ppermute | solution.py:227
  22.6 10.6 %collective-permute-start.1 = (bf16[4,16,2048]{2,1,0:T(8,128)(2,1)}, bf16[4,16,2048]{2,1,0:T(8,128)(2,1)S(1)}, u32[]{:S(2)}, u32[]{:S(2)}) collective-permute-start(bf16[4,16,2048]{2,1,0:T(8,128)(2,1)} %get-tuple-element.10), channel_id=1, source_target_pairs={{0,28},{4,0},{8,4},{12,8},{16,12},{20,16},{24,20},{28,24},{32,36},... | collective-permute-start | bytes 786440 | tf_op jit(solution)/shard_map/ppermute | solution.py:227
  24.8 20.5 %collective-permute-start.2 = (bf16[4,16,2048]{2,1,0:T(8,128)(2,1)}, bf16[4,16,2048]{2,1,0:T(8,128)(2,1)S(1)}, u32[]{:S(2)}, u32[]{:S(2)}) collective-permute-start(bf16[4,16,2048]{2,1,0:T(8,128)(2,1)} %get-tuple-element.11), channel_id=1, source_target_pairs={{0,20},{4,24},{8,28},{12,0},{16,4},{20,8},{24,12},{28,16},{32,44},... | collective-permute-start | bytes 786440 | tf_op jit(solution)/shard_map/ppermute | solution.py:227
  31.1 46.9 %copy-start.4 = (f32[1,1,16,2048]{3,2,1,0:T(8,128)S(1)}, f32[1,1,16,2048]{3,2,1,0:T(8,128)}, u32[]{:S(2)}) copy-start(f32[1,1,16,2048]{3,2,1,0:T(8,128)} %param.7) | copy-start | bytes 393220
  31.2 14.1 %collective-permute-start.6 = (bf16[4,16,2048]{2,1,0:T(8,128)(2,1)S(1)}, bf16[4,16,2048]{2,1,0:T(8,128)(2,1)S(1)}, u32[]{:S(2)}, u32[]{:S(2)}) collective-permute-start(bf16[4,16,2048]{2,1,0:T(8,128)(2,1)S(1)} %ring_add.6), channel_id=1, source_target_pairs={{0,4},{4,8},{8,12},{12,16},{16,20},{20,24},{24,28},{28,0},{32,60},... | collective-permute-start | bytes 786440 | tf_op jit(solution)/shard_map/ppermute | solution.py:227
  33.2 44.9 %copy-start.3 = (bf16[1,4,512,512]{3,2,1,0:T(8,128)(2,1)S(1)}, bf16[1,4,512,512]{3,2,1,0:T(8,128)(2,1)}, u32[]{:S(2)}) copy-start(bf16[1,4,512,512]{3,2,1,0:T(8,128)(2,1)} %param.9) | copy-start | bytes 6291460
  45.5 63.1 %copy-start.5 = (bf16[1,1,64,512]{3,2,1,0:T(8,128)(2,1)S(1)}, bf16[1,1,64,512]{3,2,1,0:T(8,128)(2,1)}, u32[]{:S(2)}) copy-start(bf16[1,1,64,512]{3,2,1,0:T(8,128)(2,1)} %param.8) | copy-start | bytes 196612

commit v6 on v5

--- a/solution.py
+++ b/solution.py
@@ -235,15 +235,15 @@
 
     chunks = gradients.reshape(ny, nz, rows, width)
     four = along(lax.dynamic_index_in_dim(chunks, at(4)[0], 0, keepdims=False), 1)
-    minus_two, two = take(chunks, at(-2), at(2))
+    minus_three, two = take(chunks, at(-3), at(2))
+    minus_three = along(minus_three, -2)
+    two = along(two, 1)
+    three, minus_two = ring_add(chunks, at(3), four, also=at(-2))
+    three = along(three, 2)
     minus_two = along(minus_two, -1)
-    two = along(two, 1)
-    three = along(ring_add(chunks, at(3), four), 2)
-    minus_one, minus_three = ring_add(chunks, at(-1), minus_two, also=at(-3), after=scalars)
-    minus_one = along(minus_one, -1)
-    minus_three = along(minus_three, -3)
+    minus_one = along(ring_add(chunks, at(-1), minus_two, minus_three), -1)
     one = along(ring_add(chunks, at(1), two, three), 1)
-    part = ring_add(chunks, at(0), minus_one, minus_three, one)
+    part = ring_add(chunks, at(0), minus_one, one, after=scalars)
 
     parts = lax.all_to_all(part, "z_hi", 0, 0, tiled=True)
     pieces, new_moment, squares = right_and_adam(

time: 125 us -> 123 us (0.984)
  waiting for transfers between devices: 13.4 us -> 11.2 us
    ppermute x7, waiting for transfers between devices: 13.4 us -> 11.2 us  [along(): return lax.ppermute(value, ('core', 'y'), pairs)]
  transfers between devices with their start and end apart: 7 -> 7, of which waited for: 2 -> 3; matrix products, arithmetic and copies ran while one was open for 0% -> 0% of each run, Pallas kernels for 2% -> 2%
where the time goes in v6:
time: 123 us; the launch traced here: 121 us
  blocking collectives  74.3 us (60%)
  starting transfers between devices  24.6 us (20%)
  waiting for transfers between devices  11.2 us (9%)
  Pallas kernels  6.45 us (5%)
  local copies, waits for them, and re-layouts  2.6 us (2%)
  between operations  1.52 us (1%)
    all_to_all x1, blocking collectives, local(): parts = lax.all_to_all(part, 'z_hi', 0, 0, tiled=True)  32.5 us
    all_to_all x1, blocking collectives, local(): lax.all_to_all(pieces, FS, 0, 0, tiled=True).reshape(members * rows, size)  29.3 us
    ppermute x7, starting transfers between devices, along(): return lax.ppermute(value, ('core', 'y'), pairs)  24.6 us
    all_to_all x1, blocking collectives, local(): returned = lax.all_to_all(sent, FS, 0, 0, tiled=True)  12.5 us
    ppermute x7, waiting for transfers between devices, along(): return lax.ppermute(value, ('core', 'y'), pairs)  11.2 us
  transfers between devices with their start and end apart: 7, of which 3 were waited for; matrix products, arithmetic and copies ran while one was open for 0% of the time, Pallas kernels for 2%

profile of v6, /device:TPU:1, one launch (start us, length us, event | category | flops | bytes accessed | tf_op | source)
XLA Modules:
  0.0 120.8 jit_solution(7596167233055600974)
XLA Ops:
  0.6 0.0 copy-start
  0.7 1.0 dynamic-slice_bitcast_fusion
  1.6 5.9 %collective-permute-start = (bf16[4,16,2048]{2,1,0:T(8,128)(2,1)S(1)}, bf16[4,16,2048]{2,1,0:T(8,128)(2,1)S(1)}, u32[]{:S(2)}, u32[]{:S(2)}) collective-permute-start(bf16[4,16,2048]{2,1,0:T(8,128)(2,1)S(1)} %dynamic-slice_bitcast_fusion), channel_id=1, source_target_pairs={{0,4},{4,8},{8,12},{12,16},{16,20},{20,24},{24,28},{28,0},{32,60},... | collective-permute-start | bytes 786440 | tf_op jit(solution)/shard_map/ppermute | solution.py:227
  7.6 0.0 copy-start.1
  7.6 1.6 %copy-done.1 = bf16[1,1,32,16,2048]{4,3,2,1,0:T(8,128)(2,1)S(1)} copy-done((bf16[1,1,32,16,2048]{4,3,2,1,0:T(8,128)(2,1)S(1)}, bf16[1,1,32,16,2048]{4,3,2,1,0:T(8,128)(2,1)}, u32[]{:S(2)}) %copy-start.1) | copy-done | bytes 2097176
  9.2 0.0 copy-start.2
  9.2 0.8 take.1
  10.0 1.9 %collective-permute-start.2 = (bf16[4,16,2048]{2,1,0:T(8,128)(2,1)}, bf16[4,16,2048]{2,1,0:T(8,128)(2,1)S(1)}, u32[]{:S(2)}, u32[]{:S(2)}) collective-permute-start(bf16[4,16,2048]{2,1,0:T(8,128)(2,1)} %get-tuple-element.10), channel_id=1, source_target_pairs={{0,24},{4,28},{8,0},{12,4},{16,8},{20,12},{24,16},{28,20},{32,40},... | collective-permute-start | bytes 786440 | tf_op jit(solution)/shard_map/ppermute | solution.py:227
  11.9 0.0 collective-permute-done.refs_4_
  11.9 0.0 copy-done.2
  12.0 0.9 ring_add.4
  12.8 2.5 %collective-permute-start.1 = (bf16[4,16,2048]{2,1,0:T(8,128)(2,1)}, bf16[4,16,2048]{2,1,0:T(8,128)(2,1)S(1)}, u32[]{:S(2)}, u32[]{:S(2)}) collective-permute-start(bf16[4,16,2048]{2,1,0:T(8,128)(2,1)} %get-tuple-element.9), channel_id=1, source_target_pairs={{0,28},{4,0},{8,4},{12,8},{16,12},{20,16},{24,20},{28,24},{32,36},... | collective-permute-start | bytes 786440 | tf_op jit(solution)/shard_map/ppermute | solution.py:227
  15.3 4.0 %collective-permute-start.4 = (bf16[4,16,2048]{2,1,0:T(8,128)(2,1)}, bf16[4,16,2048]{2,1,0:T(8,128)(2,1)S(1)}, u32[]{:S(2)}, u32[]{:S(2)}) collective-permute-start(bf16[4,16,2048]{2,1,0:T(8,128)(2,1)} %get-tuple-element.11), channel_id=1, source_target_pairs={{0,4},{4,8},{8,12},{12,16},{16,20},{20,24},{24,28},{28,0},{32,60},... | collective-permute-start | bytes 786440 | tf_op jit(solution)/shard_map/ppermute | solution.py:227
  19.3 4.3 %collective-permute-start.5 = (bf16[4,16,2048]{2,1,0:T(8,128)(2,1)}, bf16[4,16,2048]{2,1,0:T(8,128)(2,1)S(1)}, u32[]{:S(2)}, u32[]{:S(2)}) collective-permute-start(bf16[4,16,2048]{2,1,0:T(8,128)(2,1)} %get-tuple-element.12), channel_id=1, source_target_pairs={{0,8},{4,12},{8,16},{12,20},{16,24},{20,28},{24,0},{28,4},{32,56},... | collective-permute-start | bytes 786440 | tf_op jit(solution)/shard_map/ppermute | solution.py:227
  23.6 0.0 collective-permute-done.2.refs_3_
  23.6 0.1 collective-permute-done.1.refs_2_
  23.8 0.1 ring_add.5
  23.9 4.0 %collective-permute-start.3 = (bf16[4,16,2048]{2,1,0:T(8,128)(2,1)S(1)}, bf16[4,16,2048]{2,1,0:T(8,128)(2,1)S(1)}, u32[]{:S(2)}, u32[]{:S(2)}) collective-permute-start(bf16[4,16,2048]{2,1,0:T(8,128)(2,1)S(1)} %ring_add.5), channel_id=1, source_target_pairs={{0,28},{4,0},{8,4},{12,8},{16,12},{20,16},{24,20},{28,24},{32,36},... | collective-permute-start | bytes 786440 | tf_op jit(solution)/shard_map/ppermute | solution.py:227
  27.9 0.0 collective-permute-done.4.refs_2_
  27.9 5.5 %collective-permute-done.5.refs_3_ = bf16[4,16,2048]{2,1,0:T(8,128)(2,1)S(1)} collective-permute-done((bf16[4,16,2048]{2,1,0:T(8,128)(2,1)}, bf16[4,16,2048]{2,1,0:T(8,128)(2,1)S(1)}, u32[]{:S(2)}, u32[]{:S(2)}) %collective-permute-start.5) | collective-permute-done | bytes 262176 | tf_op jit(solution)/shard_map/ppermute | solution.py:227
  33.4 0.1 ring_add.6
  33.5 0.0 copy-start.4
  33.5 2.1 %collective-permute-start.6 = (bf16[4,16,2048]{2,1,0:T(8,128)(2,1)S(1)}, bf16[4,16,2048]{2,1,0:T(8,128)(2,1)S(1)}, u32[]{:S(2)}, u32[]{:S(2)}) collective-permute-start(bf16[4,16,2048]{2,1,0:T(8,128)(2,1)S(1)} %ring_add.6), channel_id=1, source_target_pairs={{0,4},{4,8},{8,12},{12,16},{16,20},{20,24},{24,28},{28,0},{32,60},... | collective-permute-start | bytes 786440 | tf_op jit(solution)/shard_map/ppermute | solution.py:227
  36.3 0.0 copy-done
  36.3 0.0 copy-start.3
  36.3 0.1 pad_add_fusion.refs_4_.idx
  36.4 0.0 collective-permute-done.3.refs_2_
  36.4 5.6 %collective-permute-done.6.refs_3_ = bf16[4,16,2048]{2,1,0:T(8,128)(2,1)S(1)} collective-permute-done((bf16[4,16,2048]{2,1,0:T(8,128)(2,1)S(1)}, bf16[4,16,2048]{2,1,0:T(8,128)(2,1)S(1)}, u32[]{:S(2)}, u32[]{:S(2)}) %collective-permute-start.6) | collective-permute-done | bytes 262176 | tf_op jit(solution)/shard_map/ppermute | solution.py:227
  42.0 0.7 ring_add.7
  42.6 0.0 copy-start.5
  42.7 32.5 %all_to_all.15.got = bf16[4,16,2048]{2,1,0:T(8,128)(2,1)S(1)} all-to-all(bf16[4,16,2048]{2,1,0:T(8,128)(2,1)S(1)} %ring_add.7), channel_id=1, replica_groups=mesh['z_lo'=4,'x'=4,'core'=2,'y'=8,'z_hi'=4] {'z_hi'}, dimensions={0} | all-to-all | bytes 524288 | tf_op jit(solution)/shard_map/all_to_all | solution.py:248
  75.2 0.0 copy-done.4
  75.2 0.0 copy-done.3
  75.2 1.5 %right_and_adam.1 = (bf16[32,16,512]{2,1,0:T(8,128)(2,1)S(1)}, f32[16,2048]{1,0:T(8,128)}, f32[8,128]{1,0:T(8,128)S(1)}) custom-call(s32[34]{0:T(128)S(1)} %pad_add_fusion.refs_4_.idx, bf16[4,16,2048]{2,1,0:T(8,128)(2,1)S(1)} %all_to_all.15.got, bf16[4,512,512]{2,1,0:T(8,128)(2,1)S(1)} %bitcast.27, f32[16,2048]{1,0:T(8,128)S(1)} %bitcast.29), custom_call_target="tpu_custom_call" | custom-call | tf_op jit(solution)/shard_map/right_and_adam/pallas_call | solution.py:131
  76.7 29.3 %all_to_all.16 = bf16[32,16,512]{2,1,0:T(8,128)(2,1)S(1)} all-to-all(bf16[32,16,512]{2,1,0:T(8,128)(2,1)S(1)} %get-tuple-element.13), channel_id=1, replica_groups=mesh['z_lo'=4,'x'=4,'core'=2,'y'=8,'z_hi'=4] {'z_lo','x','core'}, dimensions={0} | all-to-all | bytes 1048576 | tf_op jit(solution)/shard_map/all_to_all | solution.py:252
  105.9 0.0 copy-done.5
  106.0 1.0 left_product.1
  107.0 12.5 %all_to_all.17.got = bf16[32,16,128]{2,1,0:T(8,128)(2,1)S(1)} all-to-all(bf16[32,16,128]{2,1,0:T(8,128)(2,1)S(1)} %left_product.1), channel_id=1, replica_groups=mesh['z_lo'=4,'x'=4,'core'=2,'y'=8,'z_hi'=4] {'z_lo','x','core'}, dimensions={0} | all-to-all | bytes 262144 | tf_op jit(solution)/shard_map/all_to_all | solution.py:256
  119.4 1.3 %finish.1 = bf16[16,2048]{1,0:T(8,128)(2,1)} custom-call(s32[34]{0:T(128)S(1)} %pad_add_fusion.refs_4_.idx, bf16[32,16,128]{2,1,0:T(8,128)(2,1)S(1)} %all_to_all.17.got), custom_call_target="tpu_custom_call" | custom-call | tf_op jit(solution)/shard_map/finish/pallas_call | solution.py:206
  (1 shorter events, 0.0 us)
Async XLA Ops:
  0.6 35.6 %copy-start = (s32[32,32]{1,0:T(8,128)S(1)}, s32[32,32]{1,0:T(8,128)}, u32[]{:S(2)}) copy-start(s32[32,32]{1,0:T(8,128)} %param.10) | copy-start | bytes 12292
  1.6 10.3 %collective-permute-start = (bf16[4,16,2048]{2,1,0:T(8,128)(2,1)S(1)}, bf16[4,16,2048]{2,1,0:T(8,128)(2,1)S(1)}, u32[]{:S(2)}, u32[]{:S(2)}) collective-permute-start(bf16[4,16,2048]{2,1,0:T(8,128)(2,1)S(1)} %dynamic-slice_bitcast_fusion), channel_id=1, source_target_pairs={{0,4},{4,8},{8,12},{12,16},{16,20},{20,24},{24,28},{28,0},{32,60},... | collective-permute-start | bytes 786440 | tf_op jit(solution)/shard_map/ppermute | solution.py:227
  7.6 1.6 %copy-start.1 = (bf16[1,1,32,16,2048]{4,3,2,1,0:T(8,128)(2,1)S(1)}, bf16[1,1,32,16,2048]{4,3,2,1,0:T(8,128)(2,1)}, u32[]{:S(2)}) copy-start(bf16[1,1,32,16,2048]{4,3,2,1,0:T(8,128)(2,1)} %param.6) | copy-start | bytes 6291460
  9.2 2.8 %copy-start.2 = (bf16[1,1,32,16,2048]{4,3,2,1,0:T(8,128)(2,1)S(1)}, bf16[1,1,32,16,2048]{4,3,2,1,0:T(8,128)(2,1)}, u32[]{:S(2)}) copy-start(bf16[1,1,32,16,2048]{4,3,2,1,0:T(8,128)(2,1)} %param.6) | copy-start | bytes 6291460
  10.0 13.6 %collective-permute-start.2 = (bf16[4,16,2048]{2,1,0:T(8,128)(2,1)}, bf16[4,16,2048]{2,1,0:T(8,128)(2,1)S(1)}, u32[]{:S(2)}, u32[]{:S(2)}) collective-permute-start(bf16[4,16,2048]{2,1,0:T(8,128)(2,1)} %get-tuple-element.10), channel_id=1, source_target_pairs={{0,24},{4,28},{8,0},{12,4},{16,8},{20,12},{24,16},{28,20},{32,40},... | collective-permute-start | bytes 786440 | tf_op jit(solution)/shard_map/ppermute | solution.py:227
  12.8 10.9 %collective-permute-start.1 = (bf16[4,16,2048]{2,1,0:T(8,128)(2,1)}, bf16[4,16,2048]{2,1,0:T(8,128)(2,1)S(1)}, u32[]{:S(2)}, u32[]{:S(2)}) collective-permute-start(bf16[4,16,2048]{2,1,0:T(8,128)(2,1)} %get-tuple-element.9), channel_id=1, source_target_pairs={{0,28},{4,0},{8,4},{12,8},{16,12},{20,16},{24,20},{28,24},{32,36},... | collective-permute-start | bytes 786440 | tf_op jit(solution)/shard_map/ppermute | solution.py:227
  15.3 12.6 %collective-permute-start.4 = (bf16[4,16,2048]{2,1,0:T(8,128)(2,1)}, bf16[4,16,2048]{2,1,0:T(8,128)(2,1)S(1)}, u32[]{:S(2)}, u32[]{:S(2)}) collective-permute-start(bf16[4,16,2048]{2,1,0:T(8,128)(2,1)} %get-tuple-element.11), channel_id=1, source_target_pairs={{0,4},{4,8},{8,12},{12,16},{16,20},{20,24},{24,28},{28,0},{32,60},... | collective-permute-start | bytes 786440 | tf_op jit(solution)/shard_map/ppermute | solution.py:227
  19.3 14.0 %collective-permute-start.5 = (bf16[4,16,2048]{2,1,0:T(8,128)(2,1)}, bf16[4,16,2048]{2,1,0:T(8,128)(2,1)S(1)}, u32[]{:S(2)}, u32[]{:S(2)}) collective-permute-start(bf16[4,16,2048]{2,1,0:T(8,128)(2,1)} %get-tuple-element.12), channel_id=1, source_target_pairs={{0,8},{4,12},{8,16},{12,20},{16,24},{20,28},{24,0},{28,4},{32,56},... | collective-permute-start | bytes 786440 | tf_op jit(solution)/shard_map/ppermute | solution.py:227
  23.9 12.5 %collective-permute-start.3 = (bf16[4,16,2048]{2,1,0:T(8,128)(2,1)S(1)}, bf16[4,16,2048]{2,1,0:T(8,128)(2,1)S(1)}, u32[]{:S(2)}, u32[]{:S(2)}) collective-permute-start(bf16[4,16,2048]{2,1,0:T(8,128)(2,1)S(1)} %ring_add.5), channel_id=1, source_target_pairs={{0,28},{4,0},{8,4},{12,8},{16,12},{20,16},{24,20},{28,24},{32,36},... | collective-permute-start | bytes 786440 | tf_op jit(solution)/shard_map/ppermute | solution.py:227
  33.5 41.7 %copy-start.4 = (f32[1,1,16,2048]{3,2,1,0:T(8,128)S(1)}, f32[1,1,16,2048]{3,2,1,0:T(8,128)}, u32[]{:S(2)}) copy-start(f32[1,1,16,2048]{3,2,1,0:T(8,128)} %param.7) | copy-start | bytes 393220
  33.5 8.4 %collective-permute-start.6 = (bf16[4,16,2048]{2,1,0:T(8,128)(2,1)S(1)}, bf16[4,16,2048]{2,1,0:T(8,128)(2,1)S(1)}, u32[]{:S(2)}, u32[]{:S(2)}) collective-permute-start(bf16[4,16,2048]{2,1,0:T(8,128)(2,1)S(1)} %ring_add.6), channel_id=1, source_target_pairs={{0,4},{4,8},{8,12},{12,16},{16,20},{20,24},{24,28},{28,0},{32,60},... | collective-permute-start | bytes 786440 | tf_op jit(solution)/shard_map/ppermute | solution.py:227
  36.3 38.9 %copy-start.3 = (bf16[1,4,512,512]{3,2,1,0:T(8,128)(2,1)S(1)}, bf16[1,4,512,512]{3,2,1,0:T(8,128)(2,1)}, u32[]{:S(2)}) copy-start(bf16[1,4,512,512]{3,2,1,0:T(8,128)(2,1)} %param.9) | copy-start | bytes 6291460
  42.6 63.3 %copy-start.5 = (bf16[1,1,64,512]{3,2,1,0:T(8,128)(2,1)S(1)}, bf16[1,1,64,512]{3,2,1,0:T(8,128)(2,1)}, u32[]{:S(2)}) copy-start(bf16[1,1,64,512]{3,2,1,0:T(8,128)(2,1)} %param.8) | copy-start | bytes 196612

commit v7 on v6

--- a/solution.py
+++ b/solution.py
@@ -58,11 +58,11 @@
     )(*places, *[chunks] * count)
 
 
-def ring_add(chunks, index, *received, also=None, after=None):
+def ring_add(chunks, index, *received, also=(), after=None):
     _, parts, rows, width = chunks.shape
     half = parts // 2
     count = len(received)
-    places = [index] + ([] if also is None else [also])
+    places = [index, *also]
     wanted = len(places)
 
     def body(*refs):
@@ -72,8 +72,8 @@
         for got in refs[2 * wanted : 2 * wanted + count]:
             total = total + got[...].astype(f32)
         outs[0][...] = total.astype(bf16)
-        if wanted == 2:
-            outs[1][...] = own[1][0]
+        for copied, out in zip(own[1:], outs[1:]):
+            out[...] = copied[0]
 
     def block_at(n):
         return pl.BlockSpec((1, half, rows, width), lambda i, *idx: (idx[n][0], i, 0, 0))
@@ -92,7 +92,7 @@
         compiler_params=pltpu.CompilerParams(vmem_limit_bytes=VMEM_LIMIT),
         name="ring_add",
     )(*places, *[chunks] * wanted, *received, *extra)
-    return out[0] if also is None else out
+    return out if also else out[0]
 
 
 def right_and_adam(parts, right, moment, scalars, step_at, owners_at, members):
@@ -234,16 +234,16 @@
     member_at, step_at, owners_at = 0, 1, 2
 
     chunks = gradients.reshape(ny, nz, rows, width)
-    four = along(lax.dynamic_index_in_dim(chunks, at(4)[0], 0, keepdims=False), 1)
-    minus_three, two = take(chunks, at(-3), at(2))
+    four, two = take(chunks, at(4), at(2))
+    four = along(four, 1)
+    two = along(two, 1)
+    three, minus_three, minus_two = ring_add(chunks, at(3), four, also=(at(-3), at(-2)))
+    three = along(three, 2)
     minus_three = along(minus_three, -2)
-    two = along(two, 1)
-    three, minus_two = ring_add(chunks, at(3), four, also=at(-2))
-    three = along(three, 2)
     minus_two = along(minus_two, -1)
+    one = along(ring_add(chunks, at(1), two, three), 1)
     minus_one = along(ring_add(chunks, at(-1), minus_two, minus_three), -1)
-    one = along(ring_add(chunks, at(1), two, three), 1)
-    part = ring_add(chunks, at(0), minus_one, one, after=scalars)
+    part = ring_add(chunks, at(0), one, minus_one, after=scalars)
 
     parts = lax.all_to_all(part, "z_hi", 0, 0, tiled=True)
     pieces, new_moment, squares = right_and_adam(

time: 123 us -> 125 us (1.016); the launches traced: 121 us -> 125 us
  starting transfers between devices: 24.6 us -> 31.2 us
  waiting for transfers between devices: 11.2 us -> 9.25 us
    ppermute x7, starting transfers between devices: 24.6 us -> 31.2 us  [along(): return lax.ppermute(value, ('core', 'y'), pairs)]
    all_to_all x1, blocking collectives: 29.3 us -> 31.4 us  [local(): lax.all_to_all(pieces, FS, 0, 0, tiled=True).reshape(members * rows, size)]
    ppermute x7, waiting for transfers between devices: 11.2 us -> 9.25 us  [along(): return lax.ppermute(value, ('core', 'y'), pairs)]
    all_to_all x1, blocking collectives: 32.5 us -> 30.9 us  [local(): parts = lax.all_to_all(part, 'z_hi', 0, 0, tiled=True)]
  transfers between devices with their start and end apart: 7 -> 7, of which waited for: 3 -> 4; matrix products, arithmetic and copies ran while one was open for 0% -> 0% of each run, Pallas kernels for 2% -> 1%
where the time goes in v7:
time: 125 us
  blocking collectives  74.8 us (60%)
  starting transfers between devices  31.2 us (25%)
  waiting for transfers between devices  9.25 us (7%)
  Pallas kernels  6.43 us (5%)
  local copies, waits for them, and re-layouts  1.63 us (1%)
  between operations  1.49 us (1%)
    all_to_all x1, blocking collectives, local(): lax.all_to_all(pieces, FS, 0, 0, tiled=True).reshape(members * rows, size)  31.4 us
    ppermute x7, starting transfers between devices, along(): return lax.ppermute(value, ('core', 'y'), pairs)  31.2 us
    all_to_all x1, blocking collectives, local(): parts = lax.all_to_all(part, 'z_hi', 0, 0, tiled=True)  30.9 us
    all_to_all x1, blocking collectives, local(): returned = lax.all_to_all(sent, FS, 0, 0, tiled=True)  12.5 us
    ppermute x7, waiting for transfers between devices, along(): return lax.ppermute(value, ('core', 'y'), pairs)  9.25 us
  transfers between devices with their start and end apart: 7, of which 4 were waited for; matrix products, arithmetic and copies ran while one was open for 0% of the time, Pallas kernels for 1%

profile of v7, /device:TPU:1, one launch (start us, length us, event | category | flops | bytes accessed | tf_op | source)
XLA Modules:
  0.0 124.9 jit_solution(13139029784285141533)
XLA Ops:
  0.6 0.0 copy-start
  0.7 0.0 copy-start.1
  0.7 1.6 %copy-done.1 = bf16[1,1,32,16,2048]{4,3,2,1,0:T(8,128)(2,1)S(1)} copy-done((bf16[1,1,32,16,2048]{4,3,2,1,0:T(8,128)(2,1)S(1)}, bf16[1,1,32,16,2048]{4,3,2,1,0:T(8,128)(2,1)}, u32[]{:S(2)}) %copy-start.1) | copy-done | bytes 2097176
  2.3 0.0 copy-start.2
  2.3 0.7 take.1
  3.0 5.9 %collective-permute-start.1 = (bf16[4,16,2048]{2,1,0:T(8,128)(2,1)S(1)}, bf16[4,16,2048]{2,1,0:T(8,128)(2,1)S(1)}, u32[]{:S(2)}, u32[]{:S(2)}) collective-permute-start(bf16[4,16,2048]{2,1,0:T(8,128)(2,1)S(1)} %get-tuple-element.11), channel_id=1, source_target_pairs={{0,4},{4,8},{8,12},{12,16},{16,20},{20,24},{24,28},{28,0},{32,60},... | collective-permute-start | bytes 786440 | tf_op jit(solution)/shard_map/ppermute | solution.py:227
  8.9 3.0 %collective-permute-start = (bf16[4,16,2048]{2,1,0:T(8,128)(2,1)}, bf16[4,16,2048]{2,1,0:T(8,128)(2,1)S(1)}, u32[]{:S(2)}, u32[]{:S(2)}) collective-permute-start(bf16[4,16,2048]{2,1,0:T(8,128)(2,1)} %get-tuple-element.10), channel_id=1, source_target_pairs={{0,4},{4,8},{8,12},{12,16},{16,20},{20,24},{24,28},{28,0},{32,60},... | collective-permute-start | bytes 786440 | tf_op jit(solution)/shard_map/ppermute | solution.py:227
  11.9 0.3 collective-permute-done.1.refs_6_
  12.2 0.0 copy-done.2
  12.2 0.9 ring_add.4
  13.1 4.9 %collective-permute-start.2 = (bf16[4,16,2048]{2,1,0:T(8,128)(2,1)}, bf16[4,16,2048]{2,1,0:T(8,128)(2,1)S(1)}, u32[]{:S(2)}, u32[]{:S(2)}) collective-permute-start(bf16[4,16,2048]{2,1,0:T(8,128)(2,1)} %get-tuple-element.12), channel_id=1, source_target_pairs={{0,8},{4,12},{8,16},{12,20},{16,24},{20,28},{24,0},{28,4},{32,56},... | collective-permute-start | bytes 786440 | tf_op jit(solution)/shard_map/ppermute | solution.py:227
  18.0 3.2 %collective-permute-start.4 = (bf16[4,16,2048]{2,1,0:T(8,128)(2,1)}, bf16[4,16,2048]{2,1,0:T(8,128)(2,1)S(1)}, u32[]{:S(2)}, u32[]{:S(2)}) collective-permute-start(bf16[4,16,2048]{2,1,0:T(8,128)(2,1)} %get-tuple-element.13), channel_id=1, source_target_pairs={{0,28},{4,0},{8,4},{12,8},{16,12},{20,16},{24,20},{28,24},{32,36},... | collective-permute-start | bytes 786440 | tf_op jit(solution)/shard_map/ppermute | solution.py:227
  21.3 1.9 %collective-permute-start.5 = (bf16[4,16,2048]{2,1,0:T(8,128)(2,1)}, bf16[4,16,2048]{2,1,0:T(8,128)(2,1)S(1)}, u32[]{:S(2)}, u32[]{:S(2)}) collective-permute-start(bf16[4,16,2048]{2,1,0:T(8,128)(2,1)} %get-tuple-element.14), channel_id=1, source_target_pairs={{0,24},{4,28},{8,0},{12,4},{16,8},{20,12},{24,16},{28,20},{32,40},... | collective-permute-start | bytes 786440 | tf_op jit(solution)/shard_map/ppermute | solution.py:227
  23.2 0.0 collective-permute-done.refs_2_
  23.2 0.0 collective-permute-done.2.refs_3_
  23.2 0.2 ring_add.5
  23.4 6.2 %collective-permute-start.3 = (bf16[4,16,2048]{2,1,0:T(8,128)(2,1)S(1)}, bf16[4,16,2048]{2,1,0:T(8,128)(2,1)S(1)}, u32[]{:S(2)}, u32[]{:S(2)}) collective-permute-start(bf16[4,16,2048]{2,1,0:T(8,128)(2,1)S(1)} %ring_add.5), channel_id=1, source_target_pairs={{0,4},{4,8},{8,12},{12,16},{16,20},{20,24},{24,28},{28,0},{32,60},... | collective-permute-start | bytes 786440 | tf_op jit(solution)/shard_map/ppermute | solution.py:227
  29.5 0.3 collective-permute-done.4.refs_2_
  29.8 5.4 %collective-permute-done.5.refs_3_ = bf16[4,16,2048]{2,1,0:T(8,128)(2,1)S(1)} collective-permute-done((bf16[4,16,2048]{2,1,0:T(8,128)(2,1)}, bf16[4,16,2048]{2,1,0:T(8,128)(2,1)S(1)}, u32[]{:S(2)}, u32[]{:S(2)}) %collective-permute-start.5) | collective-permute-done | bytes 262176 | tf_op jit(solution)/shard_map/ppermute | solution.py:227
  35.3 0.1 ring_add.6
  35.4 0.0 copy-start.4
  35.4 6.2 %collective-permute-start.6 = (bf16[4,16,2048]{2,1,0:T(8,128)(2,1)S(1)}, bf16[4,16,2048]{2,1,0:T(8,128)(2,1)S(1)}, u32[]{:S(2)}, u32[]{:S(2)}) collective-permute-start(bf16[4,16,2048]{2,1,0:T(8,128)(2,1)S(1)} %ring_add.6), channel_id=1, source_target_pairs={{0,28},{4,0},{8,4},{12,8},{16,12},{20,16},{24,20},{28,24},{32,36},... | collective-permute-start | bytes 786440 | tf_op jit(solution)/shard_map/ppermute | solution.py:227
  42.2 0.0 copy-done
  42.2 0.0 copy-start.3
  42.3 0.1 pad_add_fusion.refs_4_.idx
  42.3 0.0 collective-permute-done.3.refs_2_
  42.3 3.2 %collective-permute-done.6.refs_3_ = bf16[4,16,2048]{2,1,0:T(8,128)(2,1)S(1)} collective-permute-done((bf16[4,16,2048]{2,1,0:T(8,128)(2,1)S(1)}, bf16[4,16,2048]{2,1,0:T(8,128)(2,1)S(1)}, u32[]{:S(2)}, u32[]{:S(2)}) %collective-permute-start.6) | collective-permute-done | bytes 262176 | tf_op jit(solution)/shard_map/ppermute | solution.py:227
  45.6 0.7 ring_add.7
  46.3 0.0 copy-start.5
  46.3 30.9 %all_to_all.15.got = bf16[4,16,2048]{2,1,0:T(8,128)(2,1)S(1)} all-to-all(bf16[4,16,2048]{2,1,0:T(8,128)(2,1)S(1)} %ring_add.7), channel_id=1, replica_groups=mesh['z_lo'=4,'x'=4,'core'=2,'y'=8,'z_hi'=4] {'z_hi'}, dimensions={0} | all-to-all | bytes 524288 | tf_op jit(solution)/shard_map/all_to_all | solution.py:248
  77.2 0.0 copy-done.4
  77.2 0.0 copy-done.3
  77.2 1.5 %right_and_adam.1 = (bf16[32,16,512]{2,1,0:T(8,128)(2,1)S(1)}, f32[16,2048]{1,0:T(8,128)}, f32[8,128]{1,0:T(8,128)S(1)}) custom-call(s32[34]{0:T(128)S(1)} %pad_add_fusion.refs_4_.idx, bf16[4,16,2048]{2,1,0:T(8,128)(2,1)S(1)} %all_to_all.15.got, bf16[4,512,512]{2,1,0:T(8,128)(2,1)S(1)} %bitcast.26, f32[16,2048]{1,0:T(8,128)S(1)} %bitcast.28), custom_call_target="tpu_custom_call" | custom-call | tf_op jit(solution)/shard_map/right_and_adam/pallas_call | solution.py:131
  78.6 31.4 %all_to_all.16 = bf16[32,16,512]{2,1,0:T(8,128)(2,1)S(1)} all-to-all(bf16[32,16,512]{2,1,0:T(8,128)(2,1)S(1)} %get-tuple-element.15), channel_id=1, replica_groups=mesh['z_lo'=4,'x'=4,'core'=2,'y'=8,'z_hi'=4] {'z_lo','x','core'}, dimensions={0} | all-to-all | bytes 1048576 | tf_op jit(solution)/shard_map/all_to_all | solution.py:252
  110.0 0.0 copy-done.5
  110.0 1.0 left_product.1
  111.0 12.5 %all_to_all.17.got = bf16[32,16,128]{2,1,0:T(8,128)(2,1)S(1)} all-to-all(bf16[32,16,128]{2,1,0:T(8,128)(2,1)S(1)} %left_product.1), channel_id=1, replica_groups=mesh['z_lo'=4,'x'=4,'core'=2,'y'=8,'z_hi'=4] {'z_lo','x','core'}, dimensions={0} | all-to-all | bytes 262144 | tf_op jit(solution)/shard_map/all_to_all | solution.py:256
  123.5 1.3 %finish.1 = bf16[16,2048]{1,0:T(8,128)(2,1)} custom-call(s32[34]{0:T(128)S(1)} %pad_add_fusion.refs_4_.idx, bf16[32,16,128]{2,1,0:T(8,128)(2,1)S(1)} %all_to_all.17.got), custom_call_target="tpu_custom_call" | custom-call | tf_op jit(solution)/shard_map/finish/pallas_call | solution.py:206
  (1 shorter events, 0.0 us)
Async XLA Ops:
  0.6 41.6 %copy-start = (s32[32,32]{1,0:T(8,128)S(1)}, s32[32,32]{1,0:T(8,128)}, u32[]{:S(2)}) copy-start(s32[32,32]{1,0:T(8,128)} %param.10) | copy-start | bytes 12292
  0.7 1.6 %copy-start.1 = (bf16[1,1,32,16,2048]{4,3,2,1,0:T(8,128)(2,1)S(1)}, bf16[1,1,32,16,2048]{4,3,2,1,0:T(8,128)(2,1)}, u32[]{:S(2)}) copy-start(bf16[1,1,32,16,2048]{4,3,2,1,0:T(8,128)(2,1)} %param.6) | copy-start | bytes 6291460
  2.3 10.0 %copy-start.2 = (bf16[1,1,32,16,2048]{4,3,2,1,0:T(8,128)(2,1)S(1)}, bf16[1,1,32,16,2048]{4,3,2,1,0:T(8,128)(2,1)}, u32[]{:S(2)}) copy-start(bf16[1,1,32,16,2048]{4,3,2,1,0:T(8,128)(2,1)} %param.6) | copy-start | bytes 6291460
  3.0 9.2 %collective-permute-start.1 = (bf16[4,16,2048]{2,1,0:T(8,128)(2,1)S(1)}, bf16[4,16,2048]{2,1,0:T(8,128)(2,1)S(1)}, u32[]{:S(2)}, u32[]{:S(2)}) collective-permute-start(bf16[4,16,2048]{2,1,0:T(8,128)(2,1)S(1)} %get-tuple-element.11), channel_id=1, source_target_pairs={{0,4},{4,8},{8,12},{12,16},{16,20},{20,24},{24,28},{28,0},{32,60},... | collective-permute-start | bytes 786440 | tf_op jit(solution)/shard_map/ppermute | solution.py:227
  8.9 14.3 %collective-permute-start = (bf16[4,16,2048]{2,1,0:T(8,128)(2,1)}, bf16[4,16,2048]{2,1,0:T(8,128)(2,1)S(1)}, u32[]{:S(2)}, u32[]{:S(2)}) collective-permute-start(bf16[4,16,2048]{2,1,0:T(8,128)(2,1)} %get-tuple-element.10), channel_id=1, source_target_pairs={{0,4},{4,8},{8,12},{12,16},{16,20},{20,24},{24,28},{28,0},{32,60},... | collective-permute-start | bytes 786440 | tf_op jit(solution)/shard_map/ppermute | solution.py:227
  13.1 10.1 %collective-permute-start.2 = (bf16[4,16,2048]{2,1,0:T(8,128)(2,1)}, bf16[4,16,2048]{2,1,0:T(8,128)(2,1)S(1)}, u32[]{:S(2)}, u32[]{:S(2)}) collective-permute-start(bf16[4,16,2048]{2,1,0:T(8,128)(2,1)} %get-tuple-element.12), channel_id=1, source_target_pairs={{0,8},{4,12},{8,16},{12,20},{16,24},{20,28},{24,0},{28,4},{32,56},... | collective-permute-start | bytes 786440 | tf_op jit(solution)/shard_map/ppermute | solution.py:227
  18.0 11.8 %collective-permute-start.4 = (bf16[4,16,2048]{2,1,0:T(8,128)(2,1)}, bf16[4,16,2048]{2,1,0:T(8,128)(2,1)S(1)}, u32[]{:S(2)}, u32[]{:S(2)}) collective-permute-start(bf16[4,16,2048]{2,1,0:T(8,128)(2,1)} %get-tuple-element.13), channel_id=1, source_target_pairs={{0,28},{4,0},{8,4},{12,8},{16,12},{20,16},{24,20},{28,24},{32,36},... | collective-permute-start | bytes 786440 | tf_op jit(solution)/shard_map/ppermute | solution.py:227
  21.3 14.0 %collective-permute-start.5 = (bf16[4,16,2048]{2,1,0:T(8,128)(2,1)}, bf16[4,16,2048]{2,1,0:T(8,128)(2,1)S(1)}, u32[]{:S(2)}, u32[]{:S(2)}) collective-permute-start(bf16[4,16,2048]{2,1,0:T(8,128)(2,1)} %get-tuple-element.14), channel_id=1, source_target_pairs={{0,24},{4,28},{8,0},{12,4},{16,8},{20,12},{24,16},{28,20},{32,40},... | collective-permute-start | bytes 786440 | tf_op jit(solution)/shard_map/ppermute | solution.py:227
  23.4 19.0 %collective-permute-start.3 = (bf16[4,16,2048]{2,1,0:T(8,128)(2,1)S(1)}, bf16[4,16,2048]{2,1,0:T(8,128)(2,1)S(1)}, u32[]{:S(2)}, u32[]{:S(2)}) collective-permute-start(bf16[4,16,2048]{2,1,0:T(8,128)(2,1)S(1)} %ring_add.5), channel_id=1, source_target_pairs={{0,4},{4,8},{8,12},{12,16},{16,20},{20,24},{24,28},{28,0},{32,60},... | collective-permute-start | bytes 786440 | tf_op jit(solution)/shard_map/ppermute | solution.py:227
  35.4 41.8 %copy-start.4 = (f32[1,1,16,2048]{3,2,1,0:T(8,128)S(1)}, f32[1,1,16,2048]{3,2,1,0:T(8,128)}, u32[]{:S(2)}) copy-start(f32[1,1,16,2048]{3,2,1,0:T(8,128)} %param.7) | copy-start | bytes 393220
  35.4 10.2 %collective-permute-start.6 = (bf16[4,16,2048]{2,1,0:T(8,128)(2,1)S(1)}, bf16[4,16,2048]{2,1,0:T(8,128)(2,1)S(1)}, u32[]{:S(2)}, u32[]{:S(2)}) collective-permute-start(bf16[4,16,2048]{2,1,0:T(8,128)(2,1)S(1)} %ring_add.6), channel_id=1, source_target_pairs={{0,28},{4,0},{8,4},{12,8},{16,12},{20,16},{24,20},{28,24},{32,36},... | collective-permute-start | bytes 786440 | tf_op jit(solution)/shard_map/ppermute | solution.py:227
  42.2 34.9 %copy-start.3 = (bf16[1,4,512,512]{3,2,1,0:T(8,128)(2,1)S(1)}, bf16[1,4,512,512]{3,2,1,0:T(8,128)(2,1)}, u32[]{:S(2)}) copy-start(bf16[1,4,512,512]{3,2,1,0:T(8,128)(2,1)} %param.9) | copy-start | bytes 6291460
  46.3 63.8 %copy-start.5 = (bf16[1,1,64,512]{3,2,1,0:T(8,128)(2,1)S(1)}, bf16[1,1,64,512]{3,2,1,0:T(8,128)(2,1)}, u32[]{:S(2)}) copy-start(bf16[1,1,64,512]{3,2,1,0:T(8,128)(2,1)} %param.8) | copy-start | bytes 196612

commit v8 on v6

--- a/solution.py
+++ b/solution.py
@@ -58,41 +58,33 @@
     )(*places, *[chunks] * count)
 
 
-def ring_add(chunks, index, *received, also=None, after=None):
+def ring_add(chunks, index, *received, after=None):
     _, parts, rows, width = chunks.shape
     half = parts // 2
     count = len(received)
-    places = [index] + ([] if also is None else [also])
-    wanted = len(places)
-
-    def body(*refs):
-        own = refs[wanted : 2 * wanted]
-        outs = refs[-wanted:]
-        total = own[0][0].astype(f32)
-        for got in refs[2 * wanted : 2 * wanted + count]:
+
+    def body(idx, own, *refs):
+        total = own[0].astype(f32)
+        for got in refs[:count]:
             total = total + got[...].astype(f32)
-        outs[0][...] = total.astype(bf16)
-        if wanted == 2:
-            outs[1][...] = own[1][0]
-
-    def block_at(n):
-        return pl.BlockSpec((1, half, rows, width), lambda i, *idx: (idx[n][0], i, 0, 0))
-
-    block = pl.BlockSpec((half, rows, width), lambda i, *idx: (i, 0, 0))
+        refs[-1][...] = total.astype(bf16)
+
+    block = pl.BlockSpec((half, rows, width), lambda i, idx: (i, 0, 0))
     extra = [] if after is None else [after]
-    out = pl.pallas_call(
+    return pl.pallas_call(
         body,
         grid_spec=pltpu.PrefetchScalarGridSpec(
-            num_scalar_prefetch=wanted,
+            num_scalar_prefetch=1,
             grid=(2,),
-            in_specs=[block_at(n) for n in range(wanted)] + [block] * count + [SMEM] * len(extra),
-            out_specs=[block] * wanted,
+            in_specs=[pl.BlockSpec((1, half, rows, width), lambda i, idx: (idx[0], i, 0, 0))]
+            + [block] * count
+            + [SMEM] * len(extra),
+            out_specs=block,
         ),
-        out_shape=[jax.ShapeDtypeStruct((parts, rows, width), bf16)] * wanted,
+        out_shape=jax.ShapeDtypeStruct((parts, rows, width), bf16),
         compiler_params=pltpu.CompilerParams(vmem_limit_bytes=VMEM_LIMIT),
         name="ring_add",
-    )(*places, *[chunks] * wanted, *received, *extra)
-    return out[0] if also is None else out
+    )(index, chunks, *received, *extra)
 
 
 def right_and_adam(parts, right, moment, scalars, step_at, owners_at, members):
@@ -234,16 +226,15 @@
     member_at, step_at, owners_at = 0, 1, 2
 
     chunks = gradients.reshape(ny, nz, rows, width)
-    four = along(lax.dynamic_index_in_dim(chunks, at(4)[0], 0, keepdims=False), 1)
-    minus_three, two = take(chunks, at(-3), at(2))
+    four, minus_three, two, minus_two = take(chunks, at(4), at(-3), at(2), at(-2))
+    four = along(four, 1)
     minus_three = along(minus_three, -2)
     two = along(two, 1)
-    three, minus_two = ring_add(chunks, at(3), four, also=at(-2))
-    three = along(three, 2)
     minus_two = along(minus_two, -1)
+    three = along(ring_add(chunks, at(3), four, after=scalars), 2)
     minus_one = along(ring_add(chunks, at(-1), minus_two, minus_three), -1)
     one = along(ring_add(chunks, at(1), two, three), 1)
-    part = ring_add(chunks, at(0), minus_one, one, after=scalars)
+    part = ring_add(chunks, at(0), one, minus_one)
 
     parts = lax.all_to_all(part, "z_hi", 0, 0, tiled=True)
     pieces, new_moment, squares = right_and_adam(

time: 123 us -> 121 us (0.984)
  starting transfers between devices: 24.6 us -> 30.7 us
  waiting for transfers between devices: 11.2 us -> 6.96 us
  blocking collectives: 74.3 us -> 72.4 us
    ppermute x7, starting transfers between devices: 24.6 us -> 30.7 us  [along(): return lax.ppermute(value, ('core', 'y'), pairs)]
    ppermute x7, waiting for transfers between devices: 11.2 us -> 6.96 us  [along(): return lax.ppermute(value, ('core', 'y'), pairs)]
    all_to_all x1, blocking collectives: 32.5 us -> 30.6 us  [local(): parts = lax.all_to_all(part, 'z_hi', 0, 0, tiled=True)]
  transfers between devices with their start and end apart: 7 -> 7, of which waited for: 3 -> 2; matrix products, arithmetic and copies ran while one was open for 0% -> 0% of each run, Pallas kernels for 2% -> 1%
where the time goes in v8:
time: 121 us; the launch traced here: 120 us
  blocking collectives  72.4 us (60%)
  starting transfers between devices  30.7 us (25%)
  waiting for transfers between devices  6.96 us (6%)
  Pallas kernels  6.46 us (5%)
  local copies, waits for them, and re-layouts  1.63 us (1%)
  between operations  1.5 us (1%)
    ppermute x7, starting transfers between devices, along(): return lax.ppermute(value, ('core', 'y'), pairs)  30.7 us
    all_to_all x1, blocking collectives, local(): parts = lax.all_to_all(part, 'z_hi', 0, 0, tiled=True)  30.6 us
    all_to_all x1, blocking collectives, local(): lax.all_to_all(pieces, FS, 0, 0, tiled=True).reshape(members * rows, size)  29.3 us
    all_to_all x1, blocking collectives, local(): returned = lax.all_to_all(sent, FS, 0, 0, tiled=True)  12.5 us
    ppermute x7, waiting for transfers between devices, along(): return lax.ppermute(value, ('core', 'y'), pairs)  6.96 us
  transfers between devices with their start and end apart: 7, of which 2 were waited for; matrix products, arithmetic and copies ran while one was open for 0% of the time, Pallas kernels for 1%

profile of v8, /device:TPU:1, one launch (start us, length us, event | category | flops | bytes accessed | tf_op | source)
XLA Modules:
  0.0 119.7 jit_solution(2249327945509826493)
XLA Ops:
  0.6 0.0 copy-start
  0.7 0.0 copy-start.1
  0.7 1.6 %copy-done.1 = bf16[1,1,32,16,2048]{4,3,2,1,0:T(8,128)(2,1)S(1)} copy-done((bf16[1,1,32,16,2048]{4,3,2,1,0:T(8,128)(2,1)S(1)}, bf16[1,1,32,16,2048]{4,3,2,1,0:T(8,128)(2,1)}, u32[]{:S(2)}) %copy-start.1) | copy-done | bytes 2097176
  2.3 0.0 copy-start.2
  2.3 1.0 take.1
  3.2 5.9 %collective-permute-start.1 = (bf16[4,16,2048]{2,1,0:T(8,128)(2,1)S(1)}, bf16[4,16,2048]{2,1,0:T(8,128)(2,1)S(1)}, u32[]{:S(2)}, u32[]{:S(2)}) collective-permute-start(bf16[4,16,2048]{2,1,0:T(8,128)(2,1)S(1)} %get-tuple-element.10), channel_id=1, source_target_pairs={{0,4},{4,8},{8,12},{12,16},{16,20},{20,24},{24,28},{28,0},{32,60},... | collective-permute-start | bytes 786440 | tf_op jit(solution)/shard_map/ppermute | solution.py:219
  9.1 1.9 %collective-permute-start.4 = (bf16[4,16,2048]{2,1,0:T(8,128)(2,1)}, bf16[4,16,2048]{2,1,0:T(8,128)(2,1)S(1)}, u32[]{:S(2)}, u32[]{:S(2)}) collective-permute-start(bf16[4,16,2048]{2,1,0:T(8,128)(2,1)} %get-tuple-element.11), channel_id=1, source_target_pairs={{0,28},{4,0},{8,4},{12,8},{16,12},{20,16},{24,20},{28,24},{32,36},... | collective-permute-start | bytes 786440 | tf_op jit(solution)/shard_map/ppermute | solution.py:219
  11.1 2.5 %collective-permute-start.5 = (bf16[4,16,2048]{2,1,0:T(8,128)(2,1)}, bf16[4,16,2048]{2,1,0:T(8,128)(2,1)S(1)}, u32[]{:S(2)}, u32[]{:S(2)}) collective-permute-start(bf16[4,16,2048]{2,1,0:T(8,128)(2,1)} %get-tuple-element.12), channel_id=1, source_target_pairs={{0,24},{4,28},{8,0},{12,4},{16,8},{20,12},{24,16},{28,20},{32,40},... | collective-permute-start | bytes 786440 | tf_op jit(solution)/shard_map/ppermute | solution.py:219
  13.6 4.0 %collective-permute-start = (bf16[4,16,2048]{2,1,0:T(8,128)(2,1)}, bf16[4,16,2048]{2,1,0:T(8,128)(2,1)S(1)}, u32[]{:S(2)}, u32[]{:S(2)}) collective-permute-start(bf16[4,16,2048]{2,1,0:T(8,128)(2,1)} %get-tuple-element.9), channel_id=1, source_target_pairs={{0,4},{4,8},{8,12},{12,16},{16,20},{20,24},{24,28},{28,0},{32,60},... | collective-permute-start | bytes 786440 | tf_op jit(solution)/shard_map/ppermute | solution.py:219
  18.2 0.0 copy-done
  18.3 0.1 pad_add_fusion.refs_1_.idx
  18.3 0.0 collective-permute-done.1.refs_0_
  18.4 0.0 copy-done.2
  18.4 0.6 ring_add.4
  19.0 4.3 %collective-permute-start.2 = (bf16[4,16,2048]{2,1,0:T(8,128)(2,1)S(1)}, bf16[4,16,2048]{2,1,0:T(8,128)(2,1)S(1)}, u32[]{:S(2)}, u32[]{:S(2)}) collective-permute-start(bf16[4,16,2048]{2,1,0:T(8,128)(2,1)S(1)} %ring_add.4), channel_id=1, source_target_pairs={{0,8},{4,12},{8,16},{12,20},{16,24},{20,28},{24,0},{28,4},{32,56},... | collective-permute-start | bytes 786440 | tf_op jit(solution)/shard_map/ppermute | solution.py:219
  23.3 0.0 collective-permute-done.4.refs_0_
  23.3 0.0 collective-permute-done.5.refs_1_
  23.3 0.8 ring_add.6
  24.1 3.1 %collective-permute-start.6 = (bf16[4,16,2048]{2,1,0:T(8,128)(2,1)}, bf16[4,16,2048]{2,1,0:T(8,128)(2,1)S(1)}, u32[]{:S(2)}, u32[]{:S(2)}) collective-permute-start(bf16[4,16,2048]{2,1,0:T(8,128)(2,1)} %ring_add.6), channel_id=1, source_target_pairs={{0,28},{4,0},{8,4},{12,8},{16,12},{20,16},{24,20},{28,24},{32,36},... | collective-permute-start | bytes 786440 | tf_op jit(solution)/shard_map/ppermute | solution.py:219
  27.3 0.0 collective-permute-done.refs_0_
  27.3 3.7 %collective-permute-done.2.refs_1_ = bf16[4,16,2048]{2,1,0:T(8,128)(2,1)S(1)} collective-permute-done((bf16[4,16,2048]{2,1,0:T(8,128)(2,1)S(1)}, bf16[4,16,2048]{2,1,0:T(8,128)(2,1)S(1)}, u32[]{:S(2)}, u32[]{:S(2)}) %collective-permute-start.2) | collective-permute-done | bytes 262176 | tf_op jit(solution)/shard_map/ppermute | solution.py:219
  30.9 0.1 ring_add.5
  31.1 0.0 copy-start.4
  31.1 8.9 %collective-permute-start.3 = (bf16[4,16,2048]{2,1,0:T(8,128)(2,1)S(1)}, bf16[4,16,2048]{2,1,0:T(8,128)(2,1)S(1)}, u32[]{:S(2)}, u32[]{:S(2)}) collective-permute-start(bf16[4,16,2048]{2,1,0:T(8,128)(2,1)S(1)} %ring_add.5), channel_id=1, source_target_pairs={{0,4},{4,8},{8,12},{12,16},{16,20},{20,24},{24,28},{28,0},{32,60},... | collective-permute-start | bytes 786440 | tf_op jit(solution)/shard_map/ppermute | solution.py:219
  40.0 0.0 copy-start.3
  40.1 0.0 collective-permute-done.6.refs_1_
  40.1 3.3 %collective-permute-done.3.refs_0_ = bf16[4,16,2048]{2,1,0:T(8,128)(2,1)S(1)} collective-permute-done((bf16[4,16,2048]{2,1,0:T(8,128)(2,1)S(1)}, bf16[4,16,2048]{2,1,0:T(8,128)(2,1)S(1)}, u32[]{:S(2)}, u32[]{:S(2)}) %collective-permute-start.3) | collective-permute-done | bytes 262176 | tf_op jit(solution)/shard_map/ppermute | solution.py:219
  43.3 0.1 ring_add.7
  43.5 0.0 copy-start.5
  43.5 30.6 %all_to_all.15.got = bf16[4,16,2048]{2,1,0:T(8,128)(2,1)S(1)} all-to-all(bf16[4,16,2048]{2,1,0:T(8,128)(2,1)S(1)} %ring_add.7), channel_id=1, replica_groups=mesh['z_lo'=4,'x'=4,'core'=2,'y'=8,'z_hi'=4] {'z_hi'}, dimensions={0} | all-to-all | bytes 524288 | tf_op jit(solution)/shard_map/all_to_all | solution.py:239
  74.1 0.0 copy-done.4
  74.1 0.0 copy-done.3
  74.1 1.5 %right_and_adam.1 = (bf16[32,16,512]{2,1,0:T(8,128)(2,1)S(1)}, f32[16,2048]{1,0:T(8,128)}, f32[8,128]{1,0:T(8,128)S(1)}) custom-call(s32[34]{0:T(128)S(1)} %pad_add_fusion.refs_1_.idx, bf16[4,16,2048]{2,1,0:T(8,128)(2,1)S(1)} %all_to_all.15.got, bf16[4,512,512]{2,1,0:T(8,128)(2,1)S(1)} %bitcast.26, f32[16,2048]{1,0:T(8,128)S(1)} %bitcast.28), custom_call_target="tpu_custom_call" | custom-call | tf_op jit(solution)/shard_map/right_and_adam/pallas_call | solution.py:123
  75.6 29.3 %all_to_all.16 = bf16[32,16,512]{2,1,0:T(8,128)(2,1)S(1)} all-to-all(bf16[32,16,512]{2,1,0:T(8,128)(2,1)S(1)} %get-tuple-element.13), channel_id=1, replica_groups=mesh['z_lo'=4,'x'=4,'core'=2,'y'=8,'z_hi'=4] {'z_lo','x','core'}, dimensions={0} | all-to-all | bytes 1048576 | tf_op jit(solution)/shard_map/all_to_all | solution.py:243
  104.8 0.0 copy-done.5
  104.8 1.0 left_product.1
  105.8 12.5 %all_to_all.17.got = bf16[32,16,128]{2,1,0:T(8,128)(2,1)S(1)} all-to-all(bf16[32,16,128]{2,1,0:T(8,128)(2,1)S(1)} %left_product.1), channel_id=1, replica_groups=mesh['z_lo'=4,'x'=4,'core'=2,'y'=8,'z_hi'=4] {'z_lo','x','core'}, dimensions={0} | all-to-all | bytes 262144 | tf_op jit(solution)/shard_map/all_to_all | solution.py:247
  118.3 1.3 %finish.1 = bf16[16,2048]{1,0:T(8,128)(2,1)} custom-call(s32[34]{0:T(128)S(1)} %pad_add_fusion.refs_1_.idx, bf16[32,16,128]{2,1,0:T(8,128)(2,1)S(1)} %all_to_all.17.got), custom_call_target="tpu_custom_call" | custom-call | tf_op jit(solution)/shard_map/finish/pallas_call | solution.py:198
  (1 shorter events, 0.0 us)
Async XLA Ops:
  0.6 17.6 %copy-start = (s32[32,32]{1,0:T(8,128)S(1)}, s32[32,32]{1,0:T(8,128)}, u32[]{:S(2)}) copy-start(s32[32,32]{1,0:T(8,128)} %param.10) | copy-start | bytes 12292
  0.7 1.6 %copy-start.1 = (bf16[1,1,32,16,2048]{4,3,2,1,0:T(8,128)(2,1)S(1)}, bf16[1,1,32,16,2048]{4,3,2,1,0:T(8,128)(2,1)}, u32[]{:S(2)}) copy-start(bf16[1,1,32,16,2048]{4,3,2,1,0:T(8,128)(2,1)} %param.6) | copy-start | bytes 6291460
  2.3 16.1 %copy-start.2 = (bf16[1,1,32,16,2048]{4,3,2,1,0:T(8,128)(2,1)S(1)}, bf16[1,1,32,16,2048]{4,3,2,1,0:T(8,128)(2,1)}, u32[]{:S(2)}) copy-start(bf16[1,1,32,16,2048]{4,3,2,1,0:T(8,128)(2,1)} %param.6) | copy-start | bytes 6291460
  3.2 15.1 %collective-permute-start.1 = (bf16[4,16,2048]{2,1,0:T(8,128)(2,1)S(1)}, bf16[4,16,2048]{2,1,0:T(8,128)(2,1)S(1)}, u32[]{:S(2)}, u32[]{:S(2)}) collective-permute-start(bf16[4,16,2048]{2,1,0:T(8,128)(2,1)S(1)} %get-tuple-element.10), channel_id=1, source_target_pairs={{0,4},{4,8},{8,12},{12,16},{16,20},{20,24},{24,28},{28,0},{32,60},... | collective-permute-start | bytes 786440 | tf_op jit(solution)/shard_map/ppermute | solution.py:219
  9.1 14.1 %collective-permute-start.4 = (bf16[4,16,2048]{2,1,0:T(8,128)(2,1)}, bf16[4,16,2048]{2,1,0:T(8,128)(2,1)S(1)}, u32[]{:S(2)}, u32[]{:S(2)}) collective-permute-start(bf16[4,16,2048]{2,1,0:T(8,128)(2,1)} %get-tuple-element.11), channel_id=1, source_target_pairs={{0,28},{4,0},{8,4},{12,8},{16,12},{20,16},{24,20},{28,24},{32,36},... | collective-permute-start | bytes 786440 | tf_op jit(solution)/shard_map/ppermute | solution.py:219
  11.1 12.2 %collective-permute-start.5 = (bf16[4,16,2048]{2,1,0:T(8,128)(2,1)}, bf16[4,16,2048]{2,1,0:T(8,128)(2,1)S(1)}, u32[]{:S(2)}, u32[]{:S(2)}) collective-permute-start(bf16[4,16,2048]{2,1,0:T(8,128)(2,1)} %get-tuple-element.12), channel_id=1, source_target_pairs={{0,24},{4,28},{8,0},{12,4},{16,8},{20,12},{24,16},{28,20},{32,40},... | collective-permute-start | bytes 786440 | tf_op jit(solution)/shard_map/ppermute | solution.py:219
  13.6 13.7 %collective-permute-start = (bf16[4,16,2048]{2,1,0:T(8,128)(2,1)}, bf16[4,16,2048]{2,1,0:T(8,128)(2,1)S(1)}, u32[]{:S(2)}, u32[]{:S(2)}) collective-permute-start(bf16[4,16,2048]{2,1,0:T(8,128)(2,1)} %get-tuple-element.9), channel_id=1, source_target_pairs={{0,4},{4,8},{8,12},{12,16},{16,20},{20,24},{24,28},{28,0},{32,60},... | collective-permute-start | bytes 786440 | tf_op jit(solution)/shard_map/ppermute | solution.py:219
  19.0 11.9 %collective-permute-start.2 = (bf16[4,16,2048]{2,1,0:T(8,128)(2,1)S(1)}, bf16[4,16,2048]{2,1,0:T(8,128)(2,1)S(1)}, u32[]{:S(2)}, u32[]{:S(2)}) collective-permute-start(bf16[4,16,2048]{2,1,0:T(8,128)(2,1)S(1)} %ring_add.4), channel_id=1, source_target_pairs={{0,8},{4,12},{8,16},{12,20},{16,24},{20,28},{24,0},{28,4},{32,56},... | collective-permute-start | bytes 786440 | tf_op jit(solution)/shard_map/ppermute | solution.py:219
  24.1 16.0 %collective-permute-start.6 = (bf16[4,16,2048]{2,1,0:T(8,128)(2,1)}, bf16[4,16,2048]{2,1,0:T(8,128)(2,1)S(1)}, u32[]{:S(2)}, u32[]{:S(2)}) collective-permute-start(bf16[4,16,2048]{2,1,0:T(8,128)(2,1)} %ring_add.6), channel_id=1, source_target_pairs={{0,28},{4,0},{8,4},{12,8},{16,12},{20,16},{24,20},{28,24},{32,36},... | collective-permute-start | bytes 786440 | tf_op jit(solution)/shard_map/ppermute | solution.py:219
  31.1 43.0 %copy-start.4 = (f32[1,1,16,2048]{3,2,1,0:T(8,128)S(1)}, f32[1,1,16,2048]{3,2,1,0:T(8,128)}, u32[]{:S(2)}) copy-start(f32[1,1,16,2048]{3,2,1,0:T(8,128)} %param.7) | copy-start | bytes 393220
  31.1 12.2 %collective-permute-start.3 = (bf16[4,16,2048]{2,1,0:T(8,128)(2,1)S(1)}, bf16[4,16,2048]{2,1,0:T(8,128)(2,1)S(1)}, u32[]{:S(2)}, u32[]{:S(2)}) collective-permute-start(bf16[4,16,2048]{2,1,0:T(8,128)(2,1)S(1)} %ring_add.5), channel_id=1, source_target_pairs={{0,4},{4,8},{8,12},{12,16},{16,20},{20,24},{24,28},{28,0},{32,60},... | collective-permute-start | bytes 786440 | tf_op jit(solution)/shard_map/ppermute | solution.py:219
  40.0 34.1 %copy-start.3 = (bf16[1,4,512,512]{3,2,1,0:T(8,128)(2,1)S(1)}, bf16[1,4,512,512]{3,2,1,0:T(8,128)(2,1)}, u32[]{:S(2)}) copy-start(bf16[1,4,512,512]{3,2,1,0:T(8,128)(2,1)} %param.9) | copy-start | bytes 6291460
  43.5 61.4 %copy-start.5 = (bf16[1,1,64,512]{3,2,1,0:T(8,128)(2,1)S(1)}, bf16[1,1,64,512]{3,2,1,0:T(8,128)(2,1)}, u32[]{:S(2)}) copy-start(bf16[1,1,64,512]{3,2,1,0:T(8,128)(2,1)} %param.8) | copy-start | bytes 196612

commit v9 on v8

--- a/solution.py
+++ b/solution.py
@@ -231,10 +231,10 @@
     minus_three = along(minus_three, -2)
     two = along(two, 1)
     minus_two = along(minus_two, -1)
-    three = along(ring_add(chunks, at(3), four, after=scalars), 2)
+    three = along(ring_add(chunks, at(3), four), 2)
     minus_one = along(ring_add(chunks, at(-1), minus_two, minus_three), -1)
     one = along(ring_add(chunks, at(1), two, three), 1)
-    part = ring_add(chunks, at(0), one, minus_one)
+    part = ring_add(chunks, at(0), one, minus_one, after=scalars)
 
     parts = lax.all_to_all(part, "z_hi", 0, 0, tiled=True)
     pieces, new_moment, squares = right_and_adam(

time: 121 us -> 121 us (level)
  starting transfers between devices: 30.7 us -> 33.1 us
  waiting for transfers between devices: 6.96 us -> 4.59 us
    ppermute x7, starting transfers between devices: 30.7 us -> 33.1 us  [along(): return lax.ppermute(value, ('core', 'y'), pairs)]
    ppermute x7, waiting for transfers between devices: 6.96 us -> 4.59 us  [along(): return lax.ppermute(value, ('core', 'y'), pairs)]
where the time goes in v9:
time: 121 us; the launch traced here: 120 us
  blocking collectives  73.1 us (60%)
  starting transfers between devices  33.1 us (27%)
  Pallas kernels  6.47 us (5%)
  waiting for transfers between devices  4.59 us (4%)
  local copies, waits for them, and re-layouts  1.63 us (1%)
  between operations  1.51 us (1%)
    ppermute x7, starting transfers between devices, along(): return lax.ppermute(value, ('core', 'y'), pairs)  33.1 us
    all_to_all x1, blocking collectives, local(): parts = lax.all_to_all(part, 'z_hi', 0, 0, tiled=True)  31.2 us
    all_to_all x1, blocking collectives, local(): lax.all_to_all(pieces, FS, 0, 0, tiled=True).reshape(members * rows, size)  29.4 us
    all_to_all x1, blocking collectives, local(): returned = lax.all_to_all(sent, FS, 0, 0, tiled=True)  12.5 us
    ppermute x7, waiting for transfers between devices, along(): return lax.ppermute(value, ('core', 'y'), pairs)  4.59 us
  transfers between devices with their start and end apart: 7, of which 2 were waited for; matrix products, arithmetic and copies ran while one was open for 0% of the time, Pallas kernels for 1%

profile of v9, /device:TPU:1, one launch (start us, length us, event | category | flops | bytes accessed | tf_op | source)
XLA Modules:
  0.0 120.5 jit_solution(9668475104014709625)
XLA Ops:
  0.6 0.0 copy-start
  0.7 0.0 copy-start.1
  0.7 1.6 %copy-done.1 = bf16[1,1,32,16,2048]{4,3,2,1,0:T(8,128)(2,1)S(1)} copy-done((bf16[1,1,32,16,2048]{4,3,2,1,0:T(8,128)(2,1)S(1)}, bf16[1,1,32,16,2048]{4,3,2,1,0:T(8,128)(2,1)}, u32[]{:S(2)}) %copy-start.1) | copy-done | bytes 2097176
  2.3 0.0 copy-start.2
  2.3 0.9 take.1
  3.2 5.9 %collective-permute-start.1 = (bf16[4,16,2048]{2,1,0:T(8,128)(2,1)S(1)}, bf16[4,16,2048]{2,1,0:T(8,128)(2,1)S(1)}, u32[]{:S(2)}, u32[]{:S(2)}) collective-permute-start(bf16[4,16,2048]{2,1,0:T(8,128)(2,1)S(1)} %get-tuple-element.10), channel_id=1, source_target_pairs={{0,4},{4,8},{8,12},{12,16},{16,20},{20,24},{24,28},{28,0},{32,60},... | collective-permute-start | bytes 786440 | tf_op jit(solution)/shard_map/ppermute | solution.py:219
  9.1 1.9 %collective-permute-start.4 = (bf16[4,16,2048]{2,1,0:T(8,128)(2,1)}, bf16[4,16,2048]{2,1,0:T(8,128)(2,1)S(1)}, u32[]{:S(2)}, u32[]{:S(2)}) collective-permute-start(bf16[4,16,2048]{2,1,0:T(8,128)(2,1)} %get-tuple-element.11), channel_id=1, source_target_pairs={{0,28},{4,0},{8,4},{12,8},{16,12},{20,16},{24,20},{28,24},{32,36},... | collective-permute-start | bytes 786440 | tf_op jit(solution)/shard_map/ppermute | solution.py:219
  11.0 2.5 %collective-permute-start.5 = (bf16[4,16,2048]{2,1,0:T(8,128)(2,1)}, bf16[4,16,2048]{2,1,0:T(8,128)(2,1)S(1)}, u32[]{:S(2)}, u32[]{:S(2)}) collective-permute-start(bf16[4,16,2048]{2,1,0:T(8,128)(2,1)} %get-tuple-element.12), channel_id=1, source_target_pairs={{0,24},{4,28},{8,0},{12,4},{16,8},{20,12},{24,16},{28,20},{32,40},... | collective-permute-start | bytes 786440 | tf_op jit(solution)/shard_map/ppermute | solution.py:219
  13.5 4.0 %collective-permute-start = (bf16[4,16,2048]{2,1,0:T(8,128)(2,1)}, bf16[4,16,2048]{2,1,0:T(8,128)(2,1)S(1)}, u32[]{:S(2)}, u32[]{:S(2)}) collective-permute-start(bf16[4,16,2048]{2,1,0:T(8,128)(2,1)} %get-tuple-element.9), channel_id=1, source_target_pairs={{0,4},{4,8},{8,12},{12,16},{16,20},{20,24},{24,28},{28,0},{32,60},... | collective-permute-start | bytes 786440 | tf_op jit(solution)/shard_map/ppermute | solution.py:219
  17.6 0.0 collective-permute-done.1.refs_0_
  17.6 0.0 copy-done.2
  17.6 0.8 ring_add.4
  18.4 4.2 %collective-permute-start.2 = (bf16[4,16,2048]{2,1,0:T(8,128)(2,1)}, bf16[4,16,2048]{2,1,0:T(8,128)(2,1)S(1)}, u32[]{:S(2)}, u32[]{:S(2)}) collective-permute-start(bf16[4,16,2048]{2,1,0:T(8,128)(2,1)} %ring_add.4), channel_id=1, source_target_pairs={{0,8},{4,12},{8,16},{12,20},{16,24},{20,28},{24,0},{28,4},{32,56},... | collective-permute-start | bytes 786440 | tf_op jit(solution)/shard_map/ppermute | solution.py:219
  22.6 0.0 collective-permute-done.4.refs_0_
  22.6 0.0 collective-permute-done.5.refs_1_
  22.6 0.2 ring_add.6
  22.8 3.8 %collective-permute-start.6 = (bf16[4,16,2048]{2,1,0:T(8,128)(2,1)S(1)}, bf16[4,16,2048]{2,1,0:T(8,128)(2,1)S(1)}, u32[]{:S(2)}, u32[]{:S(2)}) collective-permute-start(bf16[4,16,2048]{2,1,0:T(8,128)(2,1)S(1)} %ring_add.6), channel_id=1, source_target_pairs={{0,28},{4,0},{8,4},{12,8},{16,12},{20,16},{24,20},{28,24},{32,36},... | collective-permute-start | bytes 786440 | tf_op jit(solution)/shard_map/ppermute | solution.py:219
  26.6 0.0 collective-permute-done.refs_0_
  26.6 2.1 %collective-permute-done.2.refs_1_ = bf16[4,16,2048]{2,1,0:T(8,128)(2,1)S(1)} collective-permute-done((bf16[4,16,2048]{2,1,0:T(8,128)(2,1)}, bf16[4,16,2048]{2,1,0:T(8,128)(2,1)S(1)}, u32[]{:S(2)}, u32[]{:S(2)}) %collective-permute-start.2) | collective-permute-done | bytes 262176 | tf_op jit(solution)/shard_map/ppermute | solution.py:219
  28.7 0.1 ring_add.5
  28.8 0.0 copy-start.4
  28.8 10.7 %collective-permute-start.3 = (bf16[4,16,2048]{2,1,0:T(8,128)(2,1)S(1)}, bf16[4,16,2048]{2,1,0:T(8,128)(2,1)S(1)}, u32[]{:S(2)}, u32[]{:S(2)}) collective-permute-start(bf16[4,16,2048]{2,1,0:T(8,128)(2,1)S(1)} %ring_add.5), channel_id=1, source_target_pairs={{0,4},{4,8},{8,12},{12,16},{16,20},{20,24},{24,28},{28,0},{32,60},... | collective-permute-start | bytes 786440 | tf_op jit(solution)/shard_map/ppermute | solution.py:219
  40.2 0.0 copy-done
  40.2 0.0 copy-start.3
  40.3 0.1 pad_add_fusion.refs_2_.idx
  40.3 0.0 collective-permute-done.6.refs_1_
  40.3 2.5 %collective-permute-done.3.refs_0_ = bf16[4,16,2048]{2,1,0:T(8,128)(2,1)S(1)} collective-permute-done((bf16[4,16,2048]{2,1,0:T(8,128)(2,1)S(1)}, bf16[4,16,2048]{2,1,0:T(8,128)(2,1)S(1)}, u32[]{:S(2)}, u32[]{:S(2)}) %collective-permute-start.3) | collective-permute-done | bytes 262176 | tf_op jit(solution)/shard_map/ppermute | solution.py:219
  42.8 0.7 ring_add.7
  43.5 0.0 copy-start.5
  43.5 31.2 %all_to_all.15.got = bf16[4,16,2048]{2,1,0:T(8,128)(2,1)S(1)} all-to-all(bf16[4,16,2048]{2,1,0:T(8,128)(2,1)S(1)} %ring_add.7), channel_id=1, replica_groups=mesh['z_lo'=4,'x'=4,'core'=2,'y'=8,'z_hi'=4] {'z_hi'}, dimensions={0} | all-to-all | bytes 524288 | tf_op jit(solution)/shard_map/all_to_all | solution.py:239
  74.7 0.0 copy-done.4
  74.7 0.0 copy-done.3
  74.7 1.5 %right_and_adam.1 = (bf16[32,16,512]{2,1,0:T(8,128)(2,1)S(1)}, f32[16,2048]{1,0:T(8,128)}, f32[8,128]{1,0:T(8,128)S(1)}) custom-call(s32[34]{0:T(128)S(1)} %pad_add_fusion.refs_2_.idx, bf16[4,16,2048]{2,1,0:T(8,128)(2,1)S(1)} %all_to_all.15.got, bf16[4,512,512]{2,1,0:T(8,128)(2,1)S(1)} %bitcast.26, f32[16,2048]{1,0:T(8,128)S(1)} %bitcast.28), custom_call_target="tpu_custom_call" | custom-call | tf_op jit(solution)/shard_map/right_and_adam/pallas_call | solution.py:123
  76.2 29.4 %all_to_all.16 = bf16[32,16,512]{2,1,0:T(8,128)(2,1)S(1)} all-to-all(bf16[32,16,512]{2,1,0:T(8,128)(2,1)S(1)} %get-tuple-element.13), channel_id=1, replica_groups=mesh['z_lo'=4,'x'=4,'core'=2,'y'=8,'z_hi'=4] {'z_lo','x','core'}, dimensions={0} | all-to-all | bytes 1048576 | tf_op jit(solution)/shard_map/all_to_all | solution.py:243
  105.7 0.0 copy-done.5
  105.7 1.0 left_product.1
  106.7 12.5 %all_to_all.17.got = bf16[32,16,128]{2,1,0:T(8,128)(2,1)S(1)} all-to-all(bf16[32,16,128]{2,1,0:T(8,128)(2,1)S(1)} %left_product.1), channel_id=1, replica_groups=mesh['z_lo'=4,'x'=4,'core'=2,'y'=8,'z_hi'=4] {'z_lo','x','core'}, dimensions={0} | all-to-all | bytes 262144 | tf_op jit(solution)/shard_map/all_to_all | solution.py:247
  119.2 1.3 %finish.1 = bf16[16,2048]{1,0:T(8,128)(2,1)} custom-call(s32[34]{0:T(128)S(1)} %pad_add_fusion.refs_2_.idx, bf16[32,16,128]{2,1,0:T(8,128)(2,1)S(1)} %all_to_all.17.got), custom_call_target="tpu_custom_call" | custom-call | tf_op jit(solution)/shard_map/finish/pallas_call | solution.py:198
  (1 shorter events, 0.0 us)
Async XLA Ops:
  0.6 39.6 %copy-start = (s32[32,32]{1,0:T(8,128)S(1)}, s32[32,32]{1,0:T(8,128)}, u32[]{:S(2)}) copy-start(s32[32,32]{1,0:T(8,128)} %param.10) | copy-start | bytes 12292
  0.7 1.6 %copy-start.1 = (bf16[1,1,32,16,2048]{4,3,2,1,0:T(8,128)(2,1)S(1)}, bf16[1,1,32,16,2048]{4,3,2,1,0:T(8,128)(2,1)}, u32[]{:S(2)}) copy-start(bf16[1,1,32,16,2048]{4,3,2,1,0:T(8,128)(2,1)} %param.6) | copy-start | bytes 6291460
  2.3 15.3 %copy-start.2 = (bf16[1,1,32,16,2048]{4,3,2,1,0:T(8,128)(2,1)S(1)}, bf16[1,1,32,16,2048]{4,3,2,1,0:T(8,128)(2,1)}, u32[]{:S(2)}) copy-start(bf16[1,1,32,16,2048]{4,3,2,1,0:T(8,128)(2,1)} %param.6) | copy-start | bytes 6291460
  3.2 14.4 %collective-permute-start.1 = (bf16[4,16,2048]{2,1,0:T(8,128)(2,1)S(1)}, bf16[4,16,2048]{2,1,0:T(8,128)(2,1)S(1)}, u32[]{:S(2)}, u32[]{:S(2)}) collective-permute-start(bf16[4,16,2048]{2,1,0:T(8,128)(2,1)S(1)} %get-tuple-element.10), channel_id=1, source_target_pairs={{0,4},{4,8},{8,12},{12,16},{16,20},{20,24},{24,28},{28,0},{32,60},... | collective-permute-start | bytes 786440 | tf_op jit(solution)/shard_map/ppermute | solution.py:219
  9.1 13.5 %collective-permute-start.4 = (bf16[4,16,2048]{2,1,0:T(8,128)(2,1)}, bf16[4,16,2048]{2,1,0:T(8,128)(2,1)S(1)}, u32[]{:S(2)}, u32[]{:S(2)}) collective-permute-start(bf16[4,16,2048]{2,1,0:T(8,128)(2,1)} %get-tuple-element.11), channel_id=1, source_target_pairs={{0,28},{4,0},{8,4},{12,8},{16,12},{20,16},{24,20},{28,24},{32,36},... | collective-permute-start | bytes 786440 | tf_op jit(solution)/shard_map/ppermute | solution.py:219
  11.0 11.6 %collective-permute-start.5 = (bf16[4,16,2048]{2,1,0:T(8,128)(2,1)}, bf16[4,16,2048]{2,1,0:T(8,128)(2,1)S(1)}, u32[]{:S(2)}, u32[]{:S(2)}) collective-permute-start(bf16[4,16,2048]{2,1,0:T(8,128)(2,1)} %get-tuple-element.12), channel_id=1, source_target_pairs={{0,24},{4,28},{8,0},{12,4},{16,8},{20,12},{24,16},{28,20},{32,40},... | collective-permute-start | bytes 786440 | tf_op jit(solution)/shard_map/ppermute | solution.py:219
  13.5 13.1 %collective-permute-start = (bf16[4,16,2048]{2,1,0:T(8,128)(2,1)}, bf16[4,16,2048]{2,1,0:T(8,128)(2,1)S(1)}, u32[]{:S(2)}, u32[]{:S(2)}) collective-permute-start(bf16[4,16,2048]{2,1,0:T(8,128)(2,1)} %get-tuple-element.9), channel_id=1, source_target_pairs={{0,4},{4,8},{8,12},{12,16},{16,20},{20,24},{24,28},{28,0},{32,60},... | collective-permute-start | bytes 786440 | tf_op jit(solution)/shard_map/ppermute | solution.py:219
  18.4 10.3 %collective-permute-start.2 = (bf16[4,16,2048]{2,1,0:T(8,128)(2,1)}, bf16[4,16,2048]{2,1,0:T(8,128)(2,1)S(1)}, u32[]{:S(2)}, u32[]{:S(2)}) collective-permute-start(bf16[4,16,2048]{2,1,0:T(8,128)(2,1)} %ring_add.4), channel_id=1, source_target_pairs={{0,8},{4,12},{8,16},{12,20},{16,24},{20,28},{24,0},{28,4},{32,56},... | collective-permute-start | bytes 786440 | tf_op jit(solution)/shard_map/ppermute | solution.py:219
  22.8 17.5 %collective-permute-start.6 = (bf16[4,16,2048]{2,1,0:T(8,128)(2,1)S(1)}, bf16[4,16,2048]{2,1,0:T(8,128)(2,1)S(1)}, u32[]{:S(2)}, u32[]{:S(2)}) collective-permute-start(bf16[4,16,2048]{2,1,0:T(8,128)(2,1)S(1)} %ring_add.6), channel_id=1, source_target_pairs={{0,28},{4,0},{8,4},{12,8},{16,12},{20,16},{24,20},{28,24},{32,36},... | collective-permute-start | bytes 786440 | tf_op jit(solution)/shard_map/ppermute | solution.py:219
  28.8 45.9 %copy-start.4 = (f32[1,1,16,2048]{3,2,1,0:T(8,128)S(1)}, f32[1,1,16,2048]{3,2,1,0:T(8,128)}, u32[]{:S(2)}) copy-start(f32[1,1,16,2048]{3,2,1,0:T(8,128)} %param.7) | copy-start | bytes 393220
  28.8 14.0 %collective-permute-start.3 = (bf16[4,16,2048]{2,1,0:T(8,128)(2,1)S(1)}, bf16[4,16,2048]{2,1,0:T(8,128)(2,1)S(1)}, u32[]{:S(2)}, u32[]{:S(2)}) collective-permute-start(bf16[4,16,2048]{2,1,0:T(8,128)(2,1)S(1)} %ring_add.5), channel_id=1, source_target_pairs={{0,4},{4,8},{8,12},{12,16},{16,20},{20,24},{24,28},{28,0},{32,60},... | collective-permute-start | bytes 786440 | tf_op jit(solution)/shard_map/ppermute | solution.py:219
  40.2 34.5 %copy-start.3 = (bf16[1,4,512,512]{3,2,1,0:T(8,128)(2,1)S(1)}, bf16[1,4,512,512]{3,2,1,0:T(8,128)(2,1)}, u32[]{:S(2)}) copy-start(bf16[1,4,512,512]{3,2,1,0:T(8,128)(2,1)} %param.9) | copy-start | bytes 6291460
  43.5 62.1 %copy-start.5 = (bf16[1,1,64,512]{3,2,1,0:T(8,128)(2,1)S(1)}, bf16[1,1,64,512]{3,2,1,0:T(8,128)(2,1)}, u32[]{:S(2)}) copy-start(bf16[1,1,64,512]{3,2,1,0:T(8,128)(2,1)} %param.8) | copy-start | bytes 196612
